TPU v7x, 32 devices: a whole 2x2x4 slice. The times are simulated.
32 devices in a mesh: ctx: 8 (over z, y), fsdp: 4 (over x, core).
Axes of the slice: x: 2, y: 2, z: 4, core: 2. Of those that a mesh axis runs over, the one named last changes fastest.
Arguments:
- grad_out: bfloat16 [1024, 8192], P('ctx', 'fsdp'), may hold values from -6 to 6
- queries: bfloat16 [1024, 8192], P('ctx', 'fsdp'), may hold values from -6 to 6
- keys_in: bfloat16 [1024, 8192], P('ctx', 'fsdp'), may hold values from -6 to 6
- values_in: bfloat16 [1024, 8192], P('ctx', 'fsdp'), may hold values from -6 to 6
- filters: bfloat16 [512, 128], P('fsdp'), may hold values from -1.25 to 1.25
- out_weight: bfloat16 [8192, 8192], P('ctx', 'fsdp'), may hold values from -0.0625 to 0.0625
Outputs:
- grad_q: bfloat16 [1024, 8192], P('ctx', 'fsdp')
- grad_k: bfloat16 [1024, 8192], P('ctx', 'fsdp')
- grad_v: bfloat16 [1024, 8192], P('ctx', 'fsdp')
- grad_filters: float32 [512, 128], P('fsdp')
All inputs are finite; a program needn't handle non-finite values.
Results may differ from a plain program's by a relative error of at most 0.015.
Values may be sent and summed in bfloat16 or wider, within the bound.
No kernel may reach another device: no remote copies, remote signals or barrier semaphores. Data moves between devices by JAX's collectives and lax.ppermute only.
A program may use at most 128 MiB of HBM per device.

v0:
```python
import jax
import jax.numpy as jnp
from jax import lax
from jax.sharding import PartitionSpec as P


def from_behind(block, axis, distance):
    devices = range(lax.axis_size(axis))
    route = [(i - distance, i) for i in devices if i - distance in devices]
    return lax.ppermute(block, axis, route)


def toeplitz_rows(line_filters, tokens_here):
    group_count = line_filters.shape[0]
    taps = line_filters.shape[1]
    span = tokens_here + taps - 1
    padded_line = jnp.concatenate(
        [line_filters, jnp.zeros((group_count, span + 1 - taps), line_filters.dtype)], axis=1
    )
    tiled = jnp.tile(padded_line, (1, tokens_here))
    return tiled[:, : tokens_here * span].reshape(group_count, tokens_here, span)


def per_device(grad_out, queries, keys_in, values_in, filters, out_weight):
    tokens_here = grad_out.shape[0]
    channels = grad_out.shape[1]
    group_count = filters.shape[0]
    taps = filters.shape[1]
    per_group = channels // group_count
    margin = taps - 1
    span = tokens_here + margin
    kvp = (keys_in.astype(jnp.float32) * values_in.astype(jnp.float32)).astype(jnp.bfloat16)
    prior = from_behind(kvp[tokens_here - margin :], "ctx", 1)
    kv_ext = jnp.concatenate([prior, kvp], axis=0)
    full_grad = lax.all_gather(grad_out, "fsdp", axis=1, tiled=True)
    grad_y32 = jnp.dot(
        full_grad,
        lax.all_gather(out_weight, "ctx", axis=0, tiled=True),
        preferred_element_type=jnp.float32,
    )
    grad_y = grad_y32.astype(jnp.bfloat16)
    grad_yf = grad_y.astype(jnp.float32)
    forward_toe = toeplitz_rows(filters[:, ::-1], tokens_here)
    kv_groups = kv_ext.reshape(span, group_count, per_group)
    z_conv = jnp.einsum(
        "gts,sgc->tgc", forward_toe, kv_groups, preferred_element_type=jnp.float32
    ).reshape(tokens_here, channels)
    grad_q = (grad_yf * z_conv).astype(jnp.bfloat16)
    grad_z = (grad_yf * queries.astype(jnp.float32)).astype(jnp.bfloat16)
    later = from_behind(grad_z[:margin], "ctx", -1)
    gz_ext = jnp.concatenate([grad_z, later], axis=0)
    backward_toe = toeplitz_rows(filters, tokens_here)
    gz_groups = gz_ext.reshape(span, group_count, per_group)
    grad_kv = jnp.einsum(
        "gts,sgc->tgc", backward_toe, gz_groups, preferred_element_type=jnp.float32
    ).reshape(tokens_here, channels)
    grad_k = (grad_kv * values_in.astype(jnp.float32)).astype(jnp.bfloat16)
    grad_v = (grad_kv * keys_in.astype(jnp.float32)).astype(jnp.bfloat16)
    pairs = jnp.einsum(
        "tgc,sgc->gts",
        grad_z.reshape(tokens_here, group_count, per_group),
        kv_groups,
        preferred_element_type=jnp.float32,
    )
    flat_pairs = pairs.reshape(group_count, tokens_here * span)
    flat_pairs = jnp.concatenate(
        [flat_pairs, jnp.zeros((group_count, tokens_here), jnp.float32)], axis=1
    )
    skewed = flat_pairs.reshape(group_count, tokens_here, span + 1)[:, :, :taps]
    local_terms = jnp.sum(skewed, axis=1)[:, ::-1]
    grad_filters = lax.psum(local_terms, "ctx")
    return (grad_q, grad_k, grad_v, grad_filters)


def solution(mesh):
    placed = (
        P("ctx", "fsdp"),
        P("ctx", "fsdp"),
        P("ctx", "fsdp"),
        P("ctx", "fsdp"),
        P("fsdp", None),
        P("ctx", "fsdp"),
    )
    return jax.shard_map(
        per_device,
        mesh=mesh,
        in_specs=placed,
        out_specs=(P("ctx", "fsdp"), P("ctx", "fsdp"), P("ctx", "fsdp"), P("fsdp", None)),
        check_vma=False,
    )
```

profile of v0, /device:TPU:0, one launch (start us, length us, event | category | flops | bytes accessed | tf_op | source)
XLA Modules:
  0.0 940.4 jit_solution(5161514140443520122)
XLA Ops:
  7.2 0.0 all-gather.3.cloned.1.call-start
  7.2 0.7 all-gather.3.cloned.1.call-update
  7.9 0.0 all-gather.5.cloned.1.call-start
  7.9 0.7 all-gather.5.cloned.1.call-update
  8.6 0.0 copy-start.1
  8.7 0.0 all-reduce.5.cloned.1.call-start
  8.7 26.2 %all-gather.3.cloned.1.call-done = bf16[128,8192]{1,0:T(8,128)(2,1)} async-done(((bf16[128,2048]{1,0:T(8,128)(2,1)}), bf16[128,8192]{1,0:T(8,128)(2,1)}) %all-gather.3.cloned.1.call-update) | async-done | bytes 2097168 | tf_op jit(solution)/shard_map/all_gather | solution.py:35
  34.9 639.3 %all-gather.5.cloned.1.call-done = bf16[8192,2048]{1,0:T(8,128)(2,1)} async-done(((bf16[1024,2048]{1,0:T(8,128)(2,1)}), bf16[8192,2048]{1,0:T(8,128)(2,1)}) %all-gather.5.cloned.1.call-update) | async-done | bytes 33554448 | tf_op jit(solution)/shard_map/all_gather | solution.py:38
  674.2 16.7 %multiply_convert_fusion = (bf16[128,2048]{1,0:T(8,128)(2,1)S(1)}, f32[128,2048]{1,0:T(8,128)}) fusion(bf16[128,2048]{1,0:T(8,128)(2,1)} %param.7, bf16[128,8192]{1,0:T(8,128)(2,1)} %all-gather.3.cloned.1.call-done, bf16[8192,2048]{1,0:T(8,128)(2,1)} %all-gather.5.cloned.1.call-done), kind=kOutput, calls=%fused_computation.11 | convolution fusion | flops 4296278016 | bytes 37748736 | tf_op jit(solution)/shard_map/dot_general | solution.py:36
  690.8 1.5 collective-permute-start.1
  692.3 0.0 copy-done.1
  692.3 3.8 tile.20
  696.1 12.3 %copy.23 = bf16[16,8,128,256]{3,1,2,0:T(8,128)(2,1)} copy(bf16[16,8,128,256]{3,2,1,0:T(8,128)(2,1)} %bitcast.26) | data formatting | bytes 16777216
  708.5 7.1 slice.23
  715.6 29.5 %reshape.47 = bf16[128,128,255]{2,1,0:T(8,128)(2,1)} reshape(bf16[128,32640]{1,0:T(8,128)(2,1)} %slice.23) | data formatting | bytes 16711680 | tf_op jit(solution)/shard_map/reshape | solution.py:21
  745.1 0.0 collective-permute-done.1
  745.1 0.1 pad_maximum_fusion.1
  745.2 0.5 copy.18
  745.7 5.6 fusion.5
  751.4 0.4 copy.19
  751.7 2.5 fusion.1
  754.3 0.1 slice.20
  754.4 4.8 collective-permute-start
  759.2 0.1 rev.6
  759.3 3.8 tile.8
  763.1 12.3 %copy.22 = bf16[16,8,128,256]{3,1,2,0:T(8,128)(2,1)} copy(bf16[16,8,128,256]{3,2,1,0:T(8,128)(2,1)} %bitcast.27) | data formatting | bytes 16777216
  775.4 7.1 slice.21
  782.6 29.5 %reshape.44 = bf16[128,128,255]{2,1,0:T(8,128)(2,1)} reshape(bf16[128,32640]{1,0:T(8,128)(2,1)} %slice.21) | data formatting | bytes 16711680 | tf_op jit(solution)/shard_map/reshape | solution.py:21
  812.1 1.0 copy.21
  813.1 0.0 collective-permute-done
  813.1 0.2 pad_maximum_fusion
  813.2 0.5 copy.16
  813.8 5.6 fusion.4
  819.4 0.4 copy.17
  819.8 9.2 fusion.6
  828.9 17.3 %reshape.50 = f32[128,32640]{1,0:T(8,128)} reshape(f32[128,128,255]{2,1,0:T(8,128)} %fusion.6) | data formatting | bytes 33423360 | tf_op jit(solution)/shard_map/reshape | solution.py:65
  846.2 6.5 concatenate.19
  852.7 9.2 copy.24
  861.8 0.0 copy-start
  861.8 1.2 slice_reduce_fusion
  863.1 0.7 rev.7
  863.8 0.0 all-reduce.5.cloned.1.call-update
  863.8 0.0 copy-done
  863.8 0.9 multiply_convert_fusion.1
  864.7 67.7 %all-reduce.5.cloned.1.call-done = f32[128,128]{1,0:T(8,128)} async-done(((f32[128,128]{1,0:T(8,128)}), f32[128,128]{1,0:T(8,128)}) %all-reduce.5.cloned.1.call-update) | async-done | bytes 65552 | tf_op jit(solution)/shard_map/psum | solution.py:71
  932.4 1.5 copy.26
  (2 shorter events, 0.0 us)
Async XLA Ops:
  7.2 27.7 %all-gather.3.cloned.1.call-start = ((), (), s32[]{:S(2)}) async-start(), calls=%async_computation | async-start | bytes 2621440 | tf_op jit(solution)/shard_map/all_gather | solution.py:35
  7.9 666.3 %all-gather.5.cloned.1.call-start = ((), (), s32[]{:S(2)}) async-start(), calls=%async_computation.1 | async-start | bytes 37748736 | tf_op jit(solution)/shard_map/all_gather | solution.py:38
  8.6 683.7 %copy-start.1 = (bf16[128,128]{1,0:T(8,128)(2,1)S(1)}, bf16[128,128]{1,0:T(8,128)(2,1)}, u32[]{:S(2)}) copy-start(bf16[128,128]{1,0:T(8,128)(2,1)} %param.10) | copy-start | bytes 98308
  8.7 923.7 %all-reduce.5.cloned.1.call-start = ((), (), s32[]{:S(2)}) async-start(), calls=%async_computation.2 | async-start | bytes 131072 | tf_op jit(solution)/shard_map/psum | solution.py:71
  690.8 54.2 %collective-permute-start.1 = (bf16[127,2048]{1,0:T(8,128)(2,1)S(1)}, bf16[127,2048]{1,0:T(8,128)(2,1)S(1)}, u32[]{:S(2)}, u32[]{:S(2)}) collective-permute-start(bf16[127,2048]{1,0:T(8,128)(2,1)S(1)} %bitcast.32), channel_id=1, source_target_pairs={{4,0},{8,4},{12,8},{16,12},{20,16},{24,20},{28,24},{5,1},{9,5},{13... | collective-permute-start | bytes 1560584 | tf_op jit(solution)/shard_map/ppermute | solution.py:10
  754.4 58.7 %collective-permute-start = (bf16[127,2048]{1,0:T(8,128)(2,1)S(1)}, bf16[127,2048]{1,0:T(8,128)(2,1)S(1)}, u32[]{:S(2)}, u32[]{:S(2)}) collective-permute-start(bf16[127,2048]{1,0:T(8,128)(2,1)S(1)} %slice.20), channel_id=1, source_target_pairs={{0,4},{4,8},{8,12},{12,16},{16,20},{20,24},{24,28},{1,5},{5,9},{9,... | collective-permute-start | bytes 1560584 | tf_op jit(solution)/shard_map/ppermute | solution.py:10
  861.8 2.0 copy-start
Sparse Core Ops, SparseCore 0:
  9.6 25.2 all-gather.2
  36.4 637.7 all-gather.4
  863.9 68.4 all-reduce.4
where the time goes:
time: 941 us; the launch traced here: 940 us
  waiting for transfers between devices  735 us (78%)
  local copies, waits for them, and re-layouts  144 us (15%)
  matrix products  37.1 us (4%)
  between operations  13.9 us (1%)
    all_gather x1, waiting for transfers between devices, per_device(): lax.all_gather(out_weight, 'ctx', axis=0, tiled=True)  639 us
    psum x1, waiting for transfers between devices, per_device(): grad_filters = lax.psum(local_terms, 'ctx')  67.7 us
    reshape x2, local copies, waits for them, and re-layouts, toeplitz_rows(): return tiled[:, :tokens_here * span].reshape(group_count, tokens_here, span)  59 us
    unnamed x8, local copies, waits for them, and re-layouts  35.3 us
    all_gather x1, waiting for transfers between devices, per_device(): full_grad = lax.all_gather(grad_out, 'fsdp', axis=1, tiled=True)  26.2 us
  transfers between devices with their start and end apart: 5, of which 3 were waited for; matrix products, arithmetic and copies ran while one was open for 11% of the time, Pallas kernels for 0%

commit v1 on v0

v1 whole, which is shorter than its diff:
```python
import jax
import jax.numpy as jnp
from jax import lax
from jax.experimental import pallas as pl
from jax.experimental.pallas import tpu as pltpu
from jax.sharding import PartitionSpec as P

F32 = jnp.float32
BF16 = jnp.bfloat16
LANES = 128


def reversed_bits(value, count):
    out = 0
    for bit in range(count):
        out |= ((value >> bit) & 1) << (count - 1 - bit)
    return out


def traced_reversed_bits(value, count):
    out = jnp.zeros((), jnp.int32)
    for bit in range(count):
        out = out | (((value >> bit) & 1) << (count - 1 - bit))
    return out


def swap(block, axis, mask):
    size = lax.axis_size(axis)
    return lax.ppermute(block, axis, [(i, i ^ mask) for i in range(size)])


def from_behind(block, axis, distance):
    devices = range(lax.axis_size(axis))
    route = [(i - distance, i) for i in devices if i - distance in devices]
    return lax.ppermute(block, axis, route)


def lane_group(rows, per_group):
    return lax.broadcasted_iota(jnp.int32, (rows, LANES), 1) // per_group


def shifted_rows(row, taps, shift):
    wide = jnp.concatenate([row, jnp.zeros((1, taps), F32)], axis=1)
    return pltpu.roll(
        jnp.broadcast_to(wide, (taps, 2 * taps)), shift, 1, stride=1, stride_axis=0
    )


def pick_groups(stacked, taps, per_group):
    groups = LANES // per_group
    lane = lane_group(taps, per_group)
    out = stacked[:taps]
    for g in range(1, groups):
        out = jnp.where(lane == g, stacked[g * taps : (g + 1) * taps], out)
    return out


def make_before_kernel(taps, per_group):
    groups = LANES // per_group

    def kernel(f_ref, frev_ref, kvp_ref, prior_ref, z_ref, near_ref, far_ref, kvrev_ref):
        kv = jnp.concatenate([prior_ref[...], kvp_ref[...]], axis=0)
        rows = []
        for g in range(groups):
            toe = shifted_rows(frev_ref[g : g + 1, :], taps, 1)
            rows.append(toe.astype(BF16))
            back = shifted_rows(f_ref[g : g + 1, :], taps, 0).astype(BF16)
            near_ref[g * taps : (g + 1) * taps, :] = back[:, :taps]
            far_ref[g * taps : (g + 1) * taps, :] = back[:, taps:]
        stacked = jnp.dot(jnp.concatenate(rows, axis=0), kv, preferred_element_type=F32)
        z_ref[...] = pick_groups(stacked, taps, per_group)
        r = lax.broadcasted_iota(jnp.int32, (2 * taps, 2 * taps), 0)
        c = lax.broadcasted_iota(jnp.int32, (2 * taps, 2 * taps), 1)
        flip = jnp.where(r + c == 2 * taps - 1, 1.0, 0.0).astype(BF16)
        kvrev_ref[...] = jnp.dot(flip, kv, preferred_element_type=F32).astype(BF16)

    return kernel


def make_pair_kernel(taps, per_group):
    groups = LANES // per_group

    def kernel(gz_ref, near_ref, kvrev_ref, own_ref, gf_ref):
        gz = gz_ref[...]
        stacked = jnp.dot(near_ref[...], gz, preferred_element_type=F32)
        own_ref[...] = pick_groups(stacked, taps, per_group)
        lane = lane_group(taps, per_group)
        kvrev = kvrev_ref[...]
        zero = jnp.zeros_like(gz)
        for g in range(groups):
            pair = lax.dot_general(
                jnp.where(lane == g, gz, zero),
                kvrev,
                (((1,), (1,)), ((), ())),
                preferred_element_type=F32,
            )
            rolled = pltpu.roll(pair, taps + 1, 1, stride=1, stride_axis=0)
            gf_ref[g : g + 1, :] = jnp.sum(rolled[:, :taps], axis=0, keepdims=True)

    return kernel


def make_after_kernel(taps, per_group):
    def kernel(later_ref, far_ref, own_ref, k_ref, v_ref, gk_ref, gv_ref):
        stacked = jnp.dot(far_ref[...], later_ref[...], preferred_element_type=F32)
        grad_kv = own_ref[...] + pick_groups(stacked, taps, per_group)
        gk_ref[...] = (grad_kv * v_ref[...].astype(F32)).astype(BF16)
        gv_ref[...] = (grad_kv * k_ref[...].astype(F32)).astype(BF16)

    return kernel


def gather_features(grad_out, rows_here):
    n = lax.axis_size("ctx")
    nf = lax.axis_size("fsdp")
    r = n // nf
    bits = nf.bit_length() - 1
    mine = lax.axis_index("ctx")
    pieces = []
    for e in reversed(range(r)):
        route = []
        for i in range(n):
            for dj in range(nf):
                source = i ^ (r * dj + e)
                target = i * nf + reversed_bits(dj, bits)
                route.append((source * nf + i // r, target))
        part = (mine % r) ^ e
        cut = lax.dynamic_slice_in_dim(grad_out, part * rows_here, rows_here, axis=1)
        got = lax.ppermute(cut, ("ctx", "fsdp"), route)
        pieces.append((e, got[None]))
    out = {}
    for e, held in pieces:
        for bit in reversed(range(bits)):
            held = jnp.concatenate([held, swap(held, "fsdp", 1 << bit)], axis=0)
        out[e] = held
    return out


def per_device(grad_out, queries, keys_in, values_in, filters, out_weight):
    n = lax.axis_size("ctx")
    nf = lax.axis_size("fsdp")
    r = n // nf
    bits = nf.bit_length() - 1
    tokens_here, channels = grad_out.shape
    group_count, taps = filters.shape
    per_group = channels // group_count
    groups = LANES // per_group
    octets = channels // LANES
    rows_here = out_weight.shape[0]

    held = gather_features(grad_out, rows_here)
    column = lax.axis_index("fsdp")

    def block(d):
        dj, e = d // r, d % r
        q = reversed_bits(dj, bits) ^ column
        place = traced_reversed_bits(q, bits)
        return lax.dynamic_index_in_dim(held[e], place, 0, keepdims=False)

    kvp = (keys_in.astype(F32) * values_in.astype(F32)).astype(BF16)
    prior = from_behind(kvp, "ctx", 1)

    def partial(blocks):
        lhs = jnp.concatenate([block(d) for d in blocks], axis=0)
        return jnp.dot(lhs, out_weight, preferred_element_type=F32)

    half = max(n // 2, 2)
    sums = {}
    for first in (half, 0):
        odd = [d for d in range(first, first + n // 2) if d & 1]
        even = [d for d in range(first, first + n // 2) if not d & 1]
        sent = swap(partial(odd).astype(BF16), "ctx", 1).astype(F32)
        total = partial(even) + sent
        for at, d in enumerate(even):
            sums[d] = total[at * tokens_here : (at + 1) * tokens_here]
    stage = 2
    while stage < n:
        for d in sorted((d for d in sums if d & stage), reverse=True):
            got = swap(sums.pop(d).astype(BF16), "ctx", stage)
            sums[d ^ stage] = sums[d ^ stage] + got.astype(F32)
        stage *= 2
    grad_y = sums[0].astype(BF16).astype(F32)

    filters32 = filters.astype(F32)
    lane_block = pl.BlockSpec((tokens_here, LANES), lambda o: (0, o))
    filter_block = pl.BlockSpec((groups, taps), lambda o: (o, 0))
    toe_block = pl.BlockSpec((groups * taps, taps), lambda o: (o, 0))
    ext_block = pl.BlockSpec((2 * tokens_here, LANES), lambda o: (0, o))
    toe_shape = jax.ShapeDtypeStruct((group_count * taps, taps), BF16)
    plane32 = jax.ShapeDtypeStruct((tokens_here, channels), F32)
    plane16 = jax.ShapeDtypeStruct((tokens_here, channels), BF16)
    macs = channels * taps * tokens_here * groups
    z_conv, near, far, kvrev = pl.pallas_call(
        make_before_kernel(taps, per_group),
        grid=(octets,),
        in_specs=[filter_block, filter_block, lane_block, lane_block],
        out_specs=[lane_block, toe_block, toe_block, ext_block],
        out_shape=[
            plane32,
            toe_shape,
            toe_shape,
            jax.ShapeDtypeStruct((2 * tokens_here, channels), BF16),
        ],
        cost_estimate=pl.CostEstimate(flops=4 * macs, bytes_accessed=24 << 20, transcendentals=0),
        name="forward_conv",
    )(filters32, filters32[:, ::-1], kvp, prior)

    grad_q = (grad_y * z_conv).astype(BF16)
    grad_z = (grad_y * queries.astype(F32)).astype(BF16)
    later = from_behind(grad_z, "ctx", -1)

    own, local_terms = pl.pallas_call(
        make_pair_kernel(taps, per_group),
        grid=(octets,),
        in_specs=[lane_block, toe_block, ext_block],
        out_specs=[lane_block, filter_block],
        out_shape=[plane32, jax.ShapeDtypeStruct((group_count, taps), F32)],
        cost_estimate=pl.CostEstimate(flops=4 * macs, bytes_accessed=12 << 20, transcendentals=0),
        name="pair_products",
    )(grad_z, near, kvrev)
    grad_filters = local_terms
    stage = 1
    while stage < n:
        grad_filters = grad_filters + swap(grad_filters, "ctx", stage)
        stage *= 2

    grad_k, grad_v = pl.pallas_call(
        make_after_kernel(taps, per_group),
        grid=(octets,),
        in_specs=[lane_block, toe_block, lane_block, lane_block, lane_block],
        out_specs=[lane_block, lane_block],
        out_shape=[plane16, plane16],
        cost_estimate=pl.CostEstimate(flops=2 * macs, bytes_accessed=8 << 20, transcendentals=0),
        name="backward_conv",
    )(later, far, own, keys_in, values_in)
    return (grad_q, grad_k, grad_v, grad_filters)


def solution(mesh):
    placed = (
        P("ctx", "fsdp"),
        P("ctx", "fsdp"),
        P("ctx", "fsdp"),
        P("ctx", "fsdp"),
        P("fsdp", None),
        P("ctx", "fsdp"),
    )
    return jax.shard_map(
        per_device,
        mesh=mesh,
        in_specs=placed,
        out_specs=(P("ctx", "fsdp"), P("ctx", "fsdp"), P("ctx", "fsdp"), P("fsdp", None)),
        check_vma=False,
    )
```

time: 941 us -> 186 us (0.20)
  waiting for transfers between devices: 735 us -> 68.8 us
  local copies, waits for them, and re-layouts: 144 us -> 3.71 us
  starting transfers between devices: 6.37 us -> 62.1 us
  Pallas kernels: 0 us -> 36.5 us
  matrix products: 37.1 us -> 5.11 us
  between operations: 13.9 us -> 0.9 us
    all_gather x2 -> x0, waiting for transfers between devices: 665 us -> none  [the longest x1 639 us: per_device(): lax.all_gather(out_weight, 'ctx', axis=0, tiled=True)]
    reshape x5 -> x0, local copies, waits for them, and re-layouts: 77 us -> none  [the longest x2 59 us: toeplitz_rows(): return tiled[:, :tokens_here * span].reshape(group_count, tokens_here, span)]
    ppermute x0 -> x14, waiting for transfers between devices: none -> 68.8 us  [the longest x12 64.3 us: swap(): return lax.ppermute(block, axis, [(i, i ^ mask) for i in range(size)])]
    psum x1 -> x0, waiting for transfers between devices: 67.7 us -> none  [per_device(): grad_filters = lax.psum(local_terms, 'ctx')]
    ppermute x0 -> x14, starting transfers between devices: none -> 58 us  [the longest x12 54.3 us: swap(): return lax.ppermute(block, axis, [(i, i ^ mask) for i in range(size)])]
    pallas_call x0 -> x3, Pallas kernels: none -> 36.5 us  [the longest x1 13.2 us: per_device(): pl.pallas_call(make_pair_kernel(taps, per_group), grid=(octets,), in_spec...]
    unnamed x8 -> x18, local copies, waits for them, and re-layouts: 35.3 us -> 0.86 us
    dot_general x4, matrix products: 37.1 us -> 5.11 us  [partial(): return jnp.dot(lhs, out_weight, preferred_element_type=F32)]
  transfers between devices with their start and end apart: 5 -> 16, of which waited for: 3 -> 10; matrix products, arithmetic and copies ran while one was open for 11% -> 6% of each run, Pallas kernels for 0% -> 7%
where the time goes in v1:
time: 186 us; the launch traced here: 184 us
  waiting for transfers between devices  68.8 us (37%)
  starting transfers between devices  62.1 us (33%)
  Pallas kernels  36.5 us (20%)
  other arithmetic  6.7 us (4%)
  matrix products  5.11 us (3%)
  local copies, waits for them, and re-layouts  3.71 us (2%)
    ppermute x12, waiting for transfers between devices, swap(): return lax.ppermute(block, axis, [(i, i ^ mask) for i in range(size)])  64.3 us
    ppermute x12, starting transfers between devices, swap(): return lax.ppermute(block, axis, [(i, i ^ mask) for i in range(size)])  54.3 us
    pallas_call x1, Pallas kernels, per_device(): pl.pallas_call(make_pair_kernel(taps, per_group), grid=(octets,), in_spec...  13.2 us
    pallas_call x1, Pallas kernels, per_device(): pl.pallas_call(make_before_kernel(taps, per_group), grid=(octets,), in_sp...  12.1 us
    pallas_call x1, Pallas kernels, per_device(): pl.pallas_call(make_after_kernel(taps, per_group), grid=(octets,), in_spe...  11.1 us
    dot_general x4, matrix products, partial(): return jnp.dot(lhs, out_weight, preferred_element_type=F32)  5.11 us
    ppermute x2, waiting for transfers between devices, gather_features(): got = lax.ppermute(cut, ('ctx', 'fsdp'), route)  4.57 us
    ppermute x2, starting transfers between devices, from_behind(): return lax.ppermute(block, axis, route)  4.16 us
  transfers between devices with their start and end apart: 16, of which 10 were waited for; matrix products, arithmetic and copies ran while one was open for 6% of the time, Pallas kernels for 7%

profile of v1, /device:TPU:0, one launch (start us, length us, event | category | flops | bytes accessed | tf_op | source)
XLA Modules:
  0.0 183.8 jit_solution(13139051038051387472)
XLA Ops:
  0.7 1.1 constant_dynamic-slice_fusion.1
  1.7 3.0 %collective-permute-start.3 = (bf16[128,1024]{1,0:T(8,128)(2,1)S(1)}, bf16[128,1024]{1,0:T(8,128)(2,1)S(1)}, u32[]{:S(2)}, u32[]{:S(2)}) collective-permute-start(bf16[128,1024]{1,0:T(8,128)(2,1)S(1)} %get-tuple-element.31), channel_id=1, source_target_pairs={{4,0},{12,2},{20,1},{28,3},{0,4},{8,6},{16,5},{24,7},{13,8},{5,10}... | collective-permute-start | bytes 786440 | tf_op jit(solution)/shard_map/ppermute | solution.py:129
  4.8 4.6 %collective-permute-done.3 = bf16[128,1024]{1,0:T(8,128)(2,1)S(1)} collective-permute-done((bf16[128,1024]{1,0:T(8,128)(2,1)S(1)}, bf16[128,1024]{1,0:T(8,128)(2,1)S(1)}, u32[]{:S(2)}, u32[]{:S(2)}) %collective-permute-start.3) | collective-permute-done | bytes 262176 | tf_op jit(solution)/shard_map/ppermute | solution.py:129
  9.3 5.0 %collective-permute-start.4 = (bf16[1,128,1024]{2,1,0:T(8,128)(2,1)S(1)}, bf16[1,128,1024]{2,1,0:T(8,128)(2,1)S(1)}, u32[]{:S(2)}, u32[]{:S(2)}) collective-permute-start(bf16[1,128,1024]{2,1,0:T(8,128)(2,1)S(1)} %bitcast.25), channel_id=1, source_target_pairs={{0,2},{1,3},{2,0},{3,1},{4,6},{5,7},{6,4},{7,5},{8,10},{9,11},{10,... | collective-permute-start | bytes 786440 | tf_op jit(solution)/shard_map/ppermute | solution.py:29
  14.3 4.3 %collective-permute-done.4 = bf16[1,128,1024]{2,1,0:T(8,128)(2,1)S(1)} collective-permute-done((bf16[1,128,1024]{2,1,0:T(8,128)(2,1)S(1)}, bf16[1,128,1024]{2,1,0:T(8,128)(2,1)S(1)}, u32[]{:S(2)}, u32[]{:S(2)}) %collective-permute-start.4) | collective-permute-done | bytes 262176 | tf_op jit(solution)/shard_map/ppermute | solution.py:29
  18.7 0.1 pad_maximum_fusion.3
  18.7 5.8 %collective-permute-start.5 = (bf16[2,128,1024]{2,1,0:T(8,128)(2,1)S(1)}, bf16[2,128,1024]{2,1,0:T(8,128)(2,1)S(1)}, u32[]{:S(2)}, u32[]{:S(2)}) collective-permute-start(bf16[2,128,1024]{2,1,0:T(8,128)(2,1)S(1)} %pad_maximum_fusion.3), channel_id=1, source_target_pairs={{0,1},{1,0},{2,3},{3,2},{4,5},{5,4},{6,7},{7,6},{8,9},{9,8},{10,11... | collective-permute-start | bytes 1572872 | tf_op jit(solution)/shard_map/ppermute | solution.py:29
  24.5 0.7 collective-permute-start
  25.3 0.0 copy-start.8
  25.3 0.0 collective-permute-done
  25.3 13.1 %collective-permute-start.1 = (bf16[1,128,1024]{2,1,0:T(8,128)(2,1)S(1)}, bf16[1,128,1024]{2,1,0:T(8,128)(2,1)S(1)}, u32[]{:S(2)}, u32[]{:S(2)}) collective-permute-start(bf16[1,128,1024]{2,1,0:T(8,128)(2,1)S(1)} %bitcast.22), channel_id=1, source_target_pairs={{0,2},{1,3},{2,0},{3,1},{4,6},{5,7},{6,4},{7,5},{8,10},{9,11},{10,... | collective-permute-start | bytes 786440 | tf_op jit(solution)/shard_map/ppermute | solution.py:29
  38.4 0.0 collective-permute-done.5
  38.4 0.1 pad_maximum_fusion.1
  38.5 0.1 dynamic-slice_bitcast_fusion.5
  38.6 0.0 copy-done.8
  38.6 1.3 convolution_convert_fusion
  39.9 0.1 collective-permute-start.8
  40.0 2.8 %collective-permute-done.1 = bf16[1,128,1024]{2,1,0:T(8,128)(2,1)S(1)} collective-permute-done((bf16[1,128,1024]{2,1,0:T(8,128)(2,1)S(1)}, bf16[1,128,1024]{2,1,0:T(8,128)(2,1)S(1)}, u32[]{:S(2)}, u32[]{:S(2)}) %collective-permute-start.1) | collective-permute-done | bytes 262176 | tf_op jit(solution)/shard_map/ppermute | solution.py:29
  42.8 0.1 pad_maximum_fusion.2
  42.8 4.3 %collective-permute-start.2 = (bf16[2,128,1024]{2,1,0:T(8,128)(2,1)S(1)}, bf16[2,128,1024]{2,1,0:T(8,128)(2,1)S(1)}, u32[]{:S(2)}, u32[]{:S(2)}) collective-permute-start(bf16[2,128,1024]{2,1,0:T(8,128)(2,1)S(1)} %pad_maximum_fusion.2), channel_id=1, source_target_pairs={{0,1},{1,0},{2,3},{3,2},{4,5},{5,4},{6,7},{7,6},{8,9},{9,8},{10,11... | collective-permute-start | bytes 1572872 | tf_op jit(solution)/shard_map/ppermute | solution.py:29
  47.2 1.3 convolution_convert_fusion.1
  48.4 0.9 collective-permute-start.6
  49.3 0.0 collective-permute-done.2
  49.3 0.1 pad_maximum_fusion
  49.4 0.1 dynamic-slice_bitcast_fusion.7
  49.5 14.3 %collective-permute-done.8 = bf16[256,2048]{1,0:T(8,128)(2,1)S(1)} collective-permute-done((bf16[256,2048]{1,0:T(8,128)(2,1)S(1)}, bf16[256,2048]{1,0:T(8,128)(2,1)S(1)}, u32[]{:S(2)}, u32[]{:S(2)}) %collective-permute-start.8) | collective-permute-done | bytes 1048608 | tf_op jit(solution)/shard_map/ppermute | solution.py:29
  63.8 1.3 convert_add_fusion
  65.1 0.1 slice.32
  65.2 7.0 %collective-permute-start.9 = (bf16[128,2048]{1,0:T(8,128)(2,1)S(1)}, bf16[128,2048]{1,0:T(8,128)(2,1)S(1)}, u32[]{:S(2)}, u32[]{:S(2)}) collective-permute-start(bf16[128,2048]{1,0:T(8,128)(2,1)S(1)} %slice.32), channel_id=1, source_target_pairs={{0,8},{4,12},{8,0},{12,4},{16,24},{20,28},{24,16},{28,20},{1,9},{5... | collective-permute-start | bytes 1572872 | tf_op jit(solution)/shard_map/ppermute | solution.py:29
  72.1 0.0 copy-done
  72.1 0.1 multiply_convert_fusion.kvp_ref
  72.3 0.0 copy-start.5
  72.3 2.9 %collective-permute-start.11 = (bf16[128,2048]{1,0:T(8,128)(2,1)S(1)}, bf16[128,2048]{1,0:T(8,128)(2,1)}, u32[]{:S(2)}, u32[]{:S(2)}) collective-permute-start(bf16[128,2048]{1,0:T(8,128)(2,1)S(1)} %multiply_convert_fusion.kvp_ref), channel_id=1, source_target_pairs={{0,4},{4,8},{8,12},{12,16},{16,20},{20,24},{24,28},{1,5},{5,9},{9,... | collective-permute-start | bytes 1572872 | tf_op jit(solution)/shard_map/ppermute | solution.py:35
  75.1 11.1 %collective-permute-done.6 = bf16[256,2048]{1,0:T(8,128)(2,1)S(1)} collective-permute-done((bf16[256,2048]{1,0:T(8,128)(2,1)S(1)}, bf16[256,2048]{1,0:T(8,128)(2,1)S(1)}, u32[]{:S(2)}, u32[]{:S(2)}) %collective-permute-start.6) | collective-permute-done | bytes 1048608 | tf_op jit(solution)/shard_map/ppermute | solution.py:29
  86.3 1.3 convert_add_fusion.1
  87.6 0.0 copy-start.4
  87.6 0.9 slice.33
  88.4 17.9 %collective-permute-start.7 = (bf16[128,2048]{1,0:T(8,128)(2,1)}, bf16[128,2048]{1,0:T(8,128)(2,1)}, u32[]{:S(2)}, u32[]{:S(2)}) collective-permute-start(bf16[128,2048]{1,0:T(8,128)(2,1)} %slice.33), channel_id=1, source_target_pairs={{0,8},{4,12},{8,0},{12,4},{16,24},{20,28},{24,16},{28,20},{1,9},{5... | collective-permute-start | bytes 1572872 | tf_op jit(solution)/shard_map/ppermute | solution.py:29
  106.4 0.0 collective-permute-done.9
  106.4 0.9 fusion.2
  107.3 0.0 collective-permute-start.10
  107.3 0.0 copy-done.7
  107.3 0.6 convert_element_type.63.f_ref
  107.9 0.7 rev.3.frev_ref
  108.6 0.0 collective-permute-done.11.prior_ref
  108.6 12.1 %forward_conv.1 = (f32[128,2048]{1,0:T(8,128)}, bf16[16384,128]{1,0:T(8,128)(2,1)}, bf16[16384,128]{1,0:T(8,128)(2,1)}, bf16[256,2048]{1,0:T(8,128)(2,1)}) custom-call(f32[128,128]{1,0:T(8,128)} %convert_element_type.63.f_ref, f32[128,128]{1,0:T(8,128)} %rev.3.frev_ref, bf16[128,2048]{1,0:T(8,128)(2,1)} %copy-done.5, ...), custom_call_target="tpu_custom_call" | custom-call | flops 1073741824 | bytes 25165824 | tf_op jit(solution)/shard_map/forward_conv/pallas_call | solution.py:193
  120.8 3.8 %collective-permute-done.7 = bf16[128,2048]{1,0:T(8,128)(2,1)} collective-permute-done((bf16[128,2048]{1,0:T(8,128)(2,1)}, bf16[128,2048]{1,0:T(8,128)(2,1)}, u32[]{:S(2)}, u32[]{:S(2)}) %collective-permute-start.7) | collective-permute-done | bytes 524320 | tf_op jit(solution)/shard_map/ppermute | solution.py:29
  124.6 8.6 %collective-permute-done.10 = bf16[128,2048]{1,0:T(8,128)(2,1)} collective-permute-done((bf16[128,2048]{1,0:T(8,128)(2,1)}, bf16[128,2048]{1,0:T(8,128)(2,1)}, u32[]{:S(2)}, u32[]{:S(2)}) %collective-permute-start.10) | collective-permute-done | bytes 524320 | tf_op jit(solution)/shard_map/ppermute | solution.py:29
  133.3 2.3 %fusion.1 = (bf16[128,2048]{1,0:T(8,128)(2,1)}, bf16[128,2048]{1,0:T(8,128)(2,1)S(1)}) fusion(bf16[128,2048]{1,0:T(8,128)(2,1)S(1)} %copy-done.4, bf16[128,2048]{1,0:T(8,128)(2,1)} %collective-permute-done.10, bf16[128,2048]{1,0:T(8,128)(2,1)} %collective-permute-done.7, f32[256,2048]{1,0:T(8,128)S(1)} %convert_add_fusion.1), kind=kLoop, calls=%fused_computation.7 | loop fusion | flops 2359296 | bytes 3670016 | tf_op jit(solution)/shard_map/convert_element_type | solution.py:209
  135.6 13.2 %pair_products.1 = (f32[128,2048]{1,0:T(8,128)}, f32[128,128]{1,0:T(8,128)}) custom-call(bf16[128,2048]{1,0:T(8,128)(2,1)} %get-tuple-element.20.gz_ref, bf16[16384,128]{1,0:T(8,128)(2,1)} %get-tuple-element.14.near_ref, bf16[256,2048]{1,0:T(8,128)(2,1)} %get-tuple-element.15.kvrev_ref), custom_call_target="tpu_custom_call" | custom-call | flops 1073741824 | bytes 12582912 | tf_op jit(solution)/shard_map/pair_products/pallas_call | solution.py:212
  148.8 0.0 collective-permute-start.13
  148.8 4.5 %collective-permute-done.13 = f32[128,128]{1,0:T(8,128)S(1)} collective-permute-done((f32[128,128]{1,0:T(8,128)}, f32[128,128]{1,0:T(8,128)S(1)}, u32[]{:S(2)}, u32[]{:S(2)}) %collective-permute-start.13) | collective-permute-done | bytes 65568 | tf_op jit(solution)/shard_map/ppermute | solution.py:29
  153.3 0.9 add.64
  154.1 0.1 collective-permute-start.14
  154.2 0.0 copy-done.2
  154.2 1.3 collective-permute-start.12
  155.5 3.7 %collective-permute-done.14 = f32[128,128]{1,0:T(8,128)S(1)} collective-permute-done((f32[128,128]{1,0:T(8,128)S(1)}, f32[128,128]{1,0:T(8,128)S(1)}, u32[]{:S(2)}, u32[]{:S(2)}) %collective-permute-start.14) | collective-permute-done | bytes 65568 | tf_op jit(solution)/shard_map/ppermute | solution.py:29
  159.2 0.1 collective-permute-start.15
  159.3 0.9 fusion
  160.2 11.0 %collective-permute-done.15 = f32[128,128]{1,0:T(8,128)S(1)} collective-permute-done((f32[128,128]{1,0:T(8,128)S(1)}, f32[128,128]{1,0:T(8,128)S(1)}, u32[]{:S(2)}, u32[]{:S(2)}) %collective-permute-start.15) | collective-permute-done | bytes 65568 | tf_op jit(solution)/shard_map/ppermute | solution.py:29
  171.3 0.6 add.66
  171.9 0.0 collective-permute-done.12.later_ref
  171.9 0.8 copy-done.6
  172.7 11.1 %backward_conv.1 = (bf16[128,2048]{1,0:T(8,128)(2,1)}, bf16[128,2048]{1,0:T(8,128)(2,1)}) custom-call(bf16[128,2048]{1,0:T(8,128)(2,1)} %copy-done.6, bf16[16384,128]{1,0:T(8,128)(2,1)} %get-tuple-element.13.far_ref, f32[128,2048]{1,0:T(8,128)} %get-tuple-element.16.own_ref, bf16[128,2048]{1,0:T(8,128)(2,1)} %k_ref.1, bf16[128,2048]{1,0:T(8,128)(2,1)} %v_ref.1), custom_call_target="tpu_custom_call" | custom-call | flops 536870912 | bytes 8388608 | tf_op jit(solution)/shard_map/backward_conv/pallas_call | solution.py:227
  (11 shorter events, 0.0 us)
Async XLA Ops:
  1.7 7.6 %collective-permute-start.3 = (bf16[128,1024]{1,0:T(8,128)(2,1)S(1)}, bf16[128,1024]{1,0:T(8,128)(2,1)S(1)}, u32[]{:S(2)}, u32[]{:S(2)}) collective-permute-start(bf16[128,1024]{1,0:T(8,128)(2,1)S(1)} %get-tuple-element.31), channel_id=1, source_target_pairs={{4,0},{12,2},{20,1},{28,3},{0,4},{8,6},{16,5},{24,7},{13,8},{5,10}... | collective-permute-start | bytes 786440 | tf_op jit(solution)/shard_map/ppermute | solution.py:129
  9.3 9.4 %collective-permute-start.4 = (bf16[1,128,1024]{2,1,0:T(8,128)(2,1)S(1)}, bf16[1,128,1024]{2,1,0:T(8,128)(2,1)S(1)}, u32[]{:S(2)}, u32[]{:S(2)}) collective-permute-start(bf16[1,128,1024]{2,1,0:T(8,128)(2,1)S(1)} %bitcast.25), channel_id=1, source_target_pairs={{0,2},{1,3},{2,0},{3,1},{4,6},{5,7},{6,4},{7,5},{8,10},{9,11},{10,... | collective-permute-start | bytes 786440 | tf_op jit(solution)/shard_map/ppermute | solution.py:29
  18.7 19.7 %collective-permute-start.5 = (bf16[2,128,1024]{2,1,0:T(8,128)(2,1)S(1)}, bf16[2,128,1024]{2,1,0:T(8,128)(2,1)S(1)}, u32[]{:S(2)}, u32[]{:S(2)}) collective-permute-start(bf16[2,128,1024]{2,1,0:T(8,128)(2,1)S(1)} %pad_maximum_fusion.3), channel_id=1, source_target_pairs={{0,1},{1,0},{2,3},{3,2},{4,5},{5,4},{6,7},{7,6},{8,9},{9,8},{10,11... | collective-permute-start | bytes 1572872 | tf_op jit(solution)/shard_map/ppermute | solution.py:29
  24.5 0.7 collective-permute-start
  25.3 13.4 %copy-start.8 = (bf16[1024,2048]{1,0:T(8,128)(2,1)S(1)}, bf16[1024,2048]{1,0:T(8,128)(2,1)}, u32[]{:S(2)}) copy-start(bf16[1024,2048]{1,0:T(8,128)(2,1)} %param.11) | copy-start | bytes 12582916
  25.3 17.5 %collective-permute-start.1 = (bf16[1,128,1024]{2,1,0:T(8,128)(2,1)S(1)}, bf16[1,128,1024]{2,1,0:T(8,128)(2,1)S(1)}, u32[]{:S(2)}, u32[]{:S(2)}) collective-permute-start(bf16[1,128,1024]{2,1,0:T(8,128)(2,1)S(1)} %bitcast.22), channel_id=1, source_target_pairs={{0,2},{1,3},{2,0},{3,1},{4,6},{5,7},{6,4},{7,5},{8,10},{9,11},{10,... | collective-permute-start | bytes 786440 | tf_op jit(solution)/shard_map/ppermute | solution.py:29
  39.9 23.9 %collective-permute-start.8 = (bf16[256,2048]{1,0:T(8,128)(2,1)S(1)}, bf16[256,2048]{1,0:T(8,128)(2,1)S(1)}, u32[]{:S(2)}, u32[]{:S(2)}) collective-permute-start(bf16[256,2048]{1,0:T(8,128)(2,1)S(1)} %convolution_convert_fusion), channel_id=1, source_target_pairs={{0,4},{4,0},{8,12},{12,8},{16,20},{20,16},{24,28},{28,24},{1,5},{5... | collective-permute-start | bytes 3145736 | tf_op jit(solution)/shard_map/ppermute | solution.py:29
  42.8 6.5 %collective-permute-start.2 = (bf16[2,128,1024]{2,1,0:T(8,128)(2,1)S(1)}, bf16[2,128,1024]{2,1,0:T(8,128)(2,1)S(1)}, u32[]{:S(2)}, u32[]{:S(2)}) collective-permute-start(bf16[2,128,1024]{2,1,0:T(8,128)(2,1)S(1)} %pad_maximum_fusion.2), channel_id=1, source_target_pairs={{0,1},{1,0},{2,3},{3,2},{4,5},{5,4},{6,7},{7,6},{8,9},{9,8},{10,11... | collective-permute-start | bytes 1572872 | tf_op jit(solution)/shard_map/ppermute | solution.py:29
  48.4 37.8 %collective-permute-start.6 = (bf16[256,2048]{1,0:T(8,128)(2,1)S(1)}, bf16[256,2048]{1,0:T(8,128)(2,1)S(1)}, u32[]{:S(2)}, u32[]{:S(2)}) collective-permute-start(bf16[256,2048]{1,0:T(8,128)(2,1)S(1)} %convolution_convert_fusion.1), channel_id=1, source_target_pairs={{0,4},{4,0},{8,12},{12,8},{16,20},{20,16},{24,28},{28,24},{1,5},{5... | collective-permute-start | bytes 3145736 | tf_op jit(solution)/shard_map/ppermute | solution.py:29
  63.8 8.3 %copy-start = (bf16[128,2048]{1,0:T(8,128)(2,1)S(1)}, bf16[128,2048]{1,0:T(8,128)(2,1)}, u32[]{:S(2)}) copy-start(bf16[128,2048]{1,0:T(8,128)(2,1)} %v_ref.1) | copy-start | bytes 1572868
  63.8 8.3 %copy-start.1 = (bf16[128,2048]{1,0:T(8,128)(2,1)S(1)}, bf16[128,2048]{1,0:T(8,128)(2,1)}, u32[]{:S(2)}) copy-start(bf16[128,2048]{1,0:T(8,128)(2,1)} %k_ref.1) | copy-start | bytes 1572868
  65.2 41.2 %collective-permute-start.9 = (bf16[128,2048]{1,0:T(8,128)(2,1)S(1)}, bf16[128,2048]{1,0:T(8,128)(2,1)S(1)}, u32[]{:S(2)}, u32[]{:S(2)}) collective-permute-start(bf16[128,2048]{1,0:T(8,128)(2,1)S(1)} %slice.32), channel_id=1, source_target_pairs={{0,8},{4,12},{8,0},{12,4},{16,24},{20,28},{24,16},{28,20},{1,9},{5... | collective-permute-start | bytes 1572872 | tf_op jit(solution)/shard_map/ppermute | solution.py:29
  72.3 15.3 %copy-start.5 = (bf16[128,2048]{1,0:T(8,128)(2,1)}, bf16[128,2048]{1,0:T(8,128)(2,1)S(1)}, u32[]{:S(2)}) copy-start(bf16[128,2048]{1,0:T(8,128)(2,1)S(1)} %multiply_convert_fusion.kvp_ref) | copy-start | bytes 1572868
  72.3 36.4 %collective-permute-start.11 = (bf16[128,2048]{1,0:T(8,128)(2,1)S(1)}, bf16[128,2048]{1,0:T(8,128)(2,1)}, u32[]{:S(2)}, u32[]{:S(2)}) collective-permute-start(bf16[128,2048]{1,0:T(8,128)(2,1)S(1)} %multiply_convert_fusion.kvp_ref), channel_id=1, source_target_pairs={{0,4},{4,8},{8,12},{12,16},{16,20},{20,24},{24,28},{1,5},{5,9},{9,... | collective-permute-start | bytes 1572872 | tf_op jit(solution)/shard_map/ppermute | solution.py:35
  86.3 21.0 %copy-start.7 = (bf16[128,128]{1,0:T(8,128)(2,1)S(1)}, bf16[128,128]{1,0:T(8,128)(2,1)}, u32[]{:S(2)}) copy-start(bf16[128,128]{1,0:T(8,128)(2,1)} %param.10) | copy-start | bytes 98308
  87.6 45.7 %copy-start.4 = (bf16[128,2048]{1,0:T(8,128)(2,1)S(1)}, bf16[128,2048]{1,0:T(8,128)(2,1)}, u32[]{:S(2)}) copy-start(bf16[128,2048]{1,0:T(8,128)(2,1)} %param.7) | copy-start | bytes 1572868
  88.4 36.2 %collective-permute-start.7 = (bf16[128,2048]{1,0:T(8,128)(2,1)}, bf16[128,2048]{1,0:T(8,128)(2,1)}, u32[]{:S(2)}, u32[]{:S(2)}) collective-permute-start(bf16[128,2048]{1,0:T(8,128)(2,1)} %slice.33), channel_id=1, source_target_pairs={{0,8},{4,12},{8,0},{12,4},{16,24},{20,28},{24,16},{28,20},{1,9},{5... | collective-permute-start | bytes 1572872 | tf_op jit(solution)/shard_map/ppermute | solution.py:29
  107.3 26.0 %collective-permute-start.10 = (bf16[128,2048]{1,0:T(8,128)(2,1)}, bf16[128,2048]{1,0:T(8,128)(2,1)}, u32[]{:S(2)}, u32[]{:S(2)}) collective-permute-start(bf16[128,2048]{1,0:T(8,128)(2,1)} %fusion.2), channel_id=1, source_target_pairs={{0,16},{4,20},{8,24},{12,28},{16,0},{20,4},{24,8},{28,12},{1,17},{... | collective-permute-start | bytes 1572872 | tf_op jit(solution)/shard_map/ppermute | solution.py:29
  135.6 18.6 %copy-start.2 = (bf16[128,2048]{1,0:T(8,128)(2,1)S(1)}, bf16[128,2048]{1,0:T(8,128)(2,1)}, u32[]{:S(2)}) copy-start(bf16[128,2048]{1,0:T(8,128)(2,1)} %get-tuple-element.20.gz_ref) | copy-start | bytes 1572868
  135.6 23.7 %copy-start.3 = (f32[128,2048]{1,0:T(8,128)S(1)}, f32[128,2048]{1,0:T(8,128)}, u32[]{:S(2)}) copy-start(f32[128,2048]{1,0:T(8,128)} %get-tuple-element.12) | copy-start | bytes 3145732
  148.8 4.5 %collective-permute-start.13 = (f32[128,128]{1,0:T(8,128)}, f32[128,128]{1,0:T(8,128)S(1)}, u32[]{:S(2)}, u32[]{:S(2)}) collective-permute-start(f32[128,128]{1,0:T(8,128)} %get-tuple-element.19), channel_id=1, source_target_pairs={{0,4},{4,0},{8,12},{12,8},{16,20},{20,16},{24,28},{28,24},{1,5},{5... | collective-permute-start | bytes 196616 | tf_op jit(solution)/shard_map/ppermute | solution.py:29
  154.1 5.1 %collective-permute-start.14 = (f32[128,128]{1,0:T(8,128)S(1)}, f32[128,128]{1,0:T(8,128)S(1)}, u32[]{:S(2)}, u32[]{:S(2)}) collective-permute-start(f32[128,128]{1,0:T(8,128)S(1)} %add.64), channel_id=1, source_target_pairs={{0,8},{4,12},{8,0},{12,4},{16,24},{20,28},{24,16},{28,20},{1,9},{5... | collective-permute-start | bytes 196616 | tf_op jit(solution)/shard_map/ppermute | solution.py:29
  154.2 17.7 %collective-permute-start.12 = (bf16[128,2048]{1,0:T(8,128)(2,1)S(1)}, bf16[128,2048]{1,0:T(8,128)(2,1)S(1)}, u32[]{:S(2)}, u32[]{:S(2)}) collective-permute-start(bf16[128,2048]{1,0:T(8,128)(2,1)S(1)} %copy-done.2), channel_id=1, source_target_pairs={{4,0},{8,4},{12,8},{16,12},{20,16},{24,20},{28,24},{5,1},{9,5},{13... | collective-permute-start | bytes 1572872 | tf_op jit(solution)/shard_map/ppermute | solution.py:35
  159.2 12.0 %collective-permute-start.15 = (f32[128,128]{1,0:T(8,128)S(1)}, f32[128,128]{1,0:T(8,128)S(1)}, u32[]{:S(2)}, u32[]{:S(2)}) collective-permute-start(f32[128,128]{1,0:T(8,128)S(1)} %add.65), channel_id=1, source_target_pairs={{0,16},{4,20},{8,24},{12,28},{16,0},{20,4},{24,8},{28,12},{1,17},{... | collective-permute-start | bytes 196616 | tf_op jit(solution)/shard_map/ppermute | solution.py:29
  171.9 0.8 copy-start.6

commit v2 on v0

v2 whole, which is shorter than its diff:
```python
import jax
import jax.numpy as jnp
from jax import lax
from jax.experimental import pallas as pl
from jax.experimental.pallas import tpu as pltpu
from jax.sharding import PartitionSpec as P

F32 = jnp.float32
BF16 = jnp.bfloat16
LANES = 128
PARTS = 1
KQ = 9
ZQ = 2
DET = True
DIRECT = 3
ROWS = 32


def reversed_bits(value, count):
    out = 0
    for bit in range(count):
        out |= ((value >> bit) & 1) << (count - 1 - bit)
    return out


def swap(block, axis, mask):
    size = lax.axis_size(axis)
    return lax.ppermute(block, axis, [(i, i ^ mask) for i in range(size)])


def from_behind(block, axis, distance):
    devices = range(lax.axis_size(axis))
    route = [(i - distance, i) for i in devices if i - distance in devices]
    return lax.ppermute(block, axis, route)


def lane_group(rows, per_group):
    return lax.broadcasted_iota(jnp.int32, (rows, LANES), 1) // per_group


def shifted_rows(row, taps, shift):
    wide = jnp.concatenate([row, jnp.zeros((1, taps), F32)], axis=1)
    return pltpu.roll(
        jnp.broadcast_to(wide, (taps, 2 * taps)), shift, 1, stride=1, stride_axis=0
    )


def pick_groups(stacked, taps, per_group):
    groups = LANES // per_group
    lane = lane_group(taps, per_group)
    out = stacked[:taps]
    for g in range(1, groups):
        out = jnp.where(lane == g, stacked[g * taps : (g + 1) * taps], out)
    return out


def make_before_kernel(taps, per_group, octets):
    groups = LANES // per_group

    def kernel(f_ref, frev_ref, kvp_ref, prior_ref, z_ref, toe_ref, kvrev_ref):
        r = lax.broadcasted_iota(jnp.int32, (2 * taps, 2 * taps), 0)
        c = lax.broadcasted_iota(jnp.int32, (2 * taps, 2 * taps), 1)
        flip = jnp.where(r + c == 2 * taps - 1, 1.0, 0.0).astype(BF16)
        for o in range(octets):
            lanes = slice(o * LANES, (o + 1) * LANES)
            kv = jnp.concatenate([prior_ref[:, lanes], kvp_ref[:, lanes]], axis=0)
            rows = []
            for g in range(o * groups, (o + 1) * groups):
                toe = shifted_rows(frev_ref[g : g + 1, :], taps, 1)
                rows.append(toe.astype(BF16))
                back = shifted_rows(f_ref[g : g + 1, :], taps, 0).astype(BF16)
                toe_ref[g * taps : (g + 1) * taps, :] = back
            stacked = jnp.dot(jnp.concatenate(rows, axis=0), kv, preferred_element_type=F32)
            z_ref[:, lanes] = pick_groups(stacked, taps, per_group)
            kvrev_ref[: taps - ROWS, lanes] = jnp.zeros((taps - ROWS, LANES), BF16)
            kvrev_ref[taps - ROWS :, lanes] = jnp.dot(flip, kv, preferred_element_type=F32).astype(BF16)

    return kernel


def make_pair_kernel(taps, per_group, octets):
    groups = LANES // per_group

    def kernel(gz_ref, kvrev_ref, gf_ref):
        lane = lane_group(taps, per_group)
        for o in range(octets):
            lanes = slice(o * LANES, (o + 1) * LANES)
            gz = gz_ref[:, lanes]
            zero = jnp.zeros((ROWS, LANES), BF16)
            pairs = None
            for at in range(0, taps, ROWS):
                rows = gz[at : at + ROWS]
                split = [jnp.where(lane[:ROWS] == g, rows, zero) for g in range(groups)]
                start = taps - ROWS - at
                term = lax.dot_general(
                    jnp.concatenate(split, axis=0),
                    kvrev_ref[start : start + 2 * taps, lanes],
                    (((1,), (1,)), ((), ())),
                    preferred_element_type=F32,
                )
                pairs = term if pairs is None else pairs + term
            for g in range(groups):
                pair = pairs[g * ROWS : (g + 1) * ROWS]
                rolled = pltpu.roll(pair, taps + 1, 1, stride=1, stride_axis=0)
                row = o * groups + g
                gf_ref[row : row + 1, :] = jnp.sum(rolled[:, :taps], axis=0, keepdims=True)

    return kernel


def make_after_kernel(taps, per_group, octets):
    groups = LANES // per_group

    def kernel(gz_ref, later_ref, toe_ref, k_ref, v_ref, *refs):
        gk_ref, gv_ref = refs[-2:]
        for o in range(octets):
            lanes = slice(o * LANES, (o + 1) * LANES)
            toes = slice(o * groups * taps, (o + 1) * groups * taps)
            ext = jnp.concatenate([gz_ref[:, lanes], later_ref[:, lanes]], axis=0)
            stacked = jnp.dot(toe_ref[toes, :], ext, preferred_element_type=F32)
            grad_kv = pick_groups(stacked, taps, per_group)
            gk_ref[:, lanes] = (grad_kv * v_ref[:, lanes].astype(F32)).astype(BF16)
            gv_ref[:, lanes] = (grad_kv * k_ref[:, lanes].astype(F32)).astype(BF16)

    return kernel


def first_piece(grad_out, rows_here, e):
    n = lax.axis_size("ctx")
    nf = lax.axis_size("fsdp")
    r = n // nf
    bits = nf.bit_length() - 1
    mine = lax.axis_index("ctx")
    detour = nf // 2 if DET and (r - 1 - e) % 2 else 0
    route = []
    for i in range(n):
        for dj in range(nf):
            source = i ^ (r * dj + e)
            target = i * nf + reversed_bits(dj, bits)
            route.append((source * nf + ((i // r) ^ detour), target))
    part = (mine % r) ^ e
    cut = lax.dynamic_slice_in_dim(grad_out, part * rows_here, rows_here, axis=1)
    if detour:
        cut = swap(cut, "fsdp", detour)
    return lax.ppermute(cut, ("ctx", "fsdp"), route)


def block_before(kvp):
    n = lax.axis_size("ctx")
    mine = lax.axis_index("ctx")
    near = swap(kvp, "ctx", 1)
    far = lax.ppermute(near, "ctx", [(i, i + 2) for i in range(0, n - 2, 2)])
    return jnp.where(mine % 2 == 1, near, far)


def to_owner(block, q):
    n = lax.axis_size("ctx")
    nf = lax.axis_size("fsdp")
    r = n // nf
    bits = nf.bit_length() - 1
    route = []
    for i in range(n):
        for j in range(nf):
            dj = reversed_bits(j ^ q, bits)
            route.append((i * nf + j, (i ^ (r * dj)) * nf + j))
    return lax.ppermute(block, ("ctx", "fsdp"), route)


def tree_sum(values):
    while len(values) > 1:
        values = [a + b for a, b in zip(values[::2], values[1::2])]
    return values[0]


def summed_over_ctx(value, after):
    n = lax.axis_size("ctx")
    stride = 1
    while stride < n:
        reach = min(DIRECT + 1, n // stride)
        sent = value.astype(BF16)
        got = [swap(sent, "ctx", k * stride) for k in range(1, reach)]
        stride *= reach
        if stride >= n:
            got, after = lax.optimization_barrier((got, after))
        value = tree_sum([each.astype(F32) for each in [sent] + got])
    return value, after


def per_device(grad_out, queries, keys_in, values_in, filters, out_weight):
    n = lax.axis_size("ctx")
    nf = lax.axis_size("fsdp")
    r = n // nf
    tokens_here, channels = grad_out.shape
    group_count, taps = filters.shape
    per_group = channels // group_count
    groups = LANES // per_group
    octets = channels // LANES
    rows_here = out_weight.shape[0]
    parts = min(PARTS, octets)
    width = channels // parts
    per_part = octets // parts
    per_step = min(per_part, 4)
    steps = per_part // per_step

    kvp = (keys_in.astype(F32) * values_in.astype(F32)).astype(BF16)
    held = {"prior": block_before(kvp)}
    pieces = {}
    for e in reversed(range(r)):
        pieces[0, e] = first_piece(grad_out, rows_here, e)
        for q in range(1, nf):
            low = q & -q
            pieces[q, e] = swap(pieces[q ^ low, e], "fsdp", low)

    filters32 = filters.astype(F32)
    ext_rows = 3 * taps - ROWS
    lane_block = pl.BlockSpec((tokens_here, per_step * LANES), lambda o: (0, o))
    filter_block = pl.BlockSpec((per_step * groups, taps), lambda o: (o, 0))
    toe_block = pl.BlockSpec((per_step * groups * taps, 2 * taps), lambda o: (o, 0))
    ext_block = pl.BlockSpec((ext_rows, per_step * LANES), lambda o: (0, o))
    macs = channels * taps * tokens_here * groups
    params = pltpu.CompilerParams(vmem_limit_bytes=40 << 20)
    def block_sum(q, cols, earlier):
        weight = out_weight[:, cols]
        sums = {e: jnp.dot(pieces[q, e], weight, preferred_element_type=F32) for e in range(r)}
        bit = 1
        while bit < r:
            for e in [e for e in sums if e & bit]:
                got = swap(sums.pop(e).astype(BF16), "ctx", bit)
                if len(earlier) == KQ:
                    got, held["prior"] = lax.optimization_barrier((got, held["prior"]))
                if len(earlier) == ZQ:
                    got, earlier[0] = lax.optimization_barrier((got, earlier[0]))
                sums[e ^ bit] = sums[e ^ bit] + got.astype(F32)
            bit *= 2
        return to_owner(sums[0].astype(BF16), q)

    whole_blocks = []
    for q in range(nf - 1):
        whole_blocks.append(block_sum(q, slice(0, channels), whole_blocks))
    z_conv, toes, kvrev = pl.pallas_call(
        make_before_kernel(taps, per_group, per_step),
        grid=(octets // per_step,),
        in_specs=[filter_block, filter_block, lane_block, lane_block],
        out_specs=[lane_block, toe_block, ext_block],
        out_shape=[
            jax.ShapeDtypeStruct((tokens_here, channels), F32),
            jax.ShapeDtypeStruct((group_count * taps, 2 * taps), BF16),
            jax.ShapeDtypeStruct((ext_rows, channels), BF16),
        ],
        compiler_params=params,
        cost_estimate=pl.CostEstimate(flops=4 * macs, bytes_accessed=24 << 20, transcendentals=0),
        name="forward_conv",
    )(filters32, filters32[:, ::-1], kvp, held["prior"])

    grad_qs, terms = [], []
    grad_k = grad_v = None
    for part in range(parts):
        cols = slice(part * width, (part + 1) * width)
        owned = [block[:, cols] for block in whole_blocks] + [block_sum(nf - 1, cols, whole_blocks)]
        grad_y = sum(block.astype(F32) for block in owned).astype(BF16).astype(F32)
        grad_qs.append((grad_y * z_conv[:, cols]).astype(BF16))
        grad_z = (grad_y * queries[:, cols].astype(F32)).astype(BF16)
        later = from_behind(grad_z, "ctx", -1)

        base = part * steps
        part_lanes = pl.BlockSpec((tokens_here, per_step * LANES), lambda o, b=base: (0, o + b))
        part_toes = pl.BlockSpec((per_step * groups * taps, 2 * taps), lambda o, b=base: (o + b, 0))
        part_ext = pl.BlockSpec((ext_rows, per_step * LANES), lambda o, b=base: (0, o + b))
        local_terms = pl.pallas_call(
            make_pair_kernel(taps, per_group, per_step),
            grid=(steps,),
            in_specs=[lane_block, part_ext],
            out_specs=filter_block,
            out_shape=jax.ShapeDtypeStruct((group_count // parts, taps), F32),
            compiler_params=params,
            cost_estimate=pl.CostEstimate(
                flops=4 * macs // parts, bytes_accessed=(12 << 20) // parts, transcendentals=0
            ),
            name="pair_products",
        )(grad_z, kvrev)
        terms.append(local_terms)

        earlier = [] if part == 0 else [grad_k, grad_v]
        plane16 = jax.ShapeDtypeStruct((tokens_here, channels), BF16)
        grad_k, grad_v = pl.pallas_call(
            make_after_kernel(taps, per_group, per_step),
            grid=(steps,),
            in_specs=[lane_block, lane_block, part_toes, part_lanes, part_lanes]
            + [pl.BlockSpec(memory_space=pl.ANY)] * len(earlier),
            out_specs=[part_lanes, part_lanes],
            out_shape=[plane16, plane16],
            input_output_aliases={5 + at: at for at in range(len(earlier))},
            compiler_params=params,
            cost_estimate=pl.CostEstimate(
                flops=2 * macs // parts, bytes_accessed=(8 << 20) // parts, transcendentals=0
            ),
            name="backward_conv",
        )(grad_z, later, toes, keys_in, values_in, *earlier)

    grad_filters, (grad_k, grad_v) = summed_over_ctx(jnp.concatenate(terms, axis=0), (grad_k, grad_v))
    return (jnp.concatenate(grad_qs, axis=1), grad_k, grad_v, grad_filters)


def solution(mesh):
    placed = (
        P("ctx", "fsdp"),
        P("ctx", "fsdp"),
        P("ctx", "fsdp"),
        P("ctx", "fsdp"),
        P("fsdp", None),
        P("ctx", "fsdp"),
    )
    return jax.shard_map(
        per_device,
        mesh=mesh,
        in_specs=placed,
        out_specs=(P("ctx", "fsdp"), P("ctx", "fsdp"), P("ctx", "fsdp"), P("fsdp", None)),
        check_vma=False,
    )
```

time: 941 us -> 125 us (0.13)
  waiting for transfers between devices: 735 us -> 38.6 us
  local copies, waits for them, and re-layouts: 144 us -> 1.93 us
  starting transfers between devices: 6.37 us -> 57.8 us
  matrix products: 37.1 us -> 7.94 us
  between operations: 13.9 us -> 0.94 us
  Pallas kernels: 0 us -> 12.6 us
    all_gather x2 -> x0, waiting for transfers between devices: 665 us -> none  [the longest x1 639 us: per_device(): lax.all_gather(out_weight, 'ctx', axis=0, tiled=True)]
    reshape x5 -> x0, local copies, waits for them, and re-layouts: 77 us -> none  [the longest x2 59 us: toeplitz_rows(): return tiled[:, :tokens_here * span].reshape(group_count, tokens_here, span)]
    psum x1 -> x0, waiting for transfers between devices: 67.7 us -> none  [per_device(): grad_filters = lax.psum(local_terms, 'ctx')]
    ppermute x0 -> x23, starting transfers between devices: none -> 56.5 us  [the longest x16 36 us: swap(): return lax.ppermute(block, axis, [(i, i ^ mask) for i in range(size)])]
    ppermute x0 -> x23, waiting for transfers between devices: none -> 38.6 us  [the longest x16 22.8 us: swap(): return lax.ppermute(block, axis, [(i, i ^ mask) for i in range(size)])]
    unnamed x8, local copies, waits for them, and re-layouts: 35.3 us -> 0.02 us
    dot_general x4 -> x8, matrix products: 37.1 us -> 7.94 us  [block_sum(): jnp.dot(pieces[q, e], weight, preferred_element_type=F32)]
    slice x3 -> x0, local copies, waits for them, and re-layouts: 14.4 us -> none  [the longest x2 14.2 us: toeplitz_rows(): return tiled[:, :tokens_here * span].reshape(group_count, tokens_here, span)]
  transfers between devices with their start and end apart: 5 -> 24, of which waited for: 3 -> 9; matrix products, arithmetic and copies ran while one was open for 11% -> 10% of each run, Pallas kernels for 0% -> 10%
where the time goes in v2:
time: 125 us; the launch traced here: 124 us
  starting transfers between devices  57.8 us (46%)
  waiting for transfers between devices  38.6 us (31%)
  Pallas kernels  12.6 us (10%)
  matrix products  7.94 us (6%)
  other arithmetic  4.39 us (4%)
  local copies, waits for them, and re-layouts  1.93 us (2%)
    ppermute x16, starting transfers between devices, swap(): return lax.ppermute(block, axis, [(i, i ^ mask) for i in range(size)])  36 us
    ppermute x16, waiting for transfers between devices, swap(): return lax.ppermute(block, axis, [(i, i ^ mask) for i in range(size)])  22.8 us
    ppermute x4, waiting for transfers between devices, to_owner(): return lax.ppermute(block, ('ctx', 'fsdp'), route)  14.4 us
    ppermute x4, starting transfers between devices, to_owner(): return lax.ppermute(block, ('ctx', 'fsdp'), route)  10.9 us
    dot_general x8, matrix products, block_sum(): jnp.dot(pieces[q, e], weight, preferred_element_type=F32)  7.94 us
    ppermute x2, starting transfers between devices, first_piece(): return lax.ppermute(cut, ('ctx', 'fsdp'), route)  7.48 us
    pallas_call x1, Pallas kernels, per_device(): pl.pallas_call(make_before_kernel(taps, per_group, per_step), grid=(octet...  5.2 us
    pallas_call x1, Pallas kernels, per_device(): pl.pallas_call(make_after_kernel(taps, per_group, per_step), grid=(steps,...  3.78 us
  transfers between devices with their start and end apart: 24, of which 9 were waited for; matrix products, arithmetic and copies ran while one was open for 10% of the time, Pallas kernels for 10%

profile of v2, /device:TPU:0, one launch (start us, length us, event | category | flops | bytes accessed | tf_op | source)
XLA Modules:
  0.0 124.2 jit_solution(18080077956102020732)
XLA Ops:
  0.7 1.1 constant_dynamic-slice_fusion.1
  1.7 3.0 %collective-permute-start = (bf16[128,1024]{1,0:T(8,128)(2,1)S(1)}, bf16[128,1024]{1,0:T(8,128)(2,1)S(1)}, u32[]{:S(2)}, u32[]{:S(2)}) collective-permute-start(bf16[128,1024]{1,0:T(8,128)(2,1)S(1)} %get-tuple-element.26), channel_id=1, source_target_pairs={{4,0},{12,2},{20,1},{28,3},{0,4},{8,6},{16,5},{24,7},{13,8},{5,10}... | collective-permute-start | bytes 786440 | tf_op jit(solution)/shard_map/ppermute | solution.py:145
  4.8 2.9 %collective-permute-start.3 = (bf16[128,1024]{1,0:T(8,128)(2,1)S(1)}, bf16[128,1024]{1,0:T(8,128)(2,1)S(1)}, u32[]{:S(2)}, u32[]{:S(2)}) collective-permute-start(bf16[128,1024]{1,0:T(8,128)(2,1)S(1)} %get-tuple-element.27), channel_id=1, source_target_pairs={{0,2},{1,3},{2,0},{3,1},{4,6},{5,7},{6,4},{7,5},{8,10},{9,11},{10,... | collective-permute-start | bytes 786440 | tf_op jit(solution)/shard_map/ppermute | solution.py:28
  7.7 1.3 %multiply_convert_fusion.kvp_ref = bf16[128,2048]{1,0:T(8,128)(2,1)S(1)} fusion(bf16[128,2048]{1,0:T(8,128)(2,1)} %v_ref.1, bf16[128,2048]{1,0:T(8,128)(2,1)} %k_ref.1), kind=kLoop, calls=%fused_computation.16 | loop fusion | flops 1048576 | bytes 1572864 | tf_op jit(solution)/shard_map/convert_element_type | solution.py:205
  9.0 0.6 collective-permute-start.17
  9.6 0.8 rev.3.frev_ref
  10.4 0.9 convert_element_type.117.f_ref
  11.3 0.0 collective-permute-done
  11.3 4.6 %collective-permute-start.1 = (bf16[128,1024]{1,0:T(8,128)(2,1)S(1)}, bf16[128,1024]{1,0:T(8,128)(2,1)S(1)}, u32[]{:S(2)}, u32[]{:S(2)}) collective-permute-start(bf16[128,1024]{1,0:T(8,128)(2,1)S(1)} %collective-permute-done), channel_id=1, source_target_pairs={{0,2},{1,3},{2,0},{3,1},{4,6},{5,7},{6,4},{7,5},{8,10},{9,11},{10,... | collective-permute-start | bytes 786440 | tf_op jit(solution)/shard_map/ppermute | solution.py:28
  15.9 2.9 %convolution_convert_fusion.2 = bf16[128,2048]{1,0:T(8,128)(2,1)S(1)} fusion(bf16[128,1024]{1,0:T(8,128)(2,1)S(1)} %collective-permute-done, bf16[1024,2048]{1,0:T(8,128)(2,1)} %param.11), kind=kOutput, calls=%fused_computation.10 | convolution fusion | flops 537133056 | bytes 4980736 | tf_op jit(solution)/shard_map/dot_general | solution.py:224
  18.8 1.5 %collective-permute-start.5 = (bf16[128,2048]{1,0:T(8,128)(2,1)S(1)}, bf16[128,2048]{1,0:T(8,128)(2,1)S(1)}, u32[]{:S(2)}, u32[]{:S(2)}) collective-permute-start(bf16[128,2048]{1,0:T(8,128)(2,1)S(1)} %convolution_convert_fusion.2), channel_id=1, source_target_pairs={{0,4},{4,0},{8,12},{12,8},{16,20},{20,16},{24,28},{28,24},{1,5},{5... | collective-permute-start | bytes 1572872 | tf_op jit(solution)/shard_map/ppermute | solution.py:28
  20.4 2.6 %collective-permute-start.8 = (bf16[128,1024]{1,0:T(8,128)(2,1)S(1)}, bf16[128,1024]{1,0:T(8,128)(2,1)S(1)}, u32[]{:S(2)}, u32[]{:S(2)}) collective-permute-start(bf16[128,1024]{1,0:T(8,128)(2,1)S(1)} %collective-permute-done), channel_id=1, source_target_pairs={{0,1},{1,0},{2,3},{3,2},{4,5},{5,4},{6,7},{7,6},{8,9},{9,8},{10,11... | collective-permute-start | bytes 786440 | tf_op jit(solution)/shard_map/ppermute | solution.py:28
  22.9 0.0 collective-permute-done.3
  22.9 4.5 %collective-permute-start.4 = (bf16[128,1024]{1,0:T(8,128)(2,1)S(1)}, bf16[128,1024]{1,0:T(8,128)(2,1)S(1)}, u32[]{:S(2)}, u32[]{:S(2)}) collective-permute-start(bf16[128,1024]{1,0:T(8,128)(2,1)S(1)} %collective-permute-done.3), channel_id=1, source_target_pairs={{2,0},{10,2},{18,1},{26,3},{6,4},{14,6},{22,5},{30,7},{11,8},{3,10... | collective-permute-start | bytes 786440 | tf_op jit(solution)/shard_map/ppermute | solution.py:145
  27.4 0.0 collective-permute-done.1
  27.4 0.7 convolution_convert_fusion.3
  28.1 0.6 collective-permute-start.2
  28.7 0.7 convolution_convert_fusion.1
  29.4 1.6 %collective-permute-start.9 = (bf16[128,2048]{1,0:T(8,128)(2,1)S(1)}, bf16[128,2048]{1,0:T(8,128)(2,1)S(1)}, u32[]{:S(2)}, u32[]{:S(2)}) collective-permute-start(bf16[128,2048]{1,0:T(8,128)(2,1)S(1)} %convolution_convert_fusion.1), channel_id=1, source_target_pairs={{0,4},{4,0},{8,12},{12,8},{16,20},{20,16},{24,28},{28,24},{1,5},{5... | collective-permute-start | bytes 1572872 | tf_op jit(solution)/shard_map/ppermute | solution.py:28
  31.0 1.4 %collective-permute-done.4 = bf16[128,1024]{1,0:T(8,128)(2,1)S(1)} collective-permute-done((bf16[128,1024]{1,0:T(8,128)(2,1)S(1)}, bf16[128,1024]{1,0:T(8,128)(2,1)S(1)}, u32[]{:S(2)}, u32[]{:S(2)}) %collective-permute-start.4) | collective-permute-done | bytes 262176 | tf_op jit(solution)/shard_map/ppermute | solution.py:145
  32.4 7.5 %collective-permute-start.14 = (bf16[128,1024]{1,0:T(8,128)(2,1)S(1)}, bf16[128,1024]{1,0:T(8,128)(2,1)S(1)}, u32[]{:S(2)}, u32[]{:S(2)}) collective-permute-start(bf16[128,1024]{1,0:T(8,128)(2,1)S(1)} %collective-permute-done.1), channel_id=1, source_target_pairs={{0,1},{1,0},{2,3},{3,2},{4,5},{5,4},{6,7},{7,6},{8,9},{9,8},{10,11... | collective-permute-start | bytes 786440 | tf_op jit(solution)/shard_map/ppermute | solution.py:28
  39.9 0.0 collective-permute-done.5
  39.9 0.0 collective-permute-start.11
  39.9 0.7 fusion
  40.6 0.1 collective-permute-start.7
  40.7 0.3 collective-permute-done.14
  41.0 0.7 collective-permute-start.6
  41.7 0.7 convolution_convert_fusion
  42.5 5.6 %collective-permute-done.11 = bf16[128,1024]{1,0:T(8,128)(2,1)S(1)} collective-permute-done((bf16[128,1024]{1,0:T(8,128)(2,1)S(1)}, bf16[128,1024]{1,0:T(8,128)(2,1)S(1)}, u32[]{:S(2)}, u32[]{:S(2)}) %collective-permute-start.11) | collective-permute-done | bytes 262176 | tf_op jit(solution)/shard_map/ppermute | solution.py:28
  48.1 2.2 %collective-permute-start.18 = (bf16[128,2048]{1,0:T(8,128)(2,1)S(1)}, bf16[128,2048]{1,0:T(8,128)(2,1)S(1)}, u32[]{:S(2)}, u32[]{:S(2)}) collective-permute-start(bf16[128,2048]{1,0:T(8,128)(2,1)S(1)} %collective-permute-done.17), channel_id=1, source_target_pairs={{0,8},{8,16},{16,24},{1,9},{9,17},{17,25},{2,10},{10,18},{18,26},{... | collective-permute-start | bytes 1572872 | tf_op jit(solution)/shard_map/ppermute | solution.py:152
  50.3 0.1 collective-permute-start.15
  50.4 9.8 %collective-permute-done.9 = bf16[128,2048]{1,0:T(8,128)(2,1)S(1)} collective-permute-done((bf16[128,2048]{1,0:T(8,128)(2,1)S(1)}, bf16[128,2048]{1,0:T(8,128)(2,1)S(1)}, u32[]{:S(2)}, u32[]{:S(2)}) %collective-permute-start.9) | collective-permute-done | bytes 524320 | tf_op jit(solution)/shard_map/ppermute | solution.py:28
  60.2 0.0 collective-permute-start.13
  60.2 0.7 fusion.1
  60.9 0.0 collective-permute-done.2
  60.9 3.6 %collective-permute-start.10 = (bf16[128,2048]{1,0:T(8,128)(2,1)S(1)}, bf16[128,2048]{1,0:T(8,128)(2,1)S(1)}, u32[]{:S(2)}, u32[]{:S(2)}) collective-permute-start(bf16[128,2048]{1,0:T(8,128)(2,1)S(1)} %fusion.1), channel_id=1, source_target_pairs={{0,16},{1,1},{2,26},{3,11},{4,20},{5,5},{6,30},{7,15},{8,24},{9,9}... | collective-permute-start | bytes 1572872 | tf_op jit(solution)/shard_map/ppermute | solution.py:166
  64.5 0.0 collective-permute-done.6
  64.5 0.7 fusion.2
  65.2 0.0 copy-start.3
  65.2 3.0 %collective-permute-start.12 = (bf16[128,2048]{1,0:T(8,128)(2,1)S(1)}, bf16[128,2048]{1,0:T(8,128)(2,1)S(1)}, u32[]{:S(2)}, u32[]{:S(2)}) collective-permute-start(bf16[128,2048]{1,0:T(8,128)(2,1)S(1)} %fusion.2), channel_id=1, source_target_pairs={{0,8},{1,25},{2,2},{3,19},{4,12},{5,29},{6,6},{7,23},{8,0},{9,17},... | collective-permute-start | bytes 1572872 | tf_op jit(solution)/shard_map/ppermute | solution.py:166
  68.2 0.0 collective-permute-done.13
  68.2 3.1 %collective-permute-done.15 = bf16[128,2048]{1,0:T(8,128)(2,1)S(1)} collective-permute-done((bf16[128,2048]{1,0:T(8,128)(2,1)S(1)}, bf16[128,2048]{1,0:T(8,128)(2,1)S(1)}, u32[]{:S(2)}, u32[]{:S(2)}) %collective-permute-start.15) | collective-permute-done | bytes 524320 | tf_op jit(solution)/shard_map/ppermute | solution.py:28
  71.3 0.7 fusion.3
  72.0 3.7 %collective-permute-start.16 = (bf16[128,2048]{1,0:T(8,128)(2,1)S(1)}, bf16[128,2048]{1,0:T(8,128)(2,1)S(1)}, u32[]{:S(2)}, u32[]{:S(2)}) collective-permute-start(bf16[128,2048]{1,0:T(8,128)(2,1)S(1)} %fusion.3), channel_id=1, source_target_pairs={{0,24},{1,9},{2,18},{3,3},{4,28},{5,13},{6,22},{7,7},{8,16},{9,1},... | collective-permute-start | bytes 1572872 | tf_op jit(solution)/shard_map/ppermute | solution.py:166
  75.8 0.1 broadcast_select_fusion.prior_ref
  75.8 5.2 %forward_conv.1 = (f32[128,2048]{1,0:T(8,128)S(1)}, bf16[16384,256]{1,0:T(8,128)(2,1)S(1)}, bf16[352,2048]{1,0:T(8,128)(2,1)S(1)}) custom-call(f32[128,128]{1,0:T(8,128)S(1)} %convert_element_type.117.f_ref, f32[128,128]{1,0:T(8,128)S(1)} %rev.3.frev_ref, bf16[128,2048]{1,0:T(8,128)(2,1)S(1)} %multiply_convert_fusion.kvp_ref, ...), custom_call_target="tpu_custom_call" | custom-call | flops 1073741824 | bytes 25165824 | tf_op jit(solution)/shard_map/forward_conv/pallas_call | solution.py:240
  81.0 0.0 copy-start
  81.0 0.0 copy-start.1
  81.1 10.6 %collective-permute-done.10 = bf16[128,2048]{1,0:T(8,128)(2,1)S(1)} collective-permute-done((bf16[128,2048]{1,0:T(8,128)(2,1)S(1)}, bf16[128,2048]{1,0:T(8,128)(2,1)S(1)}, u32[]{:S(2)}, u32[]{:S(2)}) %collective-permute-start.10) | collective-permute-done | bytes 524320 | tf_op jit(solution)/shard_map/ppermute | solution.py:166
  91.6 0.0 collective-permute-done.12
  91.6 3.8 %collective-permute-done.16 = bf16[128,2048]{1,0:T(8,128)(2,1)S(1)} collective-permute-done((bf16[128,2048]{1,0:T(8,128)(2,1)S(1)}, bf16[128,2048]{1,0:T(8,128)(2,1)S(1)}, u32[]{:S(2)}, u32[]{:S(2)}) %collective-permute-start.16) | collective-permute-done | bytes 524320 | tf_op jit(solution)/shard_map/ppermute | solution.py:166
  95.5 0.5 fusion.5
  96.0 1.3 %collective-permute-start.23 = (bf16[128,2048]{1,0:T(8,128)(2,1)S(1)}, bf16[128,2048]{1,0:T(8,128)(2,1)S(1)}, u32[]{:S(2)}, u32[]{:S(2)}) collective-permute-start(bf16[128,2048]{1,0:T(8,128)(2,1)S(1)} %get-tuple-element.24.gz_ref), channel_id=1, source_target_pairs={{4,0},{8,4},{12,8},{16,12},{20,16},{24,20},{28,24},{5,1},{9,5},{13... | collective-permute-start | bytes 1572872 | tf_op jit(solution)/shard_map/ppermute | solution.py:34
  97.3 3.6 %pair_products.1 = f32[128,128]{1,0:T(8,128)S(1)} custom-call(bf16[128,2048]{1,0:T(8,128)(2,1)S(1)} %get-tuple-element.24.gz_ref, bf16[352,2048]{1,0:T(8,128)(2,1)S(1)} %get-tuple-element.17.kvrev_ref), custom_call_target="tpu_custom_call" | custom-call | flops 1073741824 | bytes 12582912 | tf_op jit(solution)/shard_map/pair_products/pallas_call | solution.py:269
  100.9 8.2 %collective-permute-start.20 = (bf16[128,128]{1,0:T(8,128)(2,1)S(1)}, bf16[128,128]{1,0:T(8,128)(2,1)S(1)}, u32[]{:S(2)}, u32[]{:S(2)}) collective-permute-start(bf16[128,128]{1,0:T(8,128)(2,1)S(1)} %convert_element_type.124), channel_id=1, source_target_pairs={{0,8},{4,12},{8,0},{12,4},{16,24},{20,28},{24,16},{28,20},{1,9},{5... | collective-permute-start | bytes 98312 | tf_op jit(solution)/shard_map/ppermute | solution.py:28
  109.1 2.0 %collective-permute-start.19 = (bf16[128,128]{1,0:T(8,128)(2,1)S(1)}, bf16[128,128]{1,0:T(8,128)(2,1)S(1)}, u32[]{:S(2)}, u32[]{:S(2)}) collective-permute-start(bf16[128,128]{1,0:T(8,128)(2,1)S(1)} %convert_element_type.124), channel_id=1, source_target_pairs={{0,4},{4,0},{8,12},{12,8},{16,20},{20,16},{24,28},{28,24},{1,5},{5... | collective-permute-start | bytes 98312 | tf_op jit(solution)/shard_map/ppermute | solution.py:28
  111.1 0.9 fusion.4
  112.0 3.7 %collective-permute-done.20 = bf16[128,128]{1,0:T(8,128)(2,1)S(1)} collective-permute-done((bf16[128,128]{1,0:T(8,128)(2,1)S(1)}, bf16[128,128]{1,0:T(8,128)(2,1)S(1)}, u32[]{:S(2)}, u32[]{:S(2)}) %collective-permute-start.20) | collective-permute-done | bytes 32800 | tf_op jit(solution)/shard_map/ppermute | solution.py:28
  115.7 0.0 collective-permute-done.19
  115.7 0.2 collective-permute-done.21
  115.9 3.9 %collective-permute-start.22 = (bf16[128,128]{1,0:T(8,128)(2,1)S(1)}, bf16[128,128]{1,0:T(8,128)(2,1)S(1)}, u32[]{:S(2)}, u32[]{:S(2)}) collective-permute-start(bf16[128,128]{1,0:T(8,128)(2,1)S(1)} %add_convert_fusion.1), channel_id=1, source_target_pairs={{0,16},{4,20},{8,24},{12,28},{16,0},{20,4},{24,8},{28,12},{1,17},{... | collective-permute-start | bytes 98312 | tf_op jit(solution)/shard_map/ppermute | solution.py:28
  119.8 3.8 %backward_conv.1 = (bf16[128,2048]{1,0:T(8,128)(2,1)}, bf16[128,2048]{1,0:T(8,128)(2,1)}) custom-call(bf16[128,2048]{1,0:T(8,128)(2,1)S(1)} %get-tuple-element.24.gz_ref, bf16[128,2048]{1,0:T(8,128)(2,1)S(1)} %collective-permute-done.23.later_ref, bf16[16384,256]{1,0:T(8,128)(2,1)S(1)} %get-tuple-element.18.toe_ref, bf16[128,2048]{1,0:T(8,128)(2,1)S(1)} %copy-done.1, ...), custom_call_target="tpu_custom_call" | custom-call | flops 536870912 | bytes 8388608 | tf_op jit(solution)/shard_map/backward_conv/pallas_call | solution.py:285
  123.6 0.0 collective-permute-done.22
  123.6 0.6 convert_add_fusion
  (13 shorter events, 0.1 us)
Async XLA Ops:
  1.7 9.6 %collective-permute-start = (bf16[128,1024]{1,0:T(8,128)(2,1)S(1)}, bf16[128,1024]{1,0:T(8,128)(2,1)S(1)}, u32[]{:S(2)}, u32[]{:S(2)}) collective-permute-start(bf16[128,1024]{1,0:T(8,128)(2,1)S(1)} %get-tuple-element.26), channel_id=1, source_target_pairs={{4,0},{12,2},{20,1},{28,3},{0,4},{8,6},{16,5},{24,7},{13,8},{5,10}... | collective-permute-start | bytes 786440 | tf_op jit(solution)/shard_map/ppermute | solution.py:145
  4.8 18.2 %collective-permute-start.3 = (bf16[128,1024]{1,0:T(8,128)(2,1)S(1)}, bf16[128,1024]{1,0:T(8,128)(2,1)S(1)}, u32[]{:S(2)}, u32[]{:S(2)}) collective-permute-start(bf16[128,1024]{1,0:T(8,128)(2,1)S(1)} %get-tuple-element.27), channel_id=1, source_target_pairs={{0,2},{1,3},{2,0},{3,1},{4,6},{5,7},{6,4},{7,5},{8,10},{9,11},{10,... | collective-permute-start | bytes 786440 | tf_op jit(solution)/shard_map/ppermute | solution.py:28
  9.0 31.6 %collective-permute-start.17 = (bf16[128,2048]{1,0:T(8,128)(2,1)S(1)}, bf16[128,2048]{1,0:T(8,128)(2,1)S(1)}, u32[]{:S(2)}, u32[]{:S(2)}) collective-permute-start(bf16[128,2048]{1,0:T(8,128)(2,1)S(1)} %multiply_convert_fusion.kvp_ref), channel_id=1, source_target_pairs={{0,4},{4,0},{8,12},{12,8},{16,20},{20,16},{24,28},{28,24},{1,5},{5... | collective-permute-start | bytes 1572872 | tf_op jit(solution)/shard_map/ppermute | solution.py:28
  10.4 17.0 %copy-start.2 = (bf16[1024,2048]{1,0:T(8,128)(2,1)S(1)}, bf16[1024,2048]{1,0:T(8,128)(2,1)}, u32[]{:S(2)}) copy-start(bf16[1024,2048]{1,0:T(8,128)(2,1)} %param.11) | copy-start | bytes 12582916
  11.3 16.1 %collective-permute-start.1 = (bf16[128,1024]{1,0:T(8,128)(2,1)S(1)}, bf16[128,1024]{1,0:T(8,128)(2,1)S(1)}, u32[]{:S(2)}, u32[]{:S(2)}) collective-permute-start(bf16[128,1024]{1,0:T(8,128)(2,1)S(1)} %collective-permute-done), channel_id=1, source_target_pairs={{0,2},{1,3},{2,0},{3,1},{4,6},{5,7},{6,4},{7,5},{8,10},{9,11},{10,... | collective-permute-start | bytes 786440 | tf_op jit(solution)/shard_map/ppermute | solution.py:28
  18.8 21.1 %collective-permute-start.5 = (bf16[128,2048]{1,0:T(8,128)(2,1)S(1)}, bf16[128,2048]{1,0:T(8,128)(2,1)S(1)}, u32[]{:S(2)}, u32[]{:S(2)}) collective-permute-start(bf16[128,2048]{1,0:T(8,128)(2,1)S(1)} %convolution_convert_fusion.2), channel_id=1, source_target_pairs={{0,4},{4,0},{8,12},{12,8},{16,20},{20,16},{24,28},{28,24},{1,5},{5... | collective-permute-start | bytes 1572872 | tf_op jit(solution)/shard_map/ppermute | solution.py:28
  20.4 8.4 %collective-permute-start.8 = (bf16[128,1024]{1,0:T(8,128)(2,1)S(1)}, bf16[128,1024]{1,0:T(8,128)(2,1)S(1)}, u32[]{:S(2)}, u32[]{:S(2)}) collective-permute-start(bf16[128,1024]{1,0:T(8,128)(2,1)S(1)} %collective-permute-done), channel_id=1, source_target_pairs={{0,1},{1,0},{2,3},{3,2},{4,5},{5,4},{6,7},{7,6},{8,9},{9,8},{10,11... | collective-permute-start | bytes 786440 | tf_op jit(solution)/shard_map/ppermute | solution.py:28
  22.9 9.5 %collective-permute-start.4 = (bf16[128,1024]{1,0:T(8,128)(2,1)S(1)}, bf16[128,1024]{1,0:T(8,128)(2,1)S(1)}, u32[]{:S(2)}, u32[]{:S(2)}) collective-permute-start(bf16[128,1024]{1,0:T(8,128)(2,1)S(1)} %collective-permute-done.3), channel_id=1, source_target_pairs={{2,0},{10,2},{18,1},{26,3},{6,4},{14,6},{22,5},{30,7},{11,8},{3,10... | collective-permute-start | bytes 786440 | tf_op jit(solution)/shard_map/ppermute | solution.py:145
  28.1 32.8 %collective-permute-start.2 = (bf16[128,2048]{1,0:T(8,128)(2,1)S(1)}, bf16[128,2048]{1,0:T(8,128)(2,1)S(1)}, u32[]{:S(2)}, u32[]{:S(2)}) collective-permute-start(bf16[128,2048]{1,0:T(8,128)(2,1)S(1)} %convolution_convert_fusion.3), channel_id=1, source_target_pairs={{0,4},{4,0},{8,12},{12,8},{16,20},{20,16},{24,28},{28,24},{1,5},{5... | collective-permute-start | bytes 1572872 | tf_op jit(solution)/shard_map/ppermute | solution.py:28
  29.4 30.7 %collective-permute-start.9 = (bf16[128,2048]{1,0:T(8,128)(2,1)S(1)}, bf16[128,2048]{1,0:T(8,128)(2,1)S(1)}, u32[]{:S(2)}, u32[]{:S(2)}) collective-permute-start(bf16[128,2048]{1,0:T(8,128)(2,1)S(1)} %convolution_convert_fusion.1), channel_id=1, source_target_pairs={{0,4},{4,0},{8,12},{12,8},{16,20},{20,16},{24,28},{28,24},{1,5},{5... | collective-permute-start | bytes 1572872 | tf_op jit(solution)/shard_map/ppermute | solution.py:28
  32.4 8.6 %collective-permute-start.14 = (bf16[128,1024]{1,0:T(8,128)(2,1)S(1)}, bf16[128,1024]{1,0:T(8,128)(2,1)S(1)}, u32[]{:S(2)}, u32[]{:S(2)}) collective-permute-start(bf16[128,1024]{1,0:T(8,128)(2,1)S(1)} %collective-permute-done.1), channel_id=1, source_target_pairs={{0,1},{1,0},{2,3},{3,2},{4,5},{5,4},{6,7},{7,6},{8,9},{9,8},{10,11... | collective-permute-start | bytes 786440 | tf_op jit(solution)/shard_map/ppermute | solution.py:28
  39.9 8.2 %collective-permute-start.11 = (bf16[128,1024]{1,0:T(8,128)(2,1)S(1)}, bf16[128,1024]{1,0:T(8,128)(2,1)S(1)}, u32[]{:S(2)}, u32[]{:S(2)}) collective-permute-start(bf16[128,1024]{1,0:T(8,128)(2,1)S(1)} %collective-permute-done.4), channel_id=1, source_target_pairs={{0,2},{1,3},{2,0},{3,1},{4,6},{5,7},{6,4},{7,5},{8,10},{9,11},{10,... | collective-permute-start | bytes 786440 | tf_op jit(solution)/shard_map/ppermute | solution.py:28
  40.6 9.7 %collective-permute-start.7 = (bf16[128,1024]{1,0:T(8,128)(2,1)S(1)}, bf16[128,1024]{1,0:T(8,128)(2,1)S(1)}, u32[]{:S(2)}, u32[]{:S(2)}) collective-permute-start(bf16[128,1024]{1,0:T(8,128)(2,1)S(1)} %collective-permute-done.4), channel_id=1, source_target_pairs={{0,1},{1,0},{2,3},{3,2},{4,5},{5,4},{6,7},{7,6},{8,9},{9,8},{10,11... | collective-permute-start | bytes 786440 | tf_op jit(solution)/shard_map/ppermute | solution.py:28
  41.0 23.4 %collective-permute-start.6 = (bf16[128,2048]{1,0:T(8,128)(2,1)S(1)}, bf16[128,2048]{1,0:T(8,128)(2,1)S(1)}, u32[]{:S(2)}, u32[]{:S(2)}) collective-permute-start(bf16[128,2048]{1,0:T(8,128)(2,1)S(1)} %fusion), channel_id=1, source_target_pairs={{0,0},{1,17},{2,10},{3,27},{4,4},{5,21},{6,14},{7,31},{8,8},{9,25}... | collective-permute-start | bytes 1572872 | tf_op jit(solution)/shard_map/ppermute | solution.py:166
  48.1 27.6 %collective-permute-start.18 = (bf16[128,2048]{1,0:T(8,128)(2,1)S(1)}, bf16[128,2048]{1,0:T(8,128)(2,1)S(1)}, u32[]{:S(2)}, u32[]{:S(2)}) collective-permute-start(bf16[128,2048]{1,0:T(8,128)(2,1)S(1)} %collective-permute-done.17), channel_id=1, source_target_pairs={{0,8},{8,16},{16,24},{1,9},{9,17},{17,25},{2,10},{10,18},{18,26},{... | collective-permute-start | bytes 1572872 | tf_op jit(solution)/shard_map/ppermute | solution.py:152
  50.3 21.0 %collective-permute-start.15 = (bf16[128,2048]{1,0:T(8,128)(2,1)S(1)}, bf16[128,2048]{1,0:T(8,128)(2,1)S(1)}, u32[]{:S(2)}, u32[]{:S(2)}) collective-permute-start(bf16[128,2048]{1,0:T(8,128)(2,1)S(1)} %convolution_convert_fusion), channel_id=1, source_target_pairs={{0,4},{4,0},{8,12},{12,8},{16,20},{20,16},{24,28},{28,24},{1,5},{5... | collective-permute-start | bytes 1572872 | tf_op jit(solution)/shard_map/ppermute | solution.py:28
  60.2 8.0 %collective-permute-start.13 = (bf16[128,1024]{1,0:T(8,128)(2,1)S(1)}, bf16[128,1024]{1,0:T(8,128)(2,1)S(1)}, u32[]{:S(2)}, u32[]{:S(2)}) collective-permute-start(bf16[128,1024]{1,0:T(8,128)(2,1)S(1)} %collective-permute-done.11), channel_id=1, source_target_pairs={{0,1},{1,0},{2,3},{3,2},{4,5},{5,4},{6,7},{7,6},{8,9},{9,8},{10,11... | collective-permute-start | bytes 786440 | tf_op jit(solution)/shard_map/ppermute | solution.py:28
  60.9 30.7 %collective-permute-start.10 = (bf16[128,2048]{1,0:T(8,128)(2,1)S(1)}, bf16[128,2048]{1,0:T(8,128)(2,1)S(1)}, u32[]{:S(2)}, u32[]{:S(2)}) collective-permute-start(bf16[128,2048]{1,0:T(8,128)(2,1)S(1)} %fusion.1), channel_id=1, source_target_pairs={{0,16},{1,1},{2,26},{3,11},{4,20},{5,5},{6,30},{7,15},{8,24},{9,9}... | collective-permute-start | bytes 1572872 | tf_op jit(solution)/shard_map/ppermute | solution.py:166
  65.2 30.2 %copy-start.3 = (bf16[128,2048]{1,0:T(8,128)(2,1)S(1)}, bf16[128,2048]{1,0:T(8,128)(2,1)}, u32[]{:S(2)}) copy-start(bf16[128,2048]{1,0:T(8,128)(2,1)} %param.7) | copy-start | bytes 1572868
  65.2 26.4 %collective-permute-start.12 = (bf16[128,2048]{1,0:T(8,128)(2,1)S(1)}, bf16[128,2048]{1,0:T(8,128)(2,1)S(1)}, u32[]{:S(2)}, u32[]{:S(2)}) collective-permute-start(bf16[128,2048]{1,0:T(8,128)(2,1)S(1)} %fusion.2), channel_id=1, source_target_pairs={{0,8},{1,25},{2,2},{3,19},{4,12},{5,29},{6,6},{7,23},{8,0},{9,17},... | collective-permute-start | bytes 1572872 | tf_op jit(solution)/shard_map/ppermute | solution.py:166
  72.0 23.4 %collective-permute-start.16 = (bf16[128,2048]{1,0:T(8,128)(2,1)S(1)}, bf16[128,2048]{1,0:T(8,128)(2,1)S(1)}, u32[]{:S(2)}, u32[]{:S(2)}) collective-permute-start(bf16[128,2048]{1,0:T(8,128)(2,1)S(1)} %fusion.3), channel_id=1, source_target_pairs={{0,24},{1,9},{2,18},{3,3},{4,28},{5,13},{6,22},{7,7},{8,16},{9,1},... | collective-permute-start | bytes 1572872 | tf_op jit(solution)/shard_map/ppermute | solution.py:166
  81.0 38.7 %copy-start = (bf16[128,2048]{1,0:T(8,128)(2,1)S(1)}, bf16[128,2048]{1,0:T(8,128)(2,1)}, u32[]{:S(2)}) copy-start(bf16[128,2048]{1,0:T(8,128)(2,1)} %v_ref.1) | copy-start | bytes 1572868
  81.0 38.7 %copy-start.1 = (bf16[128,2048]{1,0:T(8,128)(2,1)S(1)}, bf16[128,2048]{1,0:T(8,128)(2,1)}, u32[]{:S(2)}) copy-start(bf16[128,2048]{1,0:T(8,128)(2,1)} %k_ref.1) | copy-start | bytes 1572868
  96.0 23.8 %collective-permute-start.23 = (bf16[128,2048]{1,0:T(8,128)(2,1)S(1)}, bf16[128,2048]{1,0:T(8,128)(2,1)S(1)}, u32[]{:S(2)}, u32[]{:S(2)}) collective-permute-start(bf16[128,2048]{1,0:T(8,128)(2,1)S(1)} %get-tuple-element.24.gz_ref), channel_id=1, source_target_pairs={{4,0},{8,4},{12,8},{16,12},{20,16},{24,20},{28,24},{5,1},{9,5},{13... | collective-permute-start | bytes 1572872 | tf_op jit(solution)/shard_map/ppermute | solution.py:34
  100.9 14.8 %collective-permute-start.20 = (bf16[128,128]{1,0:T(8,128)(2,1)S(1)}, bf16[128,128]{1,0:T(8,128)(2,1)S(1)}, u32[]{:S(2)}, u32[]{:S(2)}) collective-permute-start(bf16[128,128]{1,0:T(8,128)(2,1)S(1)} %convert_element_type.124), channel_id=1, source_target_pairs={{0,8},{4,12},{8,0},{12,4},{16,24},{20,28},{24,16},{28,20},{1,9},{5... | collective-permute-start | bytes 98312 | tf_op jit(solution)/shard_map/ppermute | solution.py:28
  109.1 6.7 %collective-permute-start.19 = (bf16[128,128]{1,0:T(8,128)(2,1)S(1)}, bf16[128,128]{1,0:T(8,128)(2,1)S(1)}, u32[]{:S(2)}, u32[]{:S(2)}) collective-permute-start(bf16[128,128]{1,0:T(8,128)(2,1)S(1)} %convert_element_type.124), channel_id=1, source_target_pairs={{0,4},{4,0},{8,12},{12,8},{16,20},{20,16},{24,28},{28,24},{1,5},{5... | collective-permute-start | bytes 98312 | tf_op jit(solution)/shard_map/ppermute | solution.py:28
  111.1 4.8 %collective-permute-start.21 = (bf16[128,128]{1,0:T(8,128)(2,1)S(1)}, bf16[128,128]{1,0:T(8,128)(2,1)S(1)}, u32[]{:S(2)}, u32[]{:S(2)}) collective-permute-start(bf16[128,128]{1,0:T(8,128)(2,1)S(1)} %convert_element_type.124), channel_id=1, source_target_pairs={{0,12},{4,8},{8,4},{12,0},{16,28},{20,24},{24,20},{28,16},{1,13},{... | collective-permute-start | bytes 98312 | tf_op jit(solution)/shard_map/ppermute | solution.py:28
  115.9 7.7 %collective-permute-start.22 = (bf16[128,128]{1,0:T(8,128)(2,1)S(1)}, bf16[128,128]{1,0:T(8,128)(2,1)S(1)}, u32[]{:S(2)}, u32[]{:S(2)}) collective-permute-start(bf16[128,128]{1,0:T(8,128)(2,1)S(1)} %add_convert_fusion.1), channel_id=1, source_target_pairs={{0,16},{4,20},{8,24},{12,28},{16,0},{20,4},{24,8},{28,12},{1,17},{... | collective-permute-start | bytes 98312 | tf_op jit(solution)/shard_map/ppermute | solution.py:28

commit v3 on v2

--- a/solution.py
+++ b/solution.py
@@ -9,10 +9,11 @@
 BF16 = jnp.bfloat16
 LANES = 128
 PARTS = 1
-KQ = 9
+FLIGHT = 2
+KQ = 1
+CUTX = False
 ZQ = 2
 DET = True
-DIRECT = 3
 ROWS = 32
 
 
@@ -52,6 +53,10 @@
     for g in range(1, groups):
         out = jnp.where(lane == g, stacked[g * taps : (g + 1) * taps], out)
     return out
+
+
+def product_kernel(k_ref, v_ref, kvp_ref):
+    kvp_ref[...] = (k_ref[...].astype(F32) * v_ref[...].astype(F32)).astype(BF16)
 
 
 def make_before_kernel(taps, per_group, octets):
@@ -142,15 +147,7 @@
     cut = lax.dynamic_slice_in_dim(grad_out, part * rows_here, rows_here, axis=1)
     if detour:
         cut = swap(cut, "fsdp", detour)
-    return lax.ppermute(cut, ("ctx", "fsdp"), route)
-
-
-def block_before(kvp):
-    n = lax.axis_size("ctx")
-    mine = lax.axis_index("ctx")
-    near = swap(kvp, "ctx", 1)
-    far = lax.ppermute(near, "ctx", [(i, i + 2) for i in range(0, n - 2, 2)])
-    return jnp.where(mine % 2 == 1, near, far)
+    return cut, lax.ppermute(cut, ("ctx", "fsdp"), route)
 
 
 def to_owner(block, q):
@@ -172,15 +169,20 @@
     return values[0]
 
 
-def summed_over_ctx(value, after):
+def summed_over_ctx(value, halo, after):
     n = lax.axis_size("ctx")
-    stride = 1
-    while stride < n:
-        reach = min(DIRECT + 1, n // stride)
+    steps = []
+    at = 2
+    while at < n:
+        steps.append([k * at for k in (1, 2, 3) if k * at < n])
+        at *= 4
+    steps.append([1])
+    for step in steps:
         sent = value.astype(BF16)
-        got = [swap(sent, "ctx", k * stride) for k in range(1, reach)]
-        stride *= reach
-        if stride >= n:
+        if step == [1]:
+            sent, halo = lax.optimization_barrier((sent, halo))
+        got = [swap(sent, "ctx", mask) for mask in step]
+        if step == [1]:
             got, after = lax.optimization_barrier((got, after))
         value = tree_sum([each.astype(F32) for each in [sent] + got])
     return value, after
@@ -199,17 +201,28 @@
     parts = min(PARTS, octets)
     width = channels // parts
     per_part = octets // parts
-    per_step = min(per_part, 4)
+    per_step = min(per_part, 8)
     steps = per_part // per_step
 
-    kvp = (keys_in.astype(F32) * values_in.astype(F32)).astype(BF16)
-    held = {"prior": block_before(kvp)}
+    kvp = pl.pallas_call(
+        product_kernel,
+        out_shape=jax.ShapeDtypeStruct((tokens_here, channels), BF16),
+        cost_estimate=pl.CostEstimate(flops=1 << 20, bytes_accessed=64 << 20, transcendentals=0),
+        name="kv_product",
+    )(keys_in, values_in)
+    arrived = []
+    held = {"prior": from_behind(kvp, "ctx", 1)}
     pieces = {}
-    for e in reversed(range(r)):
-        pieces[0, e] = first_piece(grad_out, rows_here, e)
+    cuts = {}
+    for e in range(r):
+        cuts[e], pieces[0, e] = first_piece(grad_out, rows_here, e)
+    for e in range(r):
         for q in range(1, nf):
             low = q & -q
-            pieces[q, e] = swap(pieces[q ^ low, e], "fsdp", low)
+            piece = pieces[q ^ low, e]
+            if CUTX and r > 1 and e == r - 1 and q == nf // 2:
+                piece, cuts[0] = lax.optimization_barrier((piece, cuts[0]))
+            pieces[q, e] = swap(piece, "fsdp", low)
 
     filters32 = filters.astype(F32)
     ext_rows = 3 * taps - ROWS
@@ -225,9 +238,13 @@
         bit = 1
         while bit < r:
             for e in [e for e in sums if e & bit]:
-                got = swap(sums.pop(e).astype(BF16), "ctx", bit)
+                sent = sums.pop(e).astype(BF16)
+                if len(arrived) >= FLIGHT:
+                    sent, arrived[-FLIGHT] = lax.optimization_barrier((sent, arrived[-FLIGHT]))
+                got = swap(sent, "ctx", bit)
                 if len(earlier) == KQ:
                     got, held["prior"] = lax.optimization_barrier((got, held["prior"]))
+                arrived.append(got)
                 if len(earlier) == ZQ:
                     got, earlier[0] = lax.optimization_barrier((got, earlier[0]))
                 sums[e ^ bit] = sums[e ^ bit] + got.astype(F32)
@@ -237,6 +254,12 @@
     whole_blocks = []
     for q in range(nf - 1):
         whole_blocks.append(block_sum(q, slice(0, channels), whole_blocks))
+    last_blocks = []
+    for part in range(parts):
+        cols = slice(part * width, (part + 1) * width)
+        last_blocks.append(block_sum(nf - 1, cols, whole_blocks))
+    prior = held["prior"]
+
     z_conv, toes, kvrev = pl.pallas_call(
         make_before_kernel(taps, per_group, per_step),
         grid=(octets // per_step,),
@@ -250,13 +273,13 @@
         compiler_params=params,
         cost_estimate=pl.CostEstimate(flops=4 * macs, bytes_accessed=24 << 20, transcendentals=0),
         name="forward_conv",
-    )(filters32, filters32[:, ::-1], kvp, held["prior"])
+    )(filters32, filters32[:, ::-1], kvp, prior)
 
     grad_qs, terms = [], []
     grad_k = grad_v = None
     for part in range(parts):
         cols = slice(part * width, (part + 1) * width)
-        owned = [block[:, cols] for block in whole_blocks] + [block_sum(nf - 1, cols, whole_blocks)]
+        owned = [block[:, cols] for block in whole_blocks] + [last_blocks[part]]
         grad_y = sum(block.astype(F32) for block in owned).astype(BF16).astype(F32)
         grad_qs.append((grad_y * z_conv[:, cols]).astype(BF16))
         grad_z = (grad_y * queries[:, cols].astype(F32)).astype(BF16)
@@ -297,7 +320,7 @@
             name="backward_conv",
         )(grad_z, later, toes, keys_in, values_in, *earlier)
 
-    grad_filters, (grad_k, grad_v) = summed_over_ctx(jnp.concatenate(terms, axis=0), (grad_k, grad_v))
+    grad_filters, (grad_k, grad_v) = summed_over_ctx(jnp.concatenate(terms, axis=0), later, (grad_k, grad_v))
     return (jnp.concatenate(grad_qs, axis=1), grad_k, grad_v, grad_filters)
 
 

time: 125 us -> 120 us (0.960)
  waiting for transfers between devices: 38.6 us -> 34.8 us
  starting transfers between devices: 57.8 us -> 55.2 us
  matrix products: 7.94 us -> 10.4 us
  other arithmetic: 4.39 us -> 3.06 us
    ppermute x4, waiting for transfers between devices: 14.4 us -> 7.83 us  [to_owner(): return lax.ppermute(block, ('ctx', 'fsdp'), route)]
    ppermute x16 -> x15, starting transfers between devices: 36 us -> 31.1 us  [swap(): return lax.ppermute(block, axis, [(i, i ^ mask) for i in range(size)])]
    ppermute x3 -> x2, waiting for transfers between devices: 1.39 us -> 5.85 us  [first_piece(): return (cut, lax.ppermute(cut, ('ctx', 'fsdp'), route))]
    ppermute x1 -> x2, starting transfers between devices: 1.29 us -> 4.17 us  [from_behind(): return lax.ppermute(block, axis, route)]
    dot_general x8, matrix products: 7.94 us -> 10.4 us  [block_sum(): jnp.dot(pieces[q, e], weight, preferred_element_type=F32)]
    ppermute x3 -> x2, starting transfers between devices: 9.64 us -> 7.2 us  [first_piece(): return (cut, lax.ppermute(cut, ('ctx', 'fsdp'), route))]
    pallas_call x0 -> x1, Pallas kernels: none -> 2.11 us  [per_device(): pl.pallas_call(product_kernel, out_shape=jax.ShapeDtypeStruct((tokens_her...]
    ppermute x4, starting transfers between devices: 10.9 us -> 12.8 us  [to_owner(): return lax.ppermute(block, ('ctx', 'fsdp'), route)]
  transfers between devices with their start and end apart: 24 -> 23, of which waited for: 9 -> 10; matrix products, arithmetic and copies ran while one was open for 10% -> 10% of each run, Pallas kernels for 10% -> 11%
where the time goes in v3:
time: 120 us; the launch traced here: 119 us
  starting transfers between devices  55.2 us (46%)
  waiting for transfers between devices  34.8 us (29%)
  Pallas kernels  13.2 us (11%)
  matrix products  10.4 us (9%)
  other arithmetic  3.06 us (3%)
    ppermute x15, starting transfers between devices, swap(): return lax.ppermute(block, axis, [(i, i ^ mask) for i in range(size)])  31.1 us
    ppermute x15, waiting for transfers between devices, swap(): return lax.ppermute(block, axis, [(i, i ^ mask) for i in range(size)])  21.1 us
    ppermute x4, starting transfers between devices, to_owner(): return lax.ppermute(block, ('ctx', 'fsdp'), route)  12.8 us
    dot_general x8, matrix products, block_sum(): jnp.dot(pieces[q, e], weight, preferred_element_type=F32)  10.4 us
    ppermute x4, waiting for transfers between devices, to_owner(): return lax.ppermute(block, ('ctx', 'fsdp'), route)  7.83 us
    ppermute x2, starting transfers between devices, first_piece(): return (cut, lax.ppermute(cut, ('ctx', 'fsdp'), route))  7.2 us
    ppermute x2, waiting for transfers between devices, first_piece(): return (cut, lax.ppermute(cut, ('ctx', 'fsdp'), route))  5.85 us
    pallas_call x1, Pallas kernels, per_device(): pl.pallas_call(make_before_kernel(taps, per_group, per_step), grid=(octet...  4.62 us
  transfers between devices with their start and end apart: 23, of which 10 were waited for; matrix products, arithmetic and copies ran while one was open for 10% of the time, Pallas kernels for 11%

profile of v3, /device:TPU:0, one launch (start us, length us, event | category | flops | bytes accessed | tf_op | source)
XLA Modules:
  0.0 118.8 jit_solution(2356704105925157436)
XLA Ops:
  0.7 1.1 constant_dynamic-slice_fusion
  1.7 3.0 %collective-permute-start = (bf16[128,1024]{1,0:T(8,128)(2,1)S(1)}, bf16[128,1024]{1,0:T(8,128)(2,1)S(1)}, u32[]{:S(2)}, u32[]{:S(2)}) collective-permute-start(bf16[128,1024]{1,0:T(8,128)(2,1)S(1)} %get-tuple-element.37), channel_id=1, source_target_pairs={{4,0},{12,2},{20,1},{28,3},{0,4},{8,6},{16,5},{24,7},{13,8},{5,10}... | collective-permute-start | bytes 786440 | tf_op jit(solution)/shard_map/ppermute | solution.py:150
  4.7 2.9 %collective-permute-start.4 = (bf16[128,1024]{1,0:T(8,128)(2,1)S(1)}, bf16[128,1024]{1,0:T(8,128)(2,1)S(1)}, u32[]{:S(2)}, u32[]{:S(2)}) collective-permute-start(bf16[128,1024]{1,0:T(8,128)(2,1)S(1)} %get-tuple-element.36), channel_id=1, source_target_pairs={{0,2},{1,3},{2,0},{3,1},{4,6},{5,7},{6,4},{7,5},{8,10},{9,11},{10,... | collective-permute-start | bytes 786440 | tf_op jit(solution)/shard_map/ppermute | solution.py:29
  7.7 2.1 %kv_product.1.kvp_ref = bf16[128,2048]{1,0:T(8,128)(2,1)} custom-call(bf16[128,2048]{1,0:T(8,128)(2,1)} %k_ref.3, bf16[128,2048]{1,0:T(8,128)(2,1)} %v_ref.3), custom_call_target="tpu_custom_call" | custom-call | flops 1048576 | bytes 67108864 | tf_op jit(solution)/shard_map/kv_product/pallas_call | solution.py:207
  9.8 2.7 %collective-permute-start.10 = (bf16[128,2048]{1,0:T(8,128)(2,1)}, bf16[128,2048]{1,0:T(8,128)(2,1)S(1)}, u32[]{:S(2)}, u32[]{:S(2)}) collective-permute-start(bf16[128,2048]{1,0:T(8,128)(2,1)} %kv_product.1.kvp_ref), channel_id=1, source_target_pairs={{0,4},{4,8},{8,12},{12,16},{16,20},{20,24},{24,28},{1,5},{5,9},{9,... | collective-permute-start | bytes 1572872 | tf_op jit(solution)/shard_map/ppermute | solution.py:35
  12.5 0.0 collective-permute-done
  12.5 6.7 %collective-permute-start.8 = (bf16[128,1024]{1,0:T(8,128)(2,1)S(1)}, bf16[128,1024]{1,0:T(8,128)(2,1)S(1)}, u32[]{:S(2)}, u32[]{:S(2)}) collective-permute-start(bf16[128,1024]{1,0:T(8,128)(2,1)S(1)} %collective-permute-done), channel_id=1, source_target_pairs={{0,1},{1,0},{2,3},{3,2},{4,5},{5,4},{6,7},{7,6},{8,9},{9,8},{10,11... | collective-permute-start | bytes 786440 | tf_op jit(solution)/shard_map/ppermute | solution.py:29
  19.2 2.9 %convolution_convert_fusion.2 = bf16[128,2048]{1,0:T(8,128)(2,1)S(1)} fusion(bf16[128,1024]{1,0:T(8,128)(2,1)S(1)} %collective-permute-done, bf16[1024,2048]{1,0:T(8,128)(2,1)} %param.11), kind=kOutput, calls=%fused_computation.10 | convolution fusion | flops 537133056 | bytes 4980736 | tf_op jit(solution)/shard_map/dot_general | solution.py:237
  22.1 1.1 collective-permute-start.2
  23.2 0.0 collective-permute-start.1
  23.2 0.0 collective-permute-done.4
  23.2 4.2 %collective-permute-start.5 = (bf16[128,1024]{1,0:T(8,128)(2,1)S(1)}, bf16[128,1024]{1,0:T(8,128)(2,1)S(1)}, u32[]{:S(2)}, u32[]{:S(2)}) collective-permute-start(bf16[128,1024]{1,0:T(8,128)(2,1)S(1)} %collective-permute-done.4), channel_id=1, source_target_pairs={{2,0},{10,2},{18,1},{26,3},{6,4},{14,6},{22,5},{30,7},{11,8},{3,10... | collective-permute-start | bytes 786440 | tf_op jit(solution)/shard_map/ppermute | solution.py:150
  27.4 0.0 collective-permute-done.8
  27.4 0.7 convolution_convert_fusion.1
  28.2 0.6 collective-permute-start.9
  28.7 5.8 %collective-permute-done.5 = bf16[128,1024]{1,0:T(8,128)(2,1)S(1)} collective-permute-done((bf16[128,1024]{1,0:T(8,128)(2,1)S(1)}, bf16[128,1024]{1,0:T(8,128)(2,1)S(1)}, u32[]{:S(2)}, u32[]{:S(2)}) %collective-permute-start.5) | collective-permute-done | bytes 262176 | tf_op jit(solution)/shard_map/ppermute | solution.py:150
  34.6 0.6 collective-permute-start.12
  35.2 0.0 collective-permute-done.1
  35.2 4.8 %collective-permute-start.7 = (bf16[128,1024]{1,0:T(8,128)(2,1)S(1)}, bf16[128,1024]{1,0:T(8,128)(2,1)S(1)}, u32[]{:S(2)}, u32[]{:S(2)}) collective-permute-start(bf16[128,1024]{1,0:T(8,128)(2,1)S(1)} %collective-permute-done.5), channel_id=1, source_target_pairs={{0,1},{1,0},{2,3},{3,2},{4,5},{5,4},{6,7},{7,6},{8,9},{9,8},{10,11... | collective-permute-start | bytes 786440 | tf_op jit(solution)/shard_map/ppermute | solution.py:29
  40.0 0.7 convolution_convert_fusion.3
  40.8 0.0 collective-permute-done.2
  40.8 0.1 collective-permute-start.15
  40.8 0.7 fusion
  41.6 0.0 collective-permute-done.10.prior_ref
  41.6 0.7 collective-permute-start.6
  42.3 0.1 collective-permute-done.15
  42.4 1.6 %collective-permute-start.3 = (bf16[128,2048]{1,0:T(8,128)(2,1)S(1)}, bf16[128,2048]{1,0:T(8,128)(2,1)S(1)}, u32[]{:S(2)}, u32[]{:S(2)}) collective-permute-start(bf16[128,2048]{1,0:T(8,128)(2,1)S(1)} %convolution_convert_fusion.3), channel_id=1, source_target_pairs={{0,4},{4,0},{8,12},{12,8},{16,20},{20,16},{24,28},{28,24},{1,5},{5... | collective-permute-start | bytes 1572872 | tf_op jit(solution)/shard_map/ppermute | solution.py:29
  44.0 0.7 convolution_convert_fusion
  44.8 0.0 collective-permute-done.12
  44.8 4.1 %collective-permute-start.14 = (bf16[128,1024]{1,0:T(8,128)(2,1)S(1)}, bf16[128,1024]{1,0:T(8,128)(2,1)S(1)}, u32[]{:S(2)}, u32[]{:S(2)}) collective-permute-start(bf16[128,1024]{1,0:T(8,128)(2,1)S(1)} %collective-permute-done.12), channel_id=1, source_target_pairs={{0,1},{1,0},{2,3},{3,2},{4,5},{5,4},{6,7},{7,6},{8,9},{9,8},{10,11... | collective-permute-start | bytes 786440 | tf_op jit(solution)/shard_map/ppermute | solution.py:29
  48.8 0.7 collective-permute-done.9
  49.5 2.5 %collective-permute-start.16 = (bf16[128,2048]{1,0:T(8,128)(2,1)S(1)}, bf16[128,2048]{1,0:T(8,128)(2,1)S(1)}, u32[]{:S(2)}, u32[]{:S(2)}) collective-permute-start(bf16[128,2048]{1,0:T(8,128)(2,1)S(1)} %convolution_convert_fusion), channel_id=1, source_target_pairs={{0,4},{4,0},{8,12},{12,8},{16,20},{20,16},{24,28},{28,24},{1,5},{5... | collective-permute-start | bytes 1572872 | tf_op jit(solution)/shard_map/ppermute | solution.py:29
  52.0 0.0 collective-permute-done.7
  52.0 1.6 %fusion.1 = bf16[128,2048]{1,0:T(8,128)(2,1)} fusion(bf16[128,1024]{1,0:T(8,128)(2,1)S(1)} %collective-permute-done.7, bf16[1024,2048]{1,0:T(8,128)(2,1)S(1)} %copy-done.3, bf16[128,2048]{1,0:T(8,128)(2,1)S(1)} %collective-permute-done.9), kind=kOutput, calls=%fused_computation.5 | convolution fusion | flops 537657344 | bytes 5505024 | tf_op jit(solution)/shard_map/dot_general | solution.py:237
  53.6 2.6 %collective-permute-start.11 = (bf16[128,2048]{1,0:T(8,128)(2,1)}, bf16[128,2048]{1,0:T(8,128)(2,1)S(1)}, u32[]{:S(2)}, u32[]{:S(2)}) collective-permute-start(bf16[128,2048]{1,0:T(8,128)(2,1)} %fusion.1), channel_id=1, source_target_pairs={{0,16},{1,1},{2,26},{3,11},{4,20},{5,5},{6,30},{7,15},{8,24},{9,9}... | collective-permute-start | bytes 1572872 | tf_op jit(solution)/shard_map/ppermute | solution.py:163
  56.1 0.0 collective-permute-done.6
  56.2 4.6 %collective-permute-done.3 = bf16[128,2048]{1,0:T(8,128)(2,1)S(1)} collective-permute-done((bf16[128,2048]{1,0:T(8,128)(2,1)S(1)}, bf16[128,2048]{1,0:T(8,128)(2,1)S(1)}, u32[]{:S(2)}, u32[]{:S(2)}) %collective-permute-start.3) | collective-permute-done | bytes 524320 | tf_op jit(solution)/shard_map/ppermute | solution.py:29
  60.8 1.5 %fusion.2 = bf16[128,2048]{1,0:T(8,128)(2,1)} fusion(bf16[128,1024]{1,0:T(8,128)(2,1)S(1)} %collective-permute-done.12, bf16[1024,2048]{1,0:T(8,128)(2,1)S(1)} %copy-done.3, bf16[128,2048]{1,0:T(8,128)(2,1)S(1)} %collective-permute-done.3), kind=kOutput, calls=%fused_computation.6 | convolution fusion | flops 537657344 | bytes 5505024 | tf_op jit(solution)/shard_map/dot_general | solution.py:237
  62.3 3.3 %collective-permute-start.13 = (bf16[128,2048]{1,0:T(8,128)(2,1)}, bf16[128,2048]{1,0:T(8,128)(2,1)S(1)}, u32[]{:S(2)}, u32[]{:S(2)}) collective-permute-start(bf16[128,2048]{1,0:T(8,128)(2,1)} %fusion.2), channel_id=1, source_target_pairs={{0,8},{1,25},{2,2},{3,19},{4,12},{5,29},{6,6},{7,23},{8,0},{9,17},... | collective-permute-start | bytes 1572872 | tf_op jit(solution)/shard_map/ppermute | solution.py:163
  65.6 6.3 %collective-permute-done.16 = bf16[128,2048]{1,0:T(8,128)(2,1)S(1)} collective-permute-done((bf16[128,2048]{1,0:T(8,128)(2,1)S(1)}, bf16[128,2048]{1,0:T(8,128)(2,1)S(1)}, u32[]{:S(2)}, u32[]{:S(2)}) %collective-permute-start.16) | collective-permute-done | bytes 524320 | tf_op jit(solution)/shard_map/ppermute | solution.py:29
  72.0 1.5 %fusion.3 = bf16[128,2048]{1,0:T(8,128)(2,1)} fusion(bf16[128,1024]{1,0:T(8,128)(2,1)S(1)} %collective-permute-done.14, bf16[1024,2048]{1,0:T(8,128)(2,1)S(1)} %copy-done.3, bf16[128,2048]{1,0:T(8,128)(2,1)S(1)} %collective-permute-done.16), kind=kOutput, calls=%fused_computation.7 | convolution fusion | flops 537657344 | bytes 5505024 | tf_op jit(solution)/shard_map/dot_general | solution.py:237
  73.5 6.2 %collective-permute-start.17 = (bf16[128,2048]{1,0:T(8,128)(2,1)}, bf16[128,2048]{1,0:T(8,128)(2,1)}, u32[]{:S(2)}, u32[]{:S(2)}) collective-permute-start(bf16[128,2048]{1,0:T(8,128)(2,1)} %fusion.3), channel_id=1, source_target_pairs={{0,24},{1,9},{2,18},{3,3},{4,28},{5,13},{6,22},{7,7},{8,16},{9,1},... | collective-permute-start | bytes 1572872 | tf_op jit(solution)/shard_map/ppermute | solution.py:163
  79.7 0.1 rev.3.frev_ref
  79.8 4.6 %forward_conv.1 = (f32[128,2048]{1,0:T(8,128)S(1)}, bf16[16384,256]{1,0:T(8,128)(2,1)S(1)}, bf16[352,2048]{1,0:T(8,128)(2,1)S(1)}) custom-call(f32[128,128]{1,0:T(8,128)S(1)} %convert_element_type.108.f_ref, f32[128,128]{1,0:T(8,128)S(1)} %rev.3.frev_ref, bf16[128,2048]{1,0:T(8,128)(2,1)S(1)} %copy-done.2, ...), custom_call_target="tpu_custom_call" | custom-call | flops 1073741824 | bytes 25165824 | tf_op jit(solution)/shard_map/forward_conv/pallas_call | solution.py:263
  84.5 0.0 copy-start
  84.5 0.0 copy-start.1
  84.5 0.0 collective-permute-done.11
  84.5 4.4 %collective-permute-done.13 = bf16[128,2048]{1,0:T(8,128)(2,1)S(1)} collective-permute-done((bf16[128,2048]{1,0:T(8,128)(2,1)}, bf16[128,2048]{1,0:T(8,128)(2,1)S(1)}, u32[]{:S(2)}, u32[]{:S(2)}) %collective-permute-start.13) | collective-permute-done | bytes 524320 | tf_op jit(solution)/shard_map/ppermute | solution.py:163
  88.9 3.4 %collective-permute-done.17 = bf16[128,2048]{1,0:T(8,128)(2,1)} collective-permute-done((bf16[128,2048]{1,0:T(8,128)(2,1)}, bf16[128,2048]{1,0:T(8,128)(2,1)}, u32[]{:S(2)}, u32[]{:S(2)}) %collective-permute-start.17) | collective-permute-done | bytes 524320 | tf_op jit(solution)/shard_map/ppermute | solution.py:163
  92.3 1.5 %fusion.5 = (bf16[128,2048]{1,0:T(8,128)(2,1)S(1)}, bf16[128,2048]{1,0:T(8,128)(2,1)S(1)}) fusion(bf16[128,2048]{1,0:T(8,128)(2,1)S(1)} %copy-done.4, bf16[128,2048]{1,0:T(8,128)(2,1)} %collective-permute-done.17, bf16[128,2048]{1,0:T(8,128)(2,1)S(1)} %collective-permute-done.13, bf16[128,2048]{1,0:T(8,128)(2,1)S(1)} %collective-permute-done.11, ...), kind=kLoop, calls=%fused_computation.15 | loop fusion | flops 3145728 | bytes 3670016 | tf_op jit(solution)/shard_map/convert_element_type | solution.py:285
  93.8 1.5 %collective-permute-start.21 = (bf16[128,2048]{1,0:T(8,128)(2,1)S(1)}, bf16[128,2048]{1,0:T(8,128)(2,1)S(1)}, u32[]{:S(2)}, u32[]{:S(2)}) collective-permute-start(bf16[128,2048]{1,0:T(8,128)(2,1)S(1)} %get-tuple-element.34.gz_ref), channel_id=1, source_target_pairs={{4,0},{8,4},{12,8},{16,12},{20,16},{24,20},{28,24},{5,1},{9,5},{13... | collective-permute-start | bytes 1572872 | tf_op jit(solution)/shard_map/ppermute | solution.py:35
  95.3 3.0 %pair_products.1 = f32[128,128]{1,0:T(8,128)S(1)} custom-call(bf16[128,2048]{1,0:T(8,128)(2,1)S(1)} %get-tuple-element.34.gz_ref, bf16[352,2048]{1,0:T(8,128)(2,1)S(1)} %get-tuple-element.26.kvrev_ref), custom_call_target="tpu_custom_call" | custom-call | flops 1073741824 | bytes 12582912 | tf_op jit(solution)/shard_map/pair_products/pallas_call | solution.py:292
  98.3 4.2 %collective-permute-start.19 = (bf16[128,128]{1,0:T(8,128)(2,1)S(1)}, bf16[128,128]{1,0:T(8,128)(2,1)S(1)}, u32[]{:S(2)}, u32[]{:S(2)}) collective-permute-start(bf16[128,128]{1,0:T(8,128)(2,1)S(1)} %convert_element_type.112), channel_id=1, source_target_pairs={{0,16},{4,20},{8,24},{12,28},{16,0},{20,4},{24,8},{28,12},{1,17},{... | collective-permute-start | bytes 98312 | tf_op jit(solution)/shard_map/ppermute | solution.py:29
  102.4 1.6 %collective-permute-start.18 = (bf16[128,128]{1,0:T(8,128)(2,1)S(1)}, bf16[128,128]{1,0:T(8,128)(2,1)S(1)}, u32[]{:S(2)}, u32[]{:S(2)}) collective-permute-start(bf16[128,128]{1,0:T(8,128)(2,1)S(1)} %convert_element_type.112), channel_id=1, source_target_pairs={{0,8},{4,12},{8,0},{12,4},{16,24},{20,28},{24,16},{28,20},{1,9},{5... | collective-permute-start | bytes 98312 | tf_op jit(solution)/shard_map/ppermute | solution.py:29
  104.1 0.2 collective-permute-start.20
  104.3 0.9 fusion.4
  105.2 7.4 %collective-permute-done.19 = bf16[128,128]{1,0:T(8,128)(2,1)S(1)} collective-permute-done((bf16[128,128]{1,0:T(8,128)(2,1)S(1)}, bf16[128,128]{1,0:T(8,128)(2,1)S(1)}, u32[]{:S(2)}, u32[]{:S(2)}) %collective-permute-start.19) | collective-permute-done | bytes 32800 | tf_op jit(solution)/shard_map/ppermute | solution.py:29
  112.6 0.0 collective-permute-done.18
  112.6 1.6 %collective-permute-done.20 = bf16[128,128]{1,0:T(8,128)(2,1)S(1)} collective-permute-done((bf16[128,128]{1,0:T(8,128)(2,1)S(1)}, bf16[128,128]{1,0:T(8,128)(2,1)S(1)}, u32[]{:S(2)}, u32[]{:S(2)}) %collective-permute-start.20) | collective-permute-done | bytes 32800 | tf_op jit(solution)/shard_map/ppermute | solution.py:29
  114.2 0.0 collective-permute-done.21.later_ref
  114.2 0.1 collective-permute-start.22
  114.3 3.5 %backward_conv.1 = (bf16[128,2048]{1,0:T(8,128)(2,1)}, bf16[128,2048]{1,0:T(8,128)(2,1)}) custom-call(bf16[128,2048]{1,0:T(8,128)(2,1)S(1)} %get-tuple-element.34.gz_ref, bf16[128,2048]{1,0:T(8,128)(2,1)S(1)} %collective-permute-done.21.later_ref, bf16[16384,256]{1,0:T(8,128)(2,1)S(1)} %get-tuple-element.28.toe_ref, bf16[128,2048]{1,0:T(8,128)(2,1)S(1)} %copy-done, ...), custom_call_target="tpu_custom_call" | custom-call | flops 536870912 | bytes 8388608 | tf_op jit(solution)/shard_map/backward_conv/pallas_call | solution.py:308
  117.8 0.4 collective-permute-done.22
  118.2 0.6 convert_add_fusion
  (14 shorter events, 0.1 us)
Async XLA Ops:
  1.7 10.8 %collective-permute-start = (bf16[128,1024]{1,0:T(8,128)(2,1)S(1)}, bf16[128,1024]{1,0:T(8,128)(2,1)S(1)}, u32[]{:S(2)}, u32[]{:S(2)}) collective-permute-start(bf16[128,1024]{1,0:T(8,128)(2,1)S(1)} %get-tuple-element.37), channel_id=1, source_target_pairs={{4,0},{12,2},{20,1},{28,3},{0,4},{8,6},{16,5},{24,7},{13,8},{5,10}... | collective-permute-start | bytes 786440 | tf_op jit(solution)/shard_map/ppermute | solution.py:150
  4.7 18.5 %collective-permute-start.4 = (bf16[128,1024]{1,0:T(8,128)(2,1)S(1)}, bf16[128,1024]{1,0:T(8,128)(2,1)S(1)}, u32[]{:S(2)}, u32[]{:S(2)}) collective-permute-start(bf16[128,1024]{1,0:T(8,128)(2,1)S(1)} %get-tuple-element.36), channel_id=1, source_target_pairs={{0,2},{1,3},{2,0},{3,1},{4,6},{5,7},{6,4},{7,5},{8,10},{9,11},{10,... | collective-permute-start | bytes 786440 | tf_op jit(solution)/shard_map/ppermute | solution.py:29
  9.8 17.6 %copy-start.3 = (bf16[1024,2048]{1,0:T(8,128)(2,1)S(1)}, bf16[1024,2048]{1,0:T(8,128)(2,1)}, u32[]{:S(2)}) copy-start(bf16[1024,2048]{1,0:T(8,128)(2,1)} %param.11) | copy-start | bytes 12582916
  9.8 31.8 %collective-permute-start.10 = (bf16[128,2048]{1,0:T(8,128)(2,1)}, bf16[128,2048]{1,0:T(8,128)(2,1)S(1)}, u32[]{:S(2)}, u32[]{:S(2)}) collective-permute-start(bf16[128,2048]{1,0:T(8,128)(2,1)} %kv_product.1.kvp_ref), channel_id=1, source_target_pairs={{0,4},{4,8},{8,12},{12,16},{16,20},{20,24},{24,28},{1,5},{5,9},{9,... | collective-permute-start | bytes 1572872 | tf_op jit(solution)/shard_map/ppermute | solution.py:35
  12.5 14.9 %collective-permute-start.8 = (bf16[128,1024]{1,0:T(8,128)(2,1)S(1)}, bf16[128,1024]{1,0:T(8,128)(2,1)S(1)}, u32[]{:S(2)}, u32[]{:S(2)}) collective-permute-start(bf16[128,1024]{1,0:T(8,128)(2,1)S(1)} %collective-permute-done), channel_id=1, source_target_pairs={{0,1},{1,0},{2,3},{3,2},{4,5},{5,4},{6,7},{7,6},{8,9},{9,8},{10,11... | collective-permute-start | bytes 786440 | tf_op jit(solution)/shard_map/ppermute | solution.py:29
  22.1 18.6 %collective-permute-start.2 = (bf16[128,2048]{1,0:T(8,128)(2,1)S(1)}, bf16[128,2048]{1,0:T(8,128)(2,1)S(1)}, u32[]{:S(2)}, u32[]{:S(2)}) collective-permute-start(bf16[128,2048]{1,0:T(8,128)(2,1)S(1)} %convolution_convert_fusion.2), channel_id=1, source_target_pairs={{0,4},{4,0},{8,12},{12,8},{16,20},{20,16},{24,28},{28,24},{1,5},{5... | collective-permute-start | bytes 1572872 | tf_op jit(solution)/shard_map/ppermute | solution.py:29
  23.2 12.0 %collective-permute-start.1 = (bf16[128,1024]{1,0:T(8,128)(2,1)S(1)}, bf16[128,1024]{1,0:T(8,128)(2,1)S(1)}, u32[]{:S(2)}, u32[]{:S(2)}) collective-permute-start(bf16[128,1024]{1,0:T(8,128)(2,1)S(1)} %collective-permute-done), channel_id=1, source_target_pairs={{0,2},{1,3},{2,0},{3,1},{4,6},{5,7},{6,4},{7,5},{8,10},{9,11},{10,... | collective-permute-start | bytes 786440 | tf_op jit(solution)/shard_map/ppermute | solution.py:29
  23.2 11.4 %collective-permute-start.5 = (bf16[128,1024]{1,0:T(8,128)(2,1)S(1)}, bf16[128,1024]{1,0:T(8,128)(2,1)S(1)}, u32[]{:S(2)}, u32[]{:S(2)}) collective-permute-start(bf16[128,1024]{1,0:T(8,128)(2,1)S(1)} %collective-permute-done.4), channel_id=1, source_target_pairs={{2,0},{10,2},{18,1},{26,3},{6,4},{14,6},{22,5},{30,7},{11,8},{3,10... | collective-permute-start | bytes 786440 | tf_op jit(solution)/shard_map/ppermute | solution.py:150
  28.2 21.4 %collective-permute-start.9 = (bf16[128,2048]{1,0:T(8,128)(2,1)S(1)}, bf16[128,2048]{1,0:T(8,128)(2,1)S(1)}, u32[]{:S(2)}, u32[]{:S(2)}) collective-permute-start(bf16[128,2048]{1,0:T(8,128)(2,1)S(1)} %convolution_convert_fusion.1), channel_id=1, source_target_pairs={{0,4},{4,0},{8,12},{12,8},{16,20},{20,16},{24,28},{28,24},{1,5},{5... | collective-permute-start | bytes 1572872 | tf_op jit(solution)/shard_map/ppermute | solution.py:29
  34.6 10.2 %collective-permute-start.12 = (bf16[128,1024]{1,0:T(8,128)(2,1)S(1)}, bf16[128,1024]{1,0:T(8,128)(2,1)S(1)}, u32[]{:S(2)}, u32[]{:S(2)}) collective-permute-start(bf16[128,1024]{1,0:T(8,128)(2,1)S(1)} %collective-permute-done.5), channel_id=1, source_target_pairs={{0,2},{1,3},{2,0},{3,1},{4,6},{5,7},{6,4},{7,5},{8,10},{9,11},{10,... | collective-permute-start | bytes 786440 | tf_op jit(solution)/shard_map/ppermute | solution.py:29
  35.2 16.8 %collective-permute-start.7 = (bf16[128,1024]{1,0:T(8,128)(2,1)S(1)}, bf16[128,1024]{1,0:T(8,128)(2,1)S(1)}, u32[]{:S(2)}, u32[]{:S(2)}) collective-permute-start(bf16[128,1024]{1,0:T(8,128)(2,1)S(1)} %collective-permute-done.5), channel_id=1, source_target_pairs={{0,1},{1,0},{2,3},{3,2},{4,5},{5,4},{6,7},{7,6},{8,9},{9,8},{10,11... | collective-permute-start | bytes 786440 | tf_op jit(solution)/shard_map/ppermute | solution.py:29
  40.8 1.6 %collective-permute-start.15 = (bf16[128,1024]{1,0:T(8,128)(2,1)S(1)}, bf16[128,1024]{1,0:T(8,128)(2,1)S(1)}, u32[]{:S(2)}, u32[]{:S(2)}) collective-permute-start(bf16[128,1024]{1,0:T(8,128)(2,1)S(1)} %collective-permute-done.1), channel_id=1, source_target_pairs={{0,1},{1,0},{2,3},{3,2},{4,5},{5,4},{6,7},{7,6},{8,9},{9,8},{10,11... | collective-permute-start | bytes 786440 | tf_op jit(solution)/shard_map/ppermute | solution.py:29
  41.6 14.5 %collective-permute-start.6 = (bf16[128,2048]{1,0:T(8,128)(2,1)S(1)}, bf16[128,2048]{1,0:T(8,128)(2,1)S(1)}, u32[]{:S(2)}, u32[]{:S(2)}) collective-permute-start(bf16[128,2048]{1,0:T(8,128)(2,1)S(1)} %fusion), channel_id=1, source_target_pairs={{0,0},{1,17},{2,10},{3,27},{4,4},{5,21},{6,14},{7,31},{8,8},{9,25}... | collective-permute-start | bytes 1572872 | tf_op jit(solution)/shard_map/ppermute | solution.py:163
  42.4 18.4 %collective-permute-start.3 = (bf16[128,2048]{1,0:T(8,128)(2,1)S(1)}, bf16[128,2048]{1,0:T(8,128)(2,1)S(1)}, u32[]{:S(2)}, u32[]{:S(2)}) collective-permute-start(bf16[128,2048]{1,0:T(8,128)(2,1)S(1)} %convolution_convert_fusion.3), channel_id=1, source_target_pairs={{0,4},{4,0},{8,12},{12,8},{16,20},{20,16},{24,28},{28,24},{1,5},{5... | collective-permute-start | bytes 1572872 | tf_op jit(solution)/shard_map/ppermute | solution.py:29
  44.8 20.9 %collective-permute-start.14 = (bf16[128,1024]{1,0:T(8,128)(2,1)S(1)}, bf16[128,1024]{1,0:T(8,128)(2,1)S(1)}, u32[]{:S(2)}, u32[]{:S(2)}) collective-permute-start(bf16[128,1024]{1,0:T(8,128)(2,1)S(1)} %collective-permute-done.12), channel_id=1, source_target_pairs={{0,1},{1,0},{2,3},{3,2},{4,5},{5,4},{6,7},{7,6},{8,9},{9,8},{10,11... | collective-permute-start | bytes 786440 | tf_op jit(solution)/shard_map/ppermute | solution.py:29
  49.5 22.4 %collective-permute-start.16 = (bf16[128,2048]{1,0:T(8,128)(2,1)S(1)}, bf16[128,2048]{1,0:T(8,128)(2,1)S(1)}, u32[]{:S(2)}, u32[]{:S(2)}) collective-permute-start(bf16[128,2048]{1,0:T(8,128)(2,1)S(1)} %convolution_convert_fusion), channel_id=1, source_target_pairs={{0,4},{4,0},{8,12},{12,8},{16,20},{20,16},{24,28},{28,24},{1,5},{5... | collective-permute-start | bytes 1572872 | tf_op jit(solution)/shard_map/ppermute | solution.py:29
  53.6 26.1 %copy-start.5 = (bf16[128,128]{1,0:T(8,128)(2,1)S(1)}, bf16[128,128]{1,0:T(8,128)(2,1)}, u32[]{:S(2)}) copy-start(bf16[128,128]{1,0:T(8,128)(2,1)} %param.10) | copy-start | bytes 98308
  53.6 30.9 %collective-permute-start.11 = (bf16[128,2048]{1,0:T(8,128)(2,1)}, bf16[128,2048]{1,0:T(8,128)(2,1)S(1)}, u32[]{:S(2)}, u32[]{:S(2)}) collective-permute-start(bf16[128,2048]{1,0:T(8,128)(2,1)} %fusion.1), channel_id=1, source_target_pairs={{0,16},{1,1},{2,26},{3,11},{4,20},{5,5},{6,30},{7,15},{8,24},{9,9}... | collective-permute-start | bytes 1572872 | tf_op jit(solution)/shard_map/ppermute | solution.py:163
  62.3 17.5 %copy-start.2 = (bf16[128,2048]{1,0:T(8,128)(2,1)S(1)}, bf16[128,2048]{1,0:T(8,128)(2,1)}, u32[]{:S(2)}) copy-start(bf16[128,2048]{1,0:T(8,128)(2,1)} %kv_product.1.kvp_ref) | copy-start | bytes 1572868
  62.3 30.0 %copy-start.4 = (bf16[128,2048]{1,0:T(8,128)(2,1)S(1)}, bf16[128,2048]{1,0:T(8,128)(2,1)}, u32[]{:S(2)}) copy-start(bf16[128,2048]{1,0:T(8,128)(2,1)} %param.7) | copy-start | bytes 1572868
  62.3 26.6 %collective-permute-start.13 = (bf16[128,2048]{1,0:T(8,128)(2,1)}, bf16[128,2048]{1,0:T(8,128)(2,1)S(1)}, u32[]{:S(2)}, u32[]{:S(2)}) collective-permute-start(bf16[128,2048]{1,0:T(8,128)(2,1)} %fusion.2), channel_id=1, source_target_pairs={{0,8},{1,25},{2,2},{3,19},{4,12},{5,29},{6,6},{7,23},{8,0},{9,17},... | collective-permute-start | bytes 1572872 | tf_op jit(solution)/shard_map/ppermute | solution.py:163
  73.5 18.8 %collective-permute-start.17 = (bf16[128,2048]{1,0:T(8,128)(2,1)}, bf16[128,2048]{1,0:T(8,128)(2,1)}, u32[]{:S(2)}, u32[]{:S(2)}) collective-permute-start(bf16[128,2048]{1,0:T(8,128)(2,1)} %fusion.3), channel_id=1, source_target_pairs={{0,24},{1,9},{2,18},{3,3},{4,28},{5,13},{6,22},{7,7},{8,16},{9,1},... | collective-permute-start | bytes 1572872 | tf_op jit(solution)/shard_map/ppermute | solution.py:163
  84.5 29.8 %copy-start = (bf16[128,2048]{1,0:T(8,128)(2,1)S(1)}, bf16[128,2048]{1,0:T(8,128)(2,1)}, u32[]{:S(2)}) copy-start(bf16[128,2048]{1,0:T(8,128)(2,1)} %k_ref.3) | copy-start | bytes 1572868
  84.5 29.8 %copy-start.1 = (bf16[128,2048]{1,0:T(8,128)(2,1)S(1)}, bf16[128,2048]{1,0:T(8,128)(2,1)}, u32[]{:S(2)}) copy-start(bf16[128,2048]{1,0:T(8,128)(2,1)} %v_ref.3) | copy-start | bytes 1572868
  93.8 20.4 %collective-permute-start.21 = (bf16[128,2048]{1,0:T(8,128)(2,1)S(1)}, bf16[128,2048]{1,0:T(8,128)(2,1)S(1)}, u32[]{:S(2)}, u32[]{:S(2)}) collective-permute-start(bf16[128,2048]{1,0:T(8,128)(2,1)S(1)} %get-tuple-element.34.gz_ref), channel_id=1, source_target_pairs={{4,0},{8,4},{12,8},{16,12},{20,16},{24,20},{28,24},{5,1},{9,5},{13... | collective-permute-start | bytes 1572872 | tf_op jit(solution)/shard_map/ppermute | solution.py:35
  98.3 14.3 %collective-permute-start.19 = (bf16[128,128]{1,0:T(8,128)(2,1)S(1)}, bf16[128,128]{1,0:T(8,128)(2,1)S(1)}, u32[]{:S(2)}, u32[]{:S(2)}) collective-permute-start(bf16[128,128]{1,0:T(8,128)(2,1)S(1)} %convert_element_type.112), channel_id=1, source_target_pairs={{0,16},{4,20},{8,24},{12,28},{16,0},{20,4},{24,8},{28,12},{1,17},{... | collective-permute-start | bytes 98312 | tf_op jit(solution)/shard_map/ppermute | solution.py:29
  102.4 10.2 %collective-permute-start.18 = (bf16[128,128]{1,0:T(8,128)(2,1)S(1)}, bf16[128,128]{1,0:T(8,128)(2,1)S(1)}, u32[]{:S(2)}, u32[]{:S(2)}) collective-permute-start(bf16[128,128]{1,0:T(8,128)(2,1)S(1)} %convert_element_type.112), channel_id=1, source_target_pairs={{0,8},{4,12},{8,0},{12,4},{16,24},{20,28},{24,16},{28,20},{1,9},{5... | collective-permute-start | bytes 98312 | tf_op jit(solution)/shard_map/ppermute | solution.py:29
  104.1 10.1 %collective-permute-start.20 = (bf16[128,128]{1,0:T(8,128)(2,1)S(1)}, bf16[128,128]{1,0:T(8,128)(2,1)S(1)}, u32[]{:S(2)}, u32[]{:S(2)}) collective-permute-start(bf16[128,128]{1,0:T(8,128)(2,1)S(1)} %convert_element_type.112), channel_id=1, source_target_pairs={{0,24},{4,28},{8,16},{12,20},{16,8},{20,12},{24,0},{28,4},{1,25},{... | collective-permute-start | bytes 98312 | tf_op jit(solution)/shard_map/ppermute | solution.py:29
  114.2 4.0 %collective-permute-start.22 = (bf16[128,128]{1,0:T(8,128)(2,1)S(1)}, bf16[128,128]{1,0:T(8,128)(2,1)S(1)}, u32[]{:S(2)}, u32[]{:S(2)}) collective-permute-start(bf16[128,128]{1,0:T(8,128)(2,1)S(1)} %add_convert_fusion.1), channel_id=1, source_target_pairs={{0,4},{4,0},{8,12},{12,8},{16,20},{20,16},{24,28},{28,24},{1,5},{5... | collective-permute-start | bytes 98312 | tf_op jit(solution)/shard_map/ppermute | solution.py:29

commit v4 on v3

--- a/solution.py
+++ b/solution.py
@@ -62,7 +62,7 @@
 def make_before_kernel(taps, per_group, octets):
     groups = LANES // per_group
 
-    def kernel(f_ref, frev_ref, kvp_ref, prior_ref, z_ref, toe_ref, kvrev_ref):
+    def kernel(f_ref, frev_ref, kvp_ref, prior_ref, z_ref, near_ref, far_ref, kvrev_ref):
         r = lax.broadcasted_iota(jnp.int32, (2 * taps, 2 * taps), 0)
         c = lax.broadcasted_iota(jnp.int32, (2 * taps, 2 * taps), 1)
         flip = jnp.where(r + c == 2 * taps - 1, 1.0, 0.0).astype(BF16)
@@ -74,7 +74,8 @@
                 toe = shifted_rows(frev_ref[g : g + 1, :], taps, 1)
                 rows.append(toe.astype(BF16))
                 back = shifted_rows(f_ref[g : g + 1, :], taps, 0).astype(BF16)
-                toe_ref[g * taps : (g + 1) * taps, :] = back
+                near_ref[g * taps : (g + 1) * taps, :] = back[:, :taps]
+                far_ref[g * taps : (g + 1) * taps, :] = back[:, taps:]
             stacked = jnp.dot(jnp.concatenate(rows, axis=0), kv, preferred_element_type=F32)
             z_ref[:, lanes] = pick_groups(stacked, taps, per_group)
             kvrev_ref[: taps - ROWS, lanes] = jnp.zeros((taps - ROWS, LANES), BF16)
@@ -86,11 +87,14 @@
 def make_pair_kernel(taps, per_group, octets):
     groups = LANES // per_group
 
-    def kernel(gz_ref, kvrev_ref, gf_ref):
+    def kernel(gz_ref, toe_ref, kvrev_ref, gf_ref, own_ref):
         lane = lane_group(taps, per_group)
         for o in range(octets):
             lanes = slice(o * LANES, (o + 1) * LANES)
+            toes = slice(o * groups * taps, (o + 1) * groups * taps)
             gz = gz_ref[:, lanes]
+            stacked = jnp.dot(toe_ref[toes, :], gz, preferred_element_type=F32)
+            own_ref[:, lanes] = pick_groups(stacked, taps, per_group)
             zero = jnp.zeros((ROWS, LANES), BF16)
             pairs = None
             for at in range(0, taps, ROWS):
@@ -116,14 +120,13 @@
 def make_after_kernel(taps, per_group, octets):
     groups = LANES // per_group
 
-    def kernel(gz_ref, later_ref, toe_ref, k_ref, v_ref, *refs):
+    def kernel(later_ref, toe_ref, own_ref, k_ref, v_ref, *refs):
         gk_ref, gv_ref = refs[-2:]
         for o in range(octets):
             lanes = slice(o * LANES, (o + 1) * LANES)
             toes = slice(o * groups * taps, (o + 1) * groups * taps)
-            ext = jnp.concatenate([gz_ref[:, lanes], later_ref[:, lanes]], axis=0)
-            stacked = jnp.dot(toe_ref[toes, :], ext, preferred_element_type=F32)
-            grad_kv = pick_groups(stacked, taps, per_group)
+            stacked = jnp.dot(toe_ref[toes, :], later_ref[:, lanes], preferred_element_type=F32)
+            grad_kv = own_ref[:, lanes] + pick_groups(stacked, taps, per_group)
             gk_ref[:, lanes] = (grad_kv * v_ref[:, lanes].astype(F32)).astype(BF16)
             gv_ref[:, lanes] = (grad_kv * k_ref[:, lanes].astype(F32)).astype(BF16)
 
@@ -228,7 +231,7 @@
     ext_rows = 3 * taps - ROWS
     lane_block = pl.BlockSpec((tokens_here, per_step * LANES), lambda o: (0, o))
     filter_block = pl.BlockSpec((per_step * groups, taps), lambda o: (o, 0))
-    toe_block = pl.BlockSpec((per_step * groups * taps, 2 * taps), lambda o: (o, 0))
+    toe_block = pl.BlockSpec((per_step * groups * taps, taps), lambda o: (o, 0))
     ext_block = pl.BlockSpec((ext_rows, per_step * LANES), lambda o: (0, o))
     macs = channels * taps * tokens_here * groups
     params = pltpu.CompilerParams(vmem_limit_bytes=40 << 20)
@@ -260,14 +263,15 @@
         last_blocks.append(block_sum(nf - 1, cols, whole_blocks))
     prior = held["prior"]
 
-    z_conv, toes, kvrev = pl.pallas_call(
+    z_conv, near, far, kvrev = pl.pallas_call(
         make_before_kernel(taps, per_group, per_step),
         grid=(octets // per_step,),
         in_specs=[filter_block, filter_block, lane_block, lane_block],
-        out_specs=[lane_block, toe_block, ext_block],
+        out_specs=[lane_block, toe_block, toe_block, ext_block],
         out_shape=[
             jax.ShapeDtypeStruct((tokens_here, channels), F32),
-            jax.ShapeDtypeStruct((group_count * taps, 2 * taps), BF16),
+            jax.ShapeDtypeStruct((group_count * taps, taps), BF16),
+            jax.ShapeDtypeStruct((group_count * taps, taps), BF16),
             jax.ShapeDtypeStruct((ext_rows, channels), BF16),
         ],
         compiler_params=params,
@@ -287,20 +291,23 @@
 
         base = part * steps
         part_lanes = pl.BlockSpec((tokens_here, per_step * LANES), lambda o, b=base: (0, o + b))
-        part_toes = pl.BlockSpec((per_step * groups * taps, 2 * taps), lambda o, b=base: (o + b, 0))
+        part_toes = pl.BlockSpec((per_step * groups * taps, taps), lambda o, b=base: (o + b, 0))
         part_ext = pl.BlockSpec((ext_rows, per_step * LANES), lambda o, b=base: (0, o + b))
-        local_terms = pl.pallas_call(
+        local_terms, own = pl.pallas_call(
             make_pair_kernel(taps, per_group, per_step),
             grid=(steps,),
-            in_specs=[lane_block, part_ext],
-            out_specs=filter_block,
-            out_shape=jax.ShapeDtypeStruct((group_count // parts, taps), F32),
+            in_specs=[lane_block, part_toes, part_ext],
+            out_specs=[filter_block, lane_block],
+            out_shape=[
+                jax.ShapeDtypeStruct((group_count // parts, taps), F32),
+                jax.ShapeDtypeStruct((tokens_here, width), F32),
+            ],
             compiler_params=params,
             cost_estimate=pl.CostEstimate(
                 flops=4 * macs // parts, bytes_accessed=(12 << 20) // parts, transcendentals=0
             ),
             name="pair_products",
-        )(grad_z, kvrev)
+        )(grad_z, near, kvrev)
         terms.append(local_terms)
 
         earlier = [] if part == 0 else [grad_k, grad_v]
@@ -308,7 +315,7 @@
         grad_k, grad_v = pl.pallas_call(
             make_after_kernel(taps, per_group, per_step),
             grid=(steps,),
-            in_specs=[lane_block, lane_block, part_toes, part_lanes, part_lanes]
+            in_specs=[lane_block, part_toes, lane_block, part_lanes, part_lanes]
             + [pl.BlockSpec(memory_space=pl.ANY)] * len(earlier),
             out_specs=[part_lanes, part_lanes],
             out_shape=[plane16, plane16],
@@ -318,7 +325,7 @@
                 flops=2 * macs // parts, bytes_accessed=(8 << 20) // parts, transcendentals=0
             ),
             name="backward_conv",
-        )(grad_z, later, toes, keys_in, values_in, *earlier)
+        )(later, far, own, keys_in, values_in, *earlier)
 
     grad_filters, (grad_k, grad_v) = summed_over_ctx(jnp.concatenate(terms, axis=0), later, (grad_k, grad_v))
     return (jnp.concatenate(grad_qs, axis=1), grad_k, grad_v, grad_filters)

time: 120 us -> 119 us (level)
  starting transfers between devices: 55.2 us -> 51.8 us
  waiting for transfers between devices: 34.8 us -> 38 us
    ppermute x15, waiting for transfers between devices: 21.1 us -> 28.3 us  [swap(): return lax.ppermute(block, axis, [(i, i ^ mask) for i in range(size)])]
    ppermute x2, waiting for transfers between devices: 5.85 us -> 1.84 us  [first_piece(): return (cut, lax.ppermute(cut, ('ctx', 'fsdp'), route))]
    ppermute x15, starting transfers between devices: 31.1 us -> 27.7 us  [swap(): return lax.ppermute(block, axis, [(i, i ^ mask) for i in range(size)])]
  transfers between devices with their start and end apart: 23 -> 23, of which waited for: 10 -> 11; matrix products, arithmetic and copies ran while one was open for 10% -> 10% of each run, Pallas kernels for 11% -> 11%
where the time goes in v4:
time: 119 us
  starting transfers between devices  51.8 us (44%)
  waiting for transfers between devices  38 us (32%)
  Pallas kernels  13.3 us (11%)
  matrix products  10.4 us (9%)
  other arithmetic  3.06 us (3%)
    ppermute x15, waiting for transfers between devices, swap(): return lax.ppermute(block, axis, [(i, i ^ mask) for i in range(size)])  28.3 us
    ppermute x15, starting transfers between devices, swap(): return lax.ppermute(block, axis, [(i, i ^ mask) for i in range(size)])  27.7 us
    ppermute x4, starting transfers between devices, to_owner(): return lax.ppermute(block, ('ctx', 'fsdp'), route)  12.8 us
    dot_general x8, matrix products, block_sum(): jnp.dot(pieces[q, e], weight, preferred_element_type=F32)  10.4 us
    ppermute x4, waiting for transfers between devices, to_owner(): return lax.ppermute(block, ('ctx', 'fsdp'), route)  7.81 us
    ppermute x2, starting transfers between devices, first_piece(): return (cut, lax.ppermute(cut, ('ctx', 'fsdp'), route))  7.2 us
    pallas_call x1, Pallas kernels, per_device(): pl.pallas_call(make_before_kernel(taps, per_group, per_step), grid=(octet...  4.66 us
    ppermute x2, starting transfers between devices, from_behind(): return lax.ppermute(block, axis, route)  4.17 us
  transfers between devices with their start and end apart: 23, of which 11 were waited for; matrix products, arithmetic and copies ran while one was open for 10% of the time, Pallas kernels for 11%

profile of v4, /device:TPU:0, one launch (start us, length us, event | category | flops | bytes accessed | tf_op | source)
XLA Modules:
  0.0 118.7 jit_solution(16804626102340738212)
XLA Ops:
  0.7 1.1 constant_dynamic-slice_fusion
  1.7 3.0 %collective-permute-start = (bf16[128,1024]{1,0:T(8,128)(2,1)S(1)}, bf16[128,1024]{1,0:T(8,128)(2,1)S(1)}, u32[]{:S(2)}, u32[]{:S(2)}) collective-permute-start(bf16[128,1024]{1,0:T(8,128)(2,1)S(1)} %get-tuple-element.43), channel_id=1, source_target_pairs={{4,0},{12,2},{20,1},{28,3},{0,4},{8,6},{16,5},{24,7},{13,8},{5,10}... | collective-permute-start | bytes 786440 | tf_op jit(solution)/shard_map/ppermute | solution.py:153
  4.7 2.9 %collective-permute-start.4 = (bf16[128,1024]{1,0:T(8,128)(2,1)S(1)}, bf16[128,1024]{1,0:T(8,128)(2,1)S(1)}, u32[]{:S(2)}, u32[]{:S(2)}) collective-permute-start(bf16[128,1024]{1,0:T(8,128)(2,1)S(1)} %get-tuple-element.42), channel_id=1, source_target_pairs={{0,2},{1,3},{2,0},{3,1},{4,6},{5,7},{6,4},{7,5},{8,10},{9,11},{10,... | collective-permute-start | bytes 786440 | tf_op jit(solution)/shard_map/ppermute | solution.py:29
  7.7 2.1 %kv_product.1.kvp_ref = bf16[128,2048]{1,0:T(8,128)(2,1)} custom-call(bf16[128,2048]{1,0:T(8,128)(2,1)} %k_ref.3, bf16[128,2048]{1,0:T(8,128)(2,1)} %v_ref.3), custom_call_target="tpu_custom_call" | custom-call | flops 1048576 | bytes 67108864 | tf_op jit(solution)/shard_map/kv_product/pallas_call | solution.py:210
  9.8 2.7 %collective-permute-start.10 = (bf16[128,2048]{1,0:T(8,128)(2,1)}, bf16[128,2048]{1,0:T(8,128)(2,1)S(1)}, u32[]{:S(2)}, u32[]{:S(2)}) collective-permute-start(bf16[128,2048]{1,0:T(8,128)(2,1)} %kv_product.1.kvp_ref), channel_id=1, source_target_pairs={{0,4},{4,8},{8,12},{12,16},{16,20},{20,24},{24,28},{1,5},{5,9},{9,... | collective-permute-start | bytes 1572872 | tf_op jit(solution)/shard_map/ppermute | solution.py:35
  12.5 0.0 collective-permute-done
  12.5 6.7 %collective-permute-start.8 = (bf16[128,1024]{1,0:T(8,128)(2,1)S(1)}, bf16[128,1024]{1,0:T(8,128)(2,1)S(1)}, u32[]{:S(2)}, u32[]{:S(2)}) collective-permute-start(bf16[128,1024]{1,0:T(8,128)(2,1)S(1)} %collective-permute-done), channel_id=1, source_target_pairs={{0,1},{1,0},{2,3},{3,2},{4,5},{5,4},{6,7},{7,6},{8,9},{9,8},{10,11... | collective-permute-start | bytes 786440 | tf_op jit(solution)/shard_map/ppermute | solution.py:29
  19.2 2.9 %convolution_convert_fusion.2 = bf16[128,2048]{1,0:T(8,128)(2,1)S(1)} fusion(bf16[128,1024]{1,0:T(8,128)(2,1)S(1)} %collective-permute-done, bf16[1024,2048]{1,0:T(8,128)(2,1)} %param.11), kind=kOutput, calls=%fused_computation.10 | convolution fusion | flops 537133056 | bytes 4980736 | tf_op jit(solution)/shard_map/dot_general | solution.py:240
  22.1 1.1 collective-permute-start.2
  23.2 0.0 collective-permute-start.1
  23.2 0.0 collective-permute-done.4
  23.2 4.2 %collective-permute-start.5 = (bf16[128,1024]{1,0:T(8,128)(2,1)S(1)}, bf16[128,1024]{1,0:T(8,128)(2,1)S(1)}, u32[]{:S(2)}, u32[]{:S(2)}) collective-permute-start(bf16[128,1024]{1,0:T(8,128)(2,1)S(1)} %collective-permute-done.4), channel_id=1, source_target_pairs={{2,0},{10,2},{18,1},{26,3},{6,4},{14,6},{22,5},{30,7},{11,8},{3,10... | collective-permute-start | bytes 786440 | tf_op jit(solution)/shard_map/ppermute | solution.py:153
  27.4 0.0 collective-permute-done.8
  27.4 0.7 convolution_convert_fusion.1
  28.2 0.6 collective-permute-start.9
  28.7 3.0 %collective-permute-done.1 = bf16[128,1024]{1,0:T(8,128)(2,1)S(1)} collective-permute-done((bf16[128,1024]{1,0:T(8,128)(2,1)S(1)}, bf16[128,1024]{1,0:T(8,128)(2,1)S(1)}, u32[]{:S(2)}, u32[]{:S(2)}) %collective-permute-start.1) | collective-permute-done | bytes 262176 | tf_op jit(solution)/shard_map/ppermute | solution.py:29
  31.8 0.7 convolution_convert_fusion.3
  32.5 0.2 collective-permute-start.15
  32.7 1.8 %collective-permute-done.5 = bf16[128,1024]{1,0:T(8,128)(2,1)S(1)} collective-permute-done((bf16[128,1024]{1,0:T(8,128)(2,1)S(1)}, bf16[128,1024]{1,0:T(8,128)(2,1)S(1)}, u32[]{:S(2)}, u32[]{:S(2)}) %collective-permute-start.5) | collective-permute-done | bytes 262176 | tf_op jit(solution)/shard_map/ppermute | solution.py:153
  34.6 0.6 collective-permute-start.12
  35.2 3.1 %collective-permute-done.2 = bf16[128,2048]{1,0:T(8,128)(2,1)S(1)} collective-permute-done((bf16[128,2048]{1,0:T(8,128)(2,1)S(1)}, bf16[128,2048]{1,0:T(8,128)(2,1)S(1)}, u32[]{:S(2)}, u32[]{:S(2)}) %collective-permute-start.2) | collective-permute-done | bytes 524320 | tf_op jit(solution)/shard_map/ppermute | solution.py:29
  38.3 1.7 %collective-permute-start.7 = (bf16[128,1024]{1,0:T(8,128)(2,1)S(1)}, bf16[128,1024]{1,0:T(8,128)(2,1)S(1)}, u32[]{:S(2)}, u32[]{:S(2)}) collective-permute-start(bf16[128,1024]{1,0:T(8,128)(2,1)S(1)} %collective-permute-done.5), channel_id=1, source_target_pairs={{0,1},{1,0},{2,3},{3,2},{4,5},{5,4},{6,7},{7,6},{8,9},{9,8},{10,11... | collective-permute-start | bytes 786440 | tf_op jit(solution)/shard_map/ppermute | solution.py:29
  40.0 0.7 fusion
  40.8 0.0 collective-permute-done.10.prior_ref
  40.8 1.7 %collective-permute-start.3 = (bf16[128,2048]{1,0:T(8,128)(2,1)S(1)}, bf16[128,2048]{1,0:T(8,128)(2,1)S(1)}, u32[]{:S(2)}, u32[]{:S(2)}) collective-permute-start(bf16[128,2048]{1,0:T(8,128)(2,1)S(1)} %convolution_convert_fusion.3), channel_id=1, source_target_pairs={{0,4},{4,0},{8,12},{12,8},{16,20},{20,16},{24,28},{28,24},{1,5},{5... | collective-permute-start | bytes 1572872 | tf_op jit(solution)/shard_map/ppermute | solution.py:29
  42.5 0.0 collective-permute-done.15
  42.5 0.7 collective-permute-start.6
  43.2 0.7 convolution_convert_fusion
  43.9 0.0 collective-permute-done.12
  43.9 3.6 %collective-permute-start.14 = (bf16[128,1024]{1,0:T(8,128)(2,1)S(1)}, bf16[128,1024]{1,0:T(8,128)(2,1)S(1)}, u32[]{:S(2)}, u32[]{:S(2)}) collective-permute-start(bf16[128,1024]{1,0:T(8,128)(2,1)S(1)} %collective-permute-done.12), channel_id=1, source_target_pairs={{0,1},{1,0},{2,3},{3,2},{4,5},{5,4},{6,7},{7,6},{8,9},{9,8},{10,11... | collective-permute-start | bytes 786440 | tf_op jit(solution)/shard_map/ppermute | solution.py:29
  47.5 2.0 %collective-permute-done.9 = bf16[128,2048]{1,0:T(8,128)(2,1)S(1)} collective-permute-done((bf16[128,2048]{1,0:T(8,128)(2,1)S(1)}, bf16[128,2048]{1,0:T(8,128)(2,1)S(1)}, u32[]{:S(2)}, u32[]{:S(2)}) %collective-permute-start.9) | collective-permute-done | bytes 524320 | tf_op jit(solution)/shard_map/ppermute | solution.py:29
  49.5 2.5 %collective-permute-start.16 = (bf16[128,2048]{1,0:T(8,128)(2,1)S(1)}, bf16[128,2048]{1,0:T(8,128)(2,1)S(1)}, u32[]{:S(2)}, u32[]{:S(2)}) collective-permute-start(bf16[128,2048]{1,0:T(8,128)(2,1)S(1)} %convolution_convert_fusion), channel_id=1, source_target_pairs={{0,4},{4,0},{8,12},{12,8},{16,20},{20,16},{24,28},{28,24},{1,5},{5... | collective-permute-start | bytes 1572872 | tf_op jit(solution)/shard_map/ppermute | solution.py:29
  52.0 0.0 collective-permute-done.7
  52.0 1.5 %fusion.1 = bf16[128,2048]{1,0:T(8,128)(2,1)} fusion(bf16[128,1024]{1,0:T(8,128)(2,1)S(1)} %collective-permute-done.7, bf16[1024,2048]{1,0:T(8,128)(2,1)S(1)} %copy-done.3, bf16[128,2048]{1,0:T(8,128)(2,1)S(1)} %collective-permute-done.9), kind=kOutput, calls=%fused_computation.5 | convolution fusion | flops 537657344 | bytes 5505024 | tf_op jit(solution)/shard_map/dot_general | solution.py:240
  53.6 2.6 %collective-permute-start.11 = (bf16[128,2048]{1,0:T(8,128)(2,1)}, bf16[128,2048]{1,0:T(8,128)(2,1)S(1)}, u32[]{:S(2)}, u32[]{:S(2)}) collective-permute-start(bf16[128,2048]{1,0:T(8,128)(2,1)} %fusion.1), channel_id=1, source_target_pairs={{0,16},{1,1},{2,26},{3,11},{4,20},{5,5},{6,30},{7,15},{8,24},{9,9}... | collective-permute-start | bytes 1572872 | tf_op jit(solution)/shard_map/ppermute | solution.py:166
  56.1 4.6 %collective-permute-done.3 = bf16[128,2048]{1,0:T(8,128)(2,1)S(1)} collective-permute-done((bf16[128,2048]{1,0:T(8,128)(2,1)S(1)}, bf16[128,2048]{1,0:T(8,128)(2,1)S(1)}, u32[]{:S(2)}, u32[]{:S(2)}) %collective-permute-start.3) | collective-permute-done | bytes 524320 | tf_op jit(solution)/shard_map/ppermute | solution.py:29
  60.8 0.0 collective-permute-done.6
  60.8 1.5 %fusion.2 = bf16[128,2048]{1,0:T(8,128)(2,1)} fusion(bf16[128,1024]{1,0:T(8,128)(2,1)S(1)} %collective-permute-done.12, bf16[1024,2048]{1,0:T(8,128)(2,1)S(1)} %copy-done.3, bf16[128,2048]{1,0:T(8,128)(2,1)S(1)} %collective-permute-done.3), kind=kOutput, calls=%fused_computation.6 | convolution fusion | flops 537657344 | bytes 5505024 | tf_op jit(solution)/shard_map/dot_general | solution.py:240
  62.3 3.3 %collective-permute-start.13 = (bf16[128,2048]{1,0:T(8,128)(2,1)}, bf16[128,2048]{1,0:T(8,128)(2,1)S(1)}, u32[]{:S(2)}, u32[]{:S(2)}) collective-permute-start(bf16[128,2048]{1,0:T(8,128)(2,1)} %fusion.2), channel_id=1, source_target_pairs={{0,8},{1,25},{2,2},{3,19},{4,12},{5,29},{6,6},{7,23},{8,0},{9,17},... | collective-permute-start | bytes 1572872 | tf_op jit(solution)/shard_map/ppermute | solution.py:166
  65.6 0.0 collective-permute-done.14
  65.6 6.3 %collective-permute-done.16 = bf16[128,2048]{1,0:T(8,128)(2,1)S(1)} collective-permute-done((bf16[128,2048]{1,0:T(8,128)(2,1)S(1)}, bf16[128,2048]{1,0:T(8,128)(2,1)S(1)}, u32[]{:S(2)}, u32[]{:S(2)}) %collective-permute-start.16) | collective-permute-done | bytes 524320 | tf_op jit(solution)/shard_map/ppermute | solution.py:29
  72.0 1.5 %fusion.3 = bf16[128,2048]{1,0:T(8,128)(2,1)} fusion(bf16[128,1024]{1,0:T(8,128)(2,1)S(1)} %collective-permute-done.14, bf16[1024,2048]{1,0:T(8,128)(2,1)S(1)} %copy-done.3, bf16[128,2048]{1,0:T(8,128)(2,1)S(1)} %collective-permute-done.16), kind=kOutput, calls=%fused_computation.7 | convolution fusion | flops 537657344 | bytes 5505024 | tf_op jit(solution)/shard_map/dot_general | solution.py:240
  73.5 6.2 %collective-permute-start.17 = (bf16[128,2048]{1,0:T(8,128)(2,1)}, bf16[128,2048]{1,0:T(8,128)(2,1)}, u32[]{:S(2)}, u32[]{:S(2)}) collective-permute-start(bf16[128,2048]{1,0:T(8,128)(2,1)} %fusion.3), channel_id=1, source_target_pairs={{0,24},{1,9},{2,18},{3,3},{4,28},{5,13},{6,22},{7,7},{8,16},{9,1},... | collective-permute-start | bytes 1572872 | tf_op jit(solution)/shard_map/ppermute | solution.py:166
  79.7 0.1 rev.3.frev_ref
  79.8 4.7 %forward_conv.1 = (f32[128,2048]{1,0:T(8,128)S(1)}, bf16[16384,128]{1,0:T(8,128)(2,1)S(1)}, bf16[16384,128]{1,0:T(8,128)(2,1)S(1)}, bf16[352,2048]{1,0:T(8,128)(2,1)S(1)}) custom-call(f32[128,128]{1,0:T(8,128)S(1)} %convert_element_type.108.f_ref, f32[128,128]{1,0:T(8,128)S(1)} %rev.3.frev_ref, bf16[128,2048]{1,0:T(8,128)(2,1)S(1)} %copy-done.2, ...), custom_call_target="tpu_custom_call" | custom-call | flops 1073741824 | bytes 25165824 | tf_op jit(solution)/shard_map/forward_conv/pallas_call | solution.py:266
  84.5 0.0 collective-permute-done.11
  84.5 4.4 %collective-permute-done.13 = bf16[128,2048]{1,0:T(8,128)(2,1)S(1)} collective-permute-done((bf16[128,2048]{1,0:T(8,128)(2,1)}, bf16[128,2048]{1,0:T(8,128)(2,1)S(1)}, u32[]{:S(2)}, u32[]{:S(2)}) %collective-permute-start.13) | collective-permute-done | bytes 524320 | tf_op jit(solution)/shard_map/ppermute | solution.py:166
  88.9 3.4 %collective-permute-done.17 = bf16[128,2048]{1,0:T(8,128)(2,1)} collective-permute-done((bf16[128,2048]{1,0:T(8,128)(2,1)}, bf16[128,2048]{1,0:T(8,128)(2,1)}, u32[]{:S(2)}, u32[]{:S(2)}) %collective-permute-start.17) | collective-permute-done | bytes 524320 | tf_op jit(solution)/shard_map/ppermute | solution.py:166
  92.3 1.5 %fusion.5 = (bf16[128,2048]{1,0:T(8,128)(2,1)S(1)}, bf16[128,2048]{1,0:T(8,128)(2,1)S(1)}) fusion(bf16[128,2048]{1,0:T(8,128)(2,1)S(1)} %copy-done.4, bf16[128,2048]{1,0:T(8,128)(2,1)} %collective-permute-done.17, bf16[128,2048]{1,0:T(8,128)(2,1)S(1)} %collective-permute-done.13, bf16[128,2048]{1,0:T(8,128)(2,1)S(1)} %collective-permute-done.11, ...), kind=kLoop, calls=%fused_computation.15 | loop fusion | flops 3145728 | bytes 3670016 | tf_op jit(solution)/shard_map/convert_element_type | solution.py:289
  93.8 1.5 %collective-permute-start.21 = (bf16[128,2048]{1,0:T(8,128)(2,1)S(1)}, bf16[128,2048]{1,0:T(8,128)(2,1)S(1)}, u32[]{:S(2)}, u32[]{:S(2)}) collective-permute-start(bf16[128,2048]{1,0:T(8,128)(2,1)S(1)} %get-tuple-element.40.gz_ref), channel_id=1, source_target_pairs={{4,0},{8,4},{12,8},{16,12},{20,16},{24,20},{28,24},{5,1},{9,5},{13... | collective-permute-start | bytes 1572872 | tf_op jit(solution)/shard_map/ppermute | solution.py:35
  95.3 0.0 copy-start
  95.3 0.0 copy-start.1
  95.3 4.1 %pair_products.1 = (f32[128,128]{1,0:T(8,128)S(1)}, f32[128,2048]{1,0:T(8,128)S(1)}) custom-call(bf16[128,2048]{1,0:T(8,128)(2,1)S(1)} %get-tuple-element.40.gz_ref, bf16[16384,128]{1,0:T(8,128)(2,1)S(1)} %get-tuple-element.29.toe_ref, bf16[352,2048]{1,0:T(8,128)(2,1)S(1)} %get-tuple-element.30.kvrev_ref), custom_call_target="tpu_custom_call" | custom-call | flops 1073741824 | bytes 12582912 | tf_op jit(solution)/shard_map/pair_products/pallas_call | solution.py:296
  99.4 3.6 %collective-permute-start.18 = (bf16[128,128]{1,0:T(8,128)(2,1)S(1)}, bf16[128,128]{1,0:T(8,128)(2,1)S(1)}, u32[]{:S(2)}, u32[]{:S(2)}) collective-permute-start(bf16[128,128]{1,0:T(8,128)(2,1)S(1)} %convert_element_type.112), channel_id=1, source_target_pairs={{0,8},{4,12},{8,0},{12,4},{16,24},{20,28},{24,16},{28,20},{1,9},{5... | collective-permute-start | bytes 98312 | tf_op jit(solution)/shard_map/ppermute | solution.py:29
  103.0 2.1 %collective-permute-start.19 = (bf16[128,128]{1,0:T(8,128)(2,1)S(1)}, bf16[128,128]{1,0:T(8,128)(2,1)S(1)}, u32[]{:S(2)}, u32[]{:S(2)}) collective-permute-start(bf16[128,128]{1,0:T(8,128)(2,1)S(1)} %convert_element_type.112), channel_id=1, source_target_pairs={{0,16},{4,20},{8,24},{12,28},{16,0},{20,4},{24,8},{28,12},{1,17},{... | collective-permute-start | bytes 98312 | tf_op jit(solution)/shard_map/ppermute | solution.py:29
  105.1 0.4 collective-permute-start.20
  105.4 0.9 fusion.4
  106.3 6.4 %collective-permute-done.18 = bf16[128,128]{1,0:T(8,128)(2,1)S(1)} collective-permute-done((bf16[128,128]{1,0:T(8,128)(2,1)S(1)}, bf16[128,128]{1,0:T(8,128)(2,1)S(1)}, u32[]{:S(2)}, u32[]{:S(2)}) %collective-permute-start.18) | collective-permute-done | bytes 32800 | tf_op jit(solution)/shard_map/ppermute | solution.py:29
  112.7 1.4 %collective-permute-done.20 = bf16[128,128]{1,0:T(8,128)(2,1)S(1)} collective-permute-done((bf16[128,128]{1,0:T(8,128)(2,1)S(1)}, bf16[128,128]{1,0:T(8,128)(2,1)S(1)}, u32[]{:S(2)}, u32[]{:S(2)}) %collective-permute-start.20) | collective-permute-done | bytes 32800 | tf_op jit(solution)/shard_map/ppermute | solution.py:29
  114.1 0.0 collective-permute-done.21.later_ref
  114.1 0.1 collective-permute-start.22
  114.2 2.5 %backward_conv.1 = (bf16[128,2048]{1,0:T(8,128)(2,1)}, bf16[128,2048]{1,0:T(8,128)(2,1)}) custom-call(bf16[128,2048]{1,0:T(8,128)(2,1)S(1)} %collective-permute-done.21.later_ref, bf16[16384,128]{1,0:T(8,128)(2,1)S(1)} %get-tuple-element.33.toe_ref, f32[128,2048]{1,0:T(8,128)S(1)} %get-tuple-element.34.own_ref, bf16[128,2048]{1,0:T(8,128)(2,1)S(1)} %copy-done, ...), custom_call_target="tpu_custom_call" | custom-call | flops 536870912 | bytes 8388608 | tf_op jit(solution)/shard_map/backward_conv/pallas_call | solution.py:315
  116.7 1.4 %collective-permute-done.22 = bf16[128,128]{1,0:T(8,128)(2,1)S(1)} collective-permute-done((bf16[128,128]{1,0:T(8,128)(2,1)S(1)}, bf16[128,128]{1,0:T(8,128)(2,1)S(1)}, u32[]{:S(2)}, u32[]{:S(2)}) %collective-permute-start.22) | collective-permute-done | bytes 32800 | tf_op jit(solution)/shard_map/ppermute | solution.py:29
  118.1 0.6 convert_add_fusion
  (14 shorter events, 0.1 us)
Async XLA Ops:
  1.7 10.8 %collective-permute-start = (bf16[128,1024]{1,0:T(8,128)(2,1)S(1)}, bf16[128,1024]{1,0:T(8,128)(2,1)S(1)}, u32[]{:S(2)}, u32[]{:S(2)}) collective-permute-start(bf16[128,1024]{1,0:T(8,128)(2,1)S(1)} %get-tuple-element.43), channel_id=1, source_target_pairs={{4,0},{12,2},{20,1},{28,3},{0,4},{8,6},{16,5},{24,7},{13,8},{5,10}... | collective-permute-start | bytes 786440 | tf_op jit(solution)/shard_map/ppermute | solution.py:153
  4.7 18.5 %collective-permute-start.4 = (bf16[128,1024]{1,0:T(8,128)(2,1)S(1)}, bf16[128,1024]{1,0:T(8,128)(2,1)S(1)}, u32[]{:S(2)}, u32[]{:S(2)}) collective-permute-start(bf16[128,1024]{1,0:T(8,128)(2,1)S(1)} %get-tuple-element.42), channel_id=1, source_target_pairs={{0,2},{1,3},{2,0},{3,1},{4,6},{5,7},{6,4},{7,5},{8,10},{9,11},{10,... | collective-permute-start | bytes 786440 | tf_op jit(solution)/shard_map/ppermute | solution.py:29
  9.8 17.6 %copy-start.3 = (bf16[1024,2048]{1,0:T(8,128)(2,1)S(1)}, bf16[1024,2048]{1,0:T(8,128)(2,1)}, u32[]{:S(2)}) copy-start(bf16[1024,2048]{1,0:T(8,128)(2,1)} %param.11) | copy-start | bytes 12582916
  9.8 31.0 %collective-permute-start.10 = (bf16[128,2048]{1,0:T(8,128)(2,1)}, bf16[128,2048]{1,0:T(8,128)(2,1)S(1)}, u32[]{:S(2)}, u32[]{:S(2)}) collective-permute-start(bf16[128,2048]{1,0:T(8,128)(2,1)} %kv_product.1.kvp_ref), channel_id=1, source_target_pairs={{0,4},{4,8},{8,12},{12,16},{16,20},{20,24},{24,28},{1,5},{5,9},{9,... | collective-permute-start | bytes 1572872 | tf_op jit(solution)/shard_map/ppermute | solution.py:35
  12.5 14.9 %collective-permute-start.8 = (bf16[128,1024]{1,0:T(8,128)(2,1)S(1)}, bf16[128,1024]{1,0:T(8,128)(2,1)S(1)}, u32[]{:S(2)}, u32[]{:S(2)}) collective-permute-start(bf16[128,1024]{1,0:T(8,128)(2,1)S(1)} %collective-permute-done), channel_id=1, source_target_pairs={{0,1},{1,0},{2,3},{3,2},{4,5},{5,4},{6,7},{7,6},{8,9},{9,8},{10,11... | collective-permute-start | bytes 786440 | tf_op jit(solution)/shard_map/ppermute | solution.py:29
  22.1 16.2 %collective-permute-start.2 = (bf16[128,2048]{1,0:T(8,128)(2,1)S(1)}, bf16[128,2048]{1,0:T(8,128)(2,1)S(1)}, u32[]{:S(2)}, u32[]{:S(2)}) collective-permute-start(bf16[128,2048]{1,0:T(8,128)(2,1)S(1)} %convolution_convert_fusion.2), channel_id=1, source_target_pairs={{0,4},{4,0},{8,12},{12,8},{16,20},{20,16},{24,28},{28,24},{1,5},{5... | collective-permute-start | bytes 1572872 | tf_op jit(solution)/shard_map/ppermute | solution.py:29
  23.2 8.6 %collective-permute-start.1 = (bf16[128,1024]{1,0:T(8,128)(2,1)S(1)}, bf16[128,1024]{1,0:T(8,128)(2,1)S(1)}, u32[]{:S(2)}, u32[]{:S(2)}) collective-permute-start(bf16[128,1024]{1,0:T(8,128)(2,1)S(1)} %collective-permute-done), channel_id=1, source_target_pairs={{0,2},{1,3},{2,0},{3,1},{4,6},{5,7},{6,4},{7,5},{8,10},{9,11},{10,... | collective-permute-start | bytes 786440 | tf_op jit(solution)/shard_map/ppermute | solution.py:29
  23.2 11.4 %collective-permute-start.5 = (bf16[128,1024]{1,0:T(8,128)(2,1)S(1)}, bf16[128,1024]{1,0:T(8,128)(2,1)S(1)}, u32[]{:S(2)}, u32[]{:S(2)}) collective-permute-start(bf16[128,1024]{1,0:T(8,128)(2,1)S(1)} %collective-permute-done.4), channel_id=1, source_target_pairs={{2,0},{10,2},{18,1},{26,3},{6,4},{14,6},{22,5},{30,7},{11,8},{3,10... | collective-permute-start | bytes 786440 | tf_op jit(solution)/shard_map/ppermute | solution.py:153
  28.2 21.4 %collective-permute-start.9 = (bf16[128,2048]{1,0:T(8,128)(2,1)S(1)}, bf16[128,2048]{1,0:T(8,128)(2,1)S(1)}, u32[]{:S(2)}, u32[]{:S(2)}) collective-permute-start(bf16[128,2048]{1,0:T(8,128)(2,1)S(1)} %convolution_convert_fusion.1), channel_id=1, source_target_pairs={{0,4},{4,0},{8,12},{12,8},{16,20},{20,16},{24,28},{28,24},{1,5},{5... | collective-permute-start | bytes 1572872 | tf_op jit(solution)/shard_map/ppermute | solution.py:29
  32.5 10.0 %collective-permute-start.15 = (bf16[128,1024]{1,0:T(8,128)(2,1)S(1)}, bf16[128,1024]{1,0:T(8,128)(2,1)S(1)}, u32[]{:S(2)}, u32[]{:S(2)}) collective-permute-start(bf16[128,1024]{1,0:T(8,128)(2,1)S(1)} %collective-permute-done.1), channel_id=1, source_target_pairs={{0,1},{1,0},{2,3},{3,2},{4,5},{5,4},{6,7},{7,6},{8,9},{9,8},{10,11... | collective-permute-start | bytes 786440 | tf_op jit(solution)/shard_map/ppermute | solution.py:29
  34.6 9.3 %collective-permute-start.12 = (bf16[128,1024]{1,0:T(8,128)(2,1)S(1)}, bf16[128,1024]{1,0:T(8,128)(2,1)S(1)}, u32[]{:S(2)}, u32[]{:S(2)}) collective-permute-start(bf16[128,1024]{1,0:T(8,128)(2,1)S(1)} %collective-permute-done.5), channel_id=1, source_target_pairs={{0,2},{1,3},{2,0},{3,1},{4,6},{5,7},{6,4},{7,5},{8,10},{9,11},{10,... | collective-permute-start | bytes 786440 | tf_op jit(solution)/shard_map/ppermute | solution.py:29
  38.3 13.7 %collective-permute-start.7 = (bf16[128,1024]{1,0:T(8,128)(2,1)S(1)}, bf16[128,1024]{1,0:T(8,128)(2,1)S(1)}, u32[]{:S(2)}, u32[]{:S(2)}) collective-permute-start(bf16[128,1024]{1,0:T(8,128)(2,1)S(1)} %collective-permute-done.5), channel_id=1, source_target_pairs={{0,1},{1,0},{2,3},{3,2},{4,5},{5,4},{6,7},{7,6},{8,9},{9,8},{10,11... | collective-permute-start | bytes 786440 | tf_op jit(solution)/shard_map/ppermute | solution.py:29
  40.8 20.0 %collective-permute-start.3 = (bf16[128,2048]{1,0:T(8,128)(2,1)S(1)}, bf16[128,2048]{1,0:T(8,128)(2,1)S(1)}, u32[]{:S(2)}, u32[]{:S(2)}) collective-permute-start(bf16[128,2048]{1,0:T(8,128)(2,1)S(1)} %convolution_convert_fusion.3), channel_id=1, source_target_pairs={{0,4},{4,0},{8,12},{12,8},{16,20},{20,16},{24,28},{28,24},{1,5},{5... | collective-permute-start | bytes 1572872 | tf_op jit(solution)/shard_map/ppermute | solution.py:29
  42.5 18.3 %collective-permute-start.6 = (bf16[128,2048]{1,0:T(8,128)(2,1)S(1)}, bf16[128,2048]{1,0:T(8,128)(2,1)S(1)}, u32[]{:S(2)}, u32[]{:S(2)}) collective-permute-start(bf16[128,2048]{1,0:T(8,128)(2,1)S(1)} %fusion), channel_id=1, source_target_pairs={{0,0},{1,17},{2,10},{3,27},{4,4},{5,21},{6,14},{7,31},{8,8},{9,25}... | collective-permute-start | bytes 1572872 | tf_op jit(solution)/shard_map/ppermute | solution.py:166
  43.9 21.7 %collective-permute-start.14 = (bf16[128,1024]{1,0:T(8,128)(2,1)S(1)}, bf16[128,1024]{1,0:T(8,128)(2,1)S(1)}, u32[]{:S(2)}, u32[]{:S(2)}) collective-permute-start(bf16[128,1024]{1,0:T(8,128)(2,1)S(1)} %collective-permute-done.12), channel_id=1, source_target_pairs={{0,1},{1,0},{2,3},{3,2},{4,5},{5,4},{6,7},{7,6},{8,9},{9,8},{10,11... | collective-permute-start | bytes 786440 | tf_op jit(solution)/shard_map/ppermute | solution.py:29
  49.5 22.4 %collective-permute-start.16 = (bf16[128,2048]{1,0:T(8,128)(2,1)S(1)}, bf16[128,2048]{1,0:T(8,128)(2,1)S(1)}, u32[]{:S(2)}, u32[]{:S(2)}) collective-permute-start(bf16[128,2048]{1,0:T(8,128)(2,1)S(1)} %convolution_convert_fusion), channel_id=1, source_target_pairs={{0,4},{4,0},{8,12},{12,8},{16,20},{20,16},{24,28},{28,24},{1,5},{5... | collective-permute-start | bytes 1572872 | tf_op jit(solution)/shard_map/ppermute | solution.py:29
  53.6 26.2 %copy-start.5 = (bf16[128,128]{1,0:T(8,128)(2,1)S(1)}, bf16[128,128]{1,0:T(8,128)(2,1)}, u32[]{:S(2)}) copy-start(bf16[128,128]{1,0:T(8,128)(2,1)} %param.10) | copy-start | bytes 98308
  53.6 30.9 %collective-permute-start.11 = (bf16[128,2048]{1,0:T(8,128)(2,1)}, bf16[128,2048]{1,0:T(8,128)(2,1)S(1)}, u32[]{:S(2)}, u32[]{:S(2)}) collective-permute-start(bf16[128,2048]{1,0:T(8,128)(2,1)} %fusion.1), channel_id=1, source_target_pairs={{0,16},{1,1},{2,26},{3,11},{4,20},{5,5},{6,30},{7,15},{8,24},{9,9}... | collective-permute-start | bytes 1572872 | tf_op jit(solution)/shard_map/ppermute | solution.py:166
  62.3 17.5 %copy-start.2 = (bf16[128,2048]{1,0:T(8,128)(2,1)S(1)}, bf16[128,2048]{1,0:T(8,128)(2,1)}, u32[]{:S(2)}) copy-start(bf16[128,2048]{1,0:T(8,128)(2,1)} %kv_product.1.kvp_ref) | copy-start | bytes 1572868
  62.3 30.0 %copy-start.4 = (bf16[128,2048]{1,0:T(8,128)(2,1)S(1)}, bf16[128,2048]{1,0:T(8,128)(2,1)}, u32[]{:S(2)}) copy-start(bf16[128,2048]{1,0:T(8,128)(2,1)} %param.7) | copy-start | bytes 1572868
  62.3 26.6 %collective-permute-start.13 = (bf16[128,2048]{1,0:T(8,128)(2,1)}, bf16[128,2048]{1,0:T(8,128)(2,1)S(1)}, u32[]{:S(2)}, u32[]{:S(2)}) collective-permute-start(bf16[128,2048]{1,0:T(8,128)(2,1)} %fusion.2), channel_id=1, source_target_pairs={{0,8},{1,25},{2,2},{3,19},{4,12},{5,29},{6,6},{7,23},{8,0},{9,17},... | collective-permute-start | bytes 1572872 | tf_op jit(solution)/shard_map/ppermute | solution.py:166
  73.5 18.8 %collective-permute-start.17 = (bf16[128,2048]{1,0:T(8,128)(2,1)}, bf16[128,2048]{1,0:T(8,128)(2,1)}, u32[]{:S(2)}, u32[]{:S(2)}) collective-permute-start(bf16[128,2048]{1,0:T(8,128)(2,1)} %fusion.3), channel_id=1, source_target_pairs={{0,24},{1,9},{2,18},{3,3},{4,28},{5,13},{6,22},{7,7},{8,16},{9,1},... | collective-permute-start | bytes 1572872 | tf_op jit(solution)/shard_map/ppermute | solution.py:166
  93.8 20.3 %collective-permute-start.21 = (bf16[128,2048]{1,0:T(8,128)(2,1)S(1)}, bf16[128,2048]{1,0:T(8,128)(2,1)S(1)}, u32[]{:S(2)}, u32[]{:S(2)}) collective-permute-start(bf16[128,2048]{1,0:T(8,128)(2,1)S(1)} %get-tuple-element.40.gz_ref), channel_id=1, source_target_pairs={{4,0},{8,4},{12,8},{16,12},{20,16},{24,20},{28,24},{5,1},{9,5},{13... | collective-permute-start | bytes 1572872 | tf_op jit(solution)/shard_map/ppermute | solution.py:35
  95.3 18.9 %copy-start = (bf16[128,2048]{1,0:T(8,128)(2,1)S(1)}, bf16[128,2048]{1,0:T(8,128)(2,1)}, u32[]{:S(2)}) copy-start(bf16[128,2048]{1,0:T(8,128)(2,1)} %k_ref.3) | copy-start | bytes 1572868
  95.3 18.9 %copy-start.1 = (bf16[128,2048]{1,0:T(8,128)(2,1)S(1)}, bf16[128,2048]{1,0:T(8,128)(2,1)}, u32[]{:S(2)}) copy-start(bf16[128,2048]{1,0:T(8,128)(2,1)} %v_ref.3) | copy-start | bytes 1572868
  99.4 13.3 %collective-permute-start.18 = (bf16[128,128]{1,0:T(8,128)(2,1)S(1)}, bf16[128,128]{1,0:T(8,128)(2,1)S(1)}, u32[]{:S(2)}, u32[]{:S(2)}) collective-permute-start(bf16[128,128]{1,0:T(8,128)(2,1)S(1)} %convert_element_type.112), channel_id=1, source_target_pairs={{0,8},{4,12},{8,0},{12,4},{16,24},{20,28},{24,16},{28,20},{1,9},{5... | collective-permute-start | bytes 98312 | tf_op jit(solution)/shard_map/ppermute | solution.py:29
  103.0 9.7 %collective-permute-start.19 = (bf16[128,128]{1,0:T(8,128)(2,1)S(1)}, bf16[128,128]{1,0:T(8,128)(2,1)S(1)}, u32[]{:S(2)}, u32[]{:S(2)}) collective-permute-start(bf16[128,128]{1,0:T(8,128)(2,1)S(1)} %convert_element_type.112), channel_id=1, source_target_pairs={{0,16},{4,20},{8,24},{12,28},{16,0},{20,4},{24,8},{28,12},{1,17},{... | collective-permute-start | bytes 98312 | tf_op jit(solution)/shard_map/ppermute | solution.py:29
  105.1 9.0 %collective-permute-start.20 = (bf16[128,128]{1,0:T(8,128)(2,1)S(1)}, bf16[128,128]{1,0:T(8,128)(2,1)S(1)}, u32[]{:S(2)}, u32[]{:S(2)}) collective-permute-start(bf16[128,128]{1,0:T(8,128)(2,1)S(1)} %convert_element_type.112), channel_id=1, source_target_pairs={{0,24},{4,28},{8,16},{12,20},{16,8},{20,12},{24,0},{28,4},{1,25},{... | collective-permute-start | bytes 98312 | tf_op jit(solution)/shard_map/ppermute | solution.py:29
  114.1 4.0 %collective-permute-start.22 = (bf16[128,128]{1,0:T(8,128)(2,1)S(1)}, bf16[128,128]{1,0:T(8,128)(2,1)S(1)}, u32[]{:S(2)}, u32[]{:S(2)}) collective-permute-start(bf16[128,128]{1,0:T(8,128)(2,1)S(1)} %add_convert_fusion.1), channel_id=1, source_target_pairs={{0,4},{4,0},{8,12},{12,8},{16,20},{20,16},{24,28},{28,24},{1,5},{5... | collective-permute-start | bytes 98312 | tf_op jit(solution)/shard_map/ppermute | solution.py:29
